TPU v7x, 32 devices: a whole 2x2x4 slice. The times are simulated.
32 devices in a mesh: groups: 2 (over y), blk: 8 (over z, x), pair: 2 (over core).
Axes of the slice: x: 2, y: 2, z: 4, core: 2. Of those that a mesh axis runs over, the one named last changes fastest.
Arguments:
- embeddings: bfloat16 [8192, 768], P(('groups', 'blk', 'pair')), parts along dimension 0, may hold values from -24 to 24
- cluster_ids: int32 [8192], P(('groups', 'blk', 'pair')), parts along dimension 0, may hold values from 0 to 7, as said below
Outputs:
- scores: float32 [8192], P(('groups', 'blk', 'pair')), parts along dimension 0
There are 2 independent parts, one for each index of `groups`. A program takes and returns all parts, laid end to end along the dimension named above; each array names one. Nothing has to cross between parts.
Inputs may be any that keep to these rules, and one draw needn't show every extreme that they name: `cluster_ids`: within the 256 rows of one device each cluster id occurs either not at all or exactly 64 times, and one cluster id occurs in the rows of every device.
All inputs are finite; a program needn't handle non-finite values.
Results may differ from a plain program's by a relative error of at most 0.0003.
Values may be sent and summed in bfloat16 or wider, within the bound.
No kernel may reach another device: no remote copies, remote signals or barrier semaphores. Data moves between devices by JAX's collectives and lax.ppermute only.
A program may use at most 64 MiB of HBM per device.

v0:
```python
import jax
import jax.numpy as jnp
from jax import lax
from jax.sharding import PartitionSpec as P

sharpness_factor = 10.0


def unit_vectors(values):
    widened = values.astype(jnp.float32)
    scale = lax.rsqrt(jnp.sum(widened * widened, axis=1, keepdims=True) + 1e-06)
    return (widened * scale).astype(jnp.bfloat16)


def tile_pass(left, left_ids, left_weight, right, right_ids, right_weight):
    row_block = 512
    col_block = 1024
    left_scale = left_weight.astype(jnp.float32)
    right_scale = right_weight.astype(jnp.float32)
    col_parts = [jnp.zeros((col_block,), jnp.float32)]
    similarity_matrix = lax.dot_general(
        left, right, (((1,), (1,)), ((), ())), preferred_element_type=jnp.float32
    )
    self_similarity = left_ids[0:row_block, None] == right_ids[None, 0:col_block]
    scaled_products = jnp.where(self_similarity, 0.0, jnp.exp(similarity_matrix * sharpness_factor))
    row_total = jnp.sum(scaled_products * right_scale[None, 0:col_block], axis=1)
    col_parts[0] = jnp.sum(scaled_products * left_scale[0:row_block, None], axis=0)
    return (row_total, col_parts[0])


def shards(embeddings, cluster_ids):
    row_count = embeddings.shape[0]
    width = embeddings.shape[1]
    owners = lax.axis_size("blk")
    capacity = 2 * row_count // owners
    slots = owners * capacity
    pair_side = lax.axis_index("pair")
    units = unit_vectors(embeddings)
    marks = (cluster_ids[:, None] == jnp.arange(owners, dtype=jnp.int32)[None, :]).astype(
        jnp.bfloat16
    )
    row_order = jnp.arange(row_count, dtype=jnp.int32)
    earlier = (row_order[:, None] > row_order[None, :]).astype(jnp.bfloat16)
    before_count = jnp.dot(earlier, marks, preferred_element_type=jnp.float32)
    ranking = jnp.sum(before_count * marks.astype(jnp.float32), axis=1).astype(jnp.int32)
    target = cluster_ids * capacity + ranking
    send_rows = (
        jnp.zeros((slots, width), jnp.bfloat16)
        .at[target]
        .set(units)
        .reshape(owners, capacity, width)
    )
    send_valid = jnp.zeros((slots,), jnp.bfloat16).at[target].set(1.0).reshape(owners, capacity)
    slot_ids = (
        jnp.arange(owners, dtype=jnp.int32)[:, None] * capacity
        + jnp.arange(capacity, dtype=jnp.int32)[None, :]
    )
    own_ids = pair_side * slots + slot_ids.reshape(slots)
    got_rows, got_valid = (
        lax.all_to_all(send_rows, "blk", split_axis=0, concat_axis=0, tiled=True),
        lax.all_to_all(send_valid, "blk", split_axis=0, concat_axis=0, tiled=True),
    )
    own_rows = got_rows.reshape(slots, width)
    own_valid = got_valid.reshape(slots)
    col_rows = lax.all_gather(own_rows, "pair", axis=0, tiled=True)
    col_valid = lax.all_gather(own_valid, "pair", axis=0, tiled=True)
    col_ids = jnp.arange(col_rows.shape[0], dtype=jnp.int32)
    density = tile_pass(own_rows, own_ids, own_valid, col_rows, col_ids, col_valid)[0]
    living = own_valid > 0
    owned_scores = jnp.log(jnp.where(living, density, 1.0)).reshape(owners, capacity)
    returned = lax.all_to_all(owned_scores, "blk", split_axis=0, concat_axis=0, tiled=True)
    return returned.reshape(slots)[target]


def solution(mesh):
    placed = (P(("groups", "blk", "pair"), None), P(("groups", "blk", "pair")))
    return jax.shard_map(
        shards, mesh=mesh, in_specs=placed, out_specs=P(("groups", "blk", "pair")), check_vma=False
    )
```

profile of v0, /device:TPU:0, one launch (start us, length us, event | category | flops | bytes accessed | tf_op | source)
XLA Modules:
  0.0 77.9 jit_solution(5557756755445427561)
XLA Ops:
  6.5 1.2 %fusion.1 = f32[256]{0:T(256)S(1)} fusion(bf16[256,768]{1,0:T(8,128)(2,1)} %param.2), kind=kLoop, calls=%fused_computation.9 | loop fusion | flops 589568 | bytes 394240 | tf_op jit(solution)/shard_map/reduce_sum | solution.py:11
  7.7 0.9 %fusion = f32[256]{0:T(256)S(1)} fusion(s32[256]{0:T(256)} %param.3), kind=kOutput, calls=%fused_computation.6 | convolution fusion | flops 1126144 | bytes 2048 | tf_op jit(solution)/shard_map/dot_general | solution.py:44
  8.7 0.7 compare_select_fusion.1
  9.3 2.4 %scatter_custom_fusion.1 = bf16[512,768]{1,0:T(8,128)(2,1)S(1)} fusion(s32[256]{0:T(256)S(1)} %compare_select_fusion.1, bf16[256,768]{1,0:T(8,128)(2,1)} %param.2, f32[256]{0:T(256)S(1)} %add_rsqrt_fusion, bf16[]{:T(256)} %constant.10.clone.1), kind=kCustom, calls=%fused_computation.11 | custom fusion | flops 589824 | bytes 1180674 | tf_op jit(solution)/shard_map/scatter | solution.py:50
  11.8 27.3 %all_to_all.21 = bf16[8,64,768]{2,1,0:T(8,128)(2,1)} all-to-all(bf16[8,64,768]{2,1,0:T(8,128)(2,1)S(1)} %bitcast.9), channel_id=1, replica_groups=mesh['groups'=2,'blk'=8,'pair'=2] {'blk'}, dimensions={0} | all-to-all | bytes 1572864 | tf_op jit(solution)/shard_map/all_to_all | solution.py:60
  39.1 0.0 all-gather.3.cloned.1.call-update
  39.1 2.2 %scatter_custom_fusion = bf16[512]{0:T(512)(128)(2,1)S(1)} fusion(s32[256]{0:T(256)S(1)} %compare_select_fusion.1, bf16[256]{0:T(256)(128)(2,1)S(1)} %broadcast.43, bf16[]{:T(256)} %constant.10.clone.1), kind=kCustom, calls=%fused_computation.25 | custom fusion | bytes 1026 | tf_op jit(solution)/shard_map/scatter | solution.py:53
  41.3 0.7 all_to_all.17
  42.0 3.6 %all-to-all-start = ((bf16[8,1,64]{2,1,0:T(2,128)(2,1)}), bf16[8,1,64]{2,1,0:T(2,128)(2,1)S(1)}, u32[]{:S(2)}, u32[]{:S(2)}) async-start(bf16[8,1,64]{2,1,0:T(2,128)(2,1)} %all_to_all.17), calls=%async_computation | async-start | bytes 8192 | tf_op jit(solution)/shard_map/all_to_all | solution.py:61
  45.6 0.1 add_add_fusion
  45.6 0.1 add.58
  45.7 6.3 %all-to-all-done = bf16[8,1,64]{2,1,0:T(2,128)(2,1)S(1)} async-done(((bf16[8,1,64]{2,1,0:T(2,128)(2,1)}), bf16[8,1,64]{2,1,0:T(2,128)(2,1)S(1)}, u32[]{:S(2)}, u32[]{:S(2)}) %all-to-all-start) | async-done | bytes 1056 | tf_op jit(solution)/shard_map/all_to_all | solution.py:61
  52.0 0.1 reshape.83
  52.1 1.8 %all-gather = bf16[2,1,512]{2,1,0:T(2,128)(2,1)S(1)} all-gather(bf16[1,1,512]{2,1,0:T(2,128)(2,1)S(1)} %reshape.83), channel_id=1, replica_groups=mesh['groups'=2,'blk'=8,'pair'=2] {'pair'}, dimensions={0}, use_global_device_ids=true | all-gather | bytes 3072 | tf_op jit(solution)/shard_map/all_gather | solution.py:66
  53.9 0.0 all-gather.3.cloned.1.call-done
  53.9 2.9 %multiply_reduce_fusion = f32[512]{0:T(512)S(1)} fusion(bf16[512,768]{1,0:T(8,128)(2,1)} %bitcast.8, bf16[1024,768]{1,0:T(8,128)(2,1)} %all-gather.3.cloned.1.call-done, f32[1024]{0:T(1024)S(1)} %bitcast.10, s32[512]{0:T(512)S(1)} %add.58), kind=kOutput, calls=%fused_computation.3 | convolution fusion | flops 807927296 | bytes 2367488 | tf_op jit(solution)/shard_map/dot_general | solution.py:21
  56.9 0.1 reduce_sum.32
  57.0 0.6 fusion.8
  57.6 3.3 %all-to-all-start.2 = ((f32[8,1,64]{2,1,0:T(1,128)}), f32[8,1,64]{2,1,0:T(1,128)S(1)}, u32[]{:S(2)}, u32[]{:S(2)}) async-start(f32[8,1,64]{2,1,0:T(1,128)} %fusion.8), calls=%async_computation.2 | async-start | bytes 8192 | tf_op jit(solution)/shard_map/all_to_all | solution.py:71
  60.9 6.4 %all-to-all-done.2 = f32[8,1,64]{2,1,0:T(1,128)S(1)} async-done(((f32[8,1,64]{2,1,0:T(1,128)}), f32[8,1,64]{2,1,0:T(1,128)S(1)}, u32[]{:S(2)}, u32[]{:S(2)}) %all-to-all-start.2) | async-done | bytes 2080 | tf_op jit(solution)/shard_map/all_to_all | solution.py:71
  67.3 0.5 broadcast.58
  67.8 0.7 reduce.4
  68.5 0.1 reshape.55
  68.6 2.5 %gather_fusion = f32[256]{0:T(256)} fusion(f32[512]{0:T(512)S(1)} %reshape.55, s32[1024]{0:T(1024)S(1)} %pad_clamp_fusion), kind=kCustom, calls=%fused_computation | custom fusion | bytes 3072 | tf_op jit(solution)/shard_map/gather | solution.py:72
  (7 shorter events, 0.1 us)
Async XLA Ops:
  6.5 47.4 %all-gather.3.cloned.1.call-start = ((), (), s32[]{:S(2)}) async-start(), calls=%async_computation.3 | async-start | bytes 2359296 | tf_op jit(solution)/shard_map/all_gather | solution.py:65
  42.0 10.1 %all-to-all-start = ((bf16[8,1,64]{2,1,0:T(2,128)(2,1)}), bf16[8,1,64]{2,1,0:T(2,128)(2,1)S(1)}, u32[]{:S(2)}, u32[]{:S(2)}) async-start(bf16[8,1,64]{2,1,0:T(2,128)(2,1)} %all_to_all.17), calls=%async_computation | async-start | bytes 8192 | tf_op jit(solution)/shard_map/all_to_all | solution.py:61
  57.6 9.7 %all-to-all-start.2 = ((f32[8,1,64]{2,1,0:T(1,128)}), f32[8,1,64]{2,1,0:T(1,128)S(1)}, u32[]{:S(2)}, u32[]{:S(2)}) async-start(f32[8,1,64]{2,1,0:T(1,128)} %fusion.8), calls=%async_computation.2 | async-start | bytes 8192 | tf_op jit(solution)/shard_map/all_to_all | solution.py:71
Sparse Core Ops, SparseCore 0:
  39.2 8.8 all-gather.2
where the time goes:
time: 78.3 us; the launch traced here: 77.9 us
  blocking collectives  29.1 us (37%)
  between operations  13.5 us (17%)
  waiting for transfers between devices  12.7 us (16%)
  starting transfers between devices  6.92 us (9%)
  local copies, waits for them, and re-layouts  6.18 us (8%)
  other arithmetic  5.66 us (7%)
  matrix products  3.88 us (5%)
    all_to_all x1, blocking collectives, shards(): lax.all_to_all(send_rows, 'blk', split_axis=0, concat_axis=0, tiled=True)  27.3 us
    all_to_all x1, waiting for transfers between devices, shards(): lax.all_to_all(owned_scores, 'blk', split_axis=0, concat_axis=0, tiled=True)  6.39 us
    all_to_all x1, waiting for transfers between devices, shards(): lax.all_to_all(send_valid, 'blk', split_axis=0, concat_axis=0, tiled=True)  6.3 us
    all_to_all x1, starting transfers between devices, shards(): lax.all_to_all(send_valid, 'blk', split_axis=0, concat_axis=0, tiled=True)  3.59 us
    all_to_all x1, starting transfers between devices, shards(): lax.all_to_all(owned_scores, 'blk', split_axis=0, concat_axis=0, tiled=True)  3.33 us
    dot_general x1, matrix products, tile_pass(): lax.dot_general(left, right, (((1,), (1,)), ((), ())), preferred_element_...  2.93 us
    gather x1, local copies, waits for them, and re-layouts, shards(): return returned.reshape(slots)[target]  2.5 us
    scatter x1, other arithmetic, shards(): send_rows = jnp.zeros((slots, width), jnp.bfloat16).at[target].set(units)...  2.42 us
  transfers between devices with their start and end apart: 3, of which 2 were waited for; matrix products, arithmetic and copies ran while one was open for 3% of the time, Pallas kernels for 0%

commit v1 on v0

v1 whole, which is shorter than its diff:
```python
import functools

import jax
import jax.numpy as jnp
from jax import lax
from jax.experimental import pallas as pl
from jax.experimental.pallas import tpu as pltpu
from jax.sharding import PartitionSpec as P

SHARPNESS = 10.0
EPSILON = 1e-06
EMPTY_MARK = 2.0
EMPTY_ABOVE = 1.5
DIRECT_OWNERS = 8


def vmem(count):
    return [pl.BlockSpec(memory_space=pltpu.VMEM)] * count


def params(mib=24):
    return pltpu.CompilerParams(vmem_limit_bytes=mib * 1024 * 1024)


def prepare_kernel(owners, capacity, me_ref, rows_ref, ids_ref, *outs):
    block_refs, pick_ref = outs[:-1], outs[-1]
    me = me_ref[0]
    row_count, width = rows_ref.shape
    values = rows_ref[...].astype(jnp.float32)
    scale = lax.rsqrt(jnp.sum(values * values, axis=1, keepdims=True) + EPSILON)
    units = (values * scale).astype(jnp.bfloat16)
    relative = jnp.reshape(ids_ref[...], (1, row_count)) ^ me
    labels = lax.broadcasted_iota(jnp.int32, (owners, row_count), 0)
    inside = (labels == relative).astype(jnp.float32)
    above = lax.broadcasted_iota(jnp.int32, (row_count, row_count), 0)
    right = lax.broadcasted_iota(jnp.int32, (row_count, row_count), 1)
    earlier = jnp.where(above < right, 1.0, 0.0).astype(jnp.bfloat16)
    before = jnp.dot(inside.astype(jnp.bfloat16), earlier, preferred_element_type=jnp.float32)
    rank = jnp.sum(before * inside, axis=0, keepdims=True).astype(jnp.int32)
    slot = relative * capacity + rank
    slots = owners * capacity
    pick = jnp.where(lax.broadcasted_iota(jnp.int32, (slots, row_count), 0) == slot, 1.0, 0.0).astype(
        jnp.bfloat16
    )
    pick_ref[...] = pick
    counts = jnp.sum(inside, axis=1, keepdims=True)
    first = lax.broadcasted_iota(jnp.int32, (capacity, 128), 1) == 0
    for k, block_ref in enumerate(block_refs):
        block = jnp.dot(
            pick[k * capacity:(k + 1) * capacity], units, preferred_element_type=jnp.float32
        ).astype(jnp.bfloat16)
        block_ref[...] = block
        empty = counts[k:k + 1] == 0.0
        block_ref[:, 0:128] = jnp.where(
            first & empty, EMPTY_MARK, block[:, 0:128].astype(jnp.float32)
        ).astype(jnp.bfloat16)


def prepare(me, rows, ids, owners, capacity):
    row_count, width = rows.shape
    shapes = [jax.ShapeDtypeStruct((capacity, width), jnp.bfloat16)] * owners
    shapes.append(jax.ShapeDtypeStruct((owners * capacity, row_count), jnp.bfloat16))
    return pl.pallas_call(
        functools.partial(prepare_kernel, owners, capacity),
        out_shape=shapes,
        in_specs=[pl.BlockSpec(memory_space=pltpu.SMEM)] + vmem(2),
        out_specs=vmem(len(shapes)),
        compiler_params=params(),
    )(me, rows, ids)


def partial_sums(own, others, others_refs, own_block):
    capacity = others_refs[0].shape[0]
    count = own.shape[0]
    total = jnp.zeros((1, count), jnp.float32)
    products = lax.dot_general(others, own, (((1,), (1,)), ((), ())), preferred_element_type=jnp.float32)
    for k, block_ref in enumerate(others_refs):
        powers = jnp.exp(products[k * capacity:(k + 1) * capacity] * SHARPNESS)
        if own_block:
            row = lax.broadcasted_iota(jnp.int32, powers.shape, 0) + k * capacity
            powers = jnp.where(row == lax.broadcasted_iota(jnp.int32, powers.shape, 1), 0.0, powers)
        living = block_ref[0:1, 0:1].astype(jnp.float32) < EMPTY_ABOVE
        total = total + jnp.where(living, jnp.sum(powers, axis=0, keepdims=True), 0.0)
    return total


def own_kernel(owners, *refs):
    block_refs, joined_ref, total_ref = refs[:owners], refs[owners], refs[owners + 1]
    capacity = block_refs[0].shape[0]
    for k, block_ref in enumerate(block_refs):
        joined_ref[k * capacity:(k + 1) * capacity, :] = block_ref[...]
    own = joined_ref[...]
    total_ref[...] = partial_sums(own, own, block_refs, True)


def own_sums(blocks):
    capacity, width = blocks[0].shape
    slots = len(blocks) * capacity
    return pl.pallas_call(
        functools.partial(own_kernel, len(blocks)),
        out_shape=[
            jax.ShapeDtypeStruct((slots, width), jnp.bfloat16),
            jax.ShapeDtypeStruct((1, slots), jnp.float32),
        ],
        in_specs=vmem(len(blocks)),
        out_specs=vmem(2),
        compiler_params=params(),
        cost_estimate=pl.CostEstimate(
            flops=2 * slots * slots * width, bytes_accessed=4 * slots * width, transcendentals=slots * slots
        ),
    )(*blocks)


def cross_kernel(owners, *refs):
    block_refs, joined_ref, total_ref = refs[:owners], refs[owners], refs[owners + 1]
    score_refs = refs[owners + 2:2 * owners + 2]
    others_ref = refs[-1]
    capacity = block_refs[0].shape[0]
    for k, block_ref in enumerate(block_refs):
        others_ref[k * capacity:(k + 1) * capacity, :] = block_ref[...]
    total = total_ref[...] + partial_sums(joined_ref[...], others_ref[...], block_refs, False)
    scores = jnp.log(jnp.where(total > 0.0, total, 1.0))
    for k, score_ref in enumerate(score_refs):
        score_ref[...] = scores[:, k * capacity:(k + 1) * capacity]


def cross_scores(blocks, joined, total):
    capacity, width = blocks[0].shape
    slots = len(blocks) * capacity
    return pl.pallas_call(
        functools.partial(cross_kernel, len(blocks)),
        out_shape=[jax.ShapeDtypeStruct((1, capacity), jnp.float32)] * len(blocks),
        in_specs=vmem(len(blocks) + 2),
        out_specs=vmem(len(blocks)),
        scratch_shapes=[pltpu.VMEM((slots, width), jnp.bfloat16)],
        compiler_params=params(),
    )(*blocks, joined, total)


def collect_kernel(owners, *refs):
    score_refs, pick_ref, out_ref = refs[:owners], refs[owners], refs[owners + 1]
    scores = jnp.concatenate([score_ref[...] for score_ref in score_refs], axis=1)
    high = scores.astype(jnp.bfloat16)
    rest = scores - high.astype(jnp.float32)
    middle = rest.astype(jnp.bfloat16)
    low = (rest - middle.astype(jnp.float32)).astype(jnp.bfloat16)
    pick = pick_ref[...]
    parts = [jnp.dot(part, pick, preferred_element_type=jnp.float32) for part in (high, middle, low)]
    out_ref[...] = jnp.reshape((parts[0] + parts[1]) + parts[2], out_ref.shape)


def collect(scores, pick):
    return pl.pallas_call(
        functools.partial(collect_kernel, len(scores)),
        out_shape=jax.ShapeDtypeStruct((pick.shape[1],), jnp.float32),
        in_specs=vmem(len(scores) + 1),
        out_specs=pl.BlockSpec(memory_space=pltpu.VMEM),
        compiler_params=params(),
    )(*scores, pick)


def swap(block, axis, step, size):
    if step == 0:
        return block
    return lax.ppermute(block, axis, [(i, i ^ step) for i in range(size)])


def direct_shards(embeddings, cluster_ids):
    owners = lax.axis_size("blk")
    capacity = 2 * embeddings.shape[0] // owners
    me = jnp.reshape(lax.axis_index("blk").astype(jnp.int32), (1,))
    *blocks, pick = prepare(me, embeddings, cluster_ids, owners, capacity)
    own_blocks = [None] * owners
    for k in reversed(range(owners)):
        own_blocks[k] = swap(blocks[k], "blk", k, owners)
    other_blocks = [swap(block, "pair", 1, 2) for block in own_blocks]
    joined, total = own_sums(own_blocks)
    scores = cross_scores(other_blocks, joined, total)
    returned = [swap(scores[k], "blk", k, owners) for k in range(owners)]
    return collect(returned, pick)


def unit_vectors(values):
    widened = values.astype(jnp.float32)
    scale = lax.rsqrt(jnp.sum(widened * widened, axis=1, keepdims=True) + EPSILON)
    return (widened * scale).astype(jnp.bfloat16)


def wide_shards(embeddings, cluster_ids):
    row_count, width = embeddings.shape
    owners = lax.axis_size("blk")
    capacity = 2 * row_count // owners
    slots = owners * capacity
    units = unit_vectors(embeddings)
    marks = (cluster_ids[:, None] == jnp.arange(owners, dtype=jnp.int32)[None, :]).astype(jnp.bfloat16)
    row_order = jnp.arange(row_count, dtype=jnp.int32)
    earlier = (row_order[:, None] > row_order[None, :]).astype(jnp.bfloat16)
    before = jnp.dot(earlier, marks, preferred_element_type=jnp.float32)
    rank = jnp.sum(before * marks.astype(jnp.float32), axis=1).astype(jnp.int32)
    target = cluster_ids * capacity + rank
    empty_row = jnp.where(jnp.arange(width) == 0, EMPTY_MARK, 0.0).astype(jnp.bfloat16)
    send = jnp.broadcast_to(empty_row[None, :], (slots, width)).at[target].set(units)
    own = lax.all_to_all(
        send.reshape(owners, capacity, width), "blk", split_axis=0, concat_axis=0, tiled=True
    ).reshape(slots, width)
    other = lax.ppermute(own, "pair", [(0, 1), (1, 0)])
    columns = jnp.concatenate([own, other], axis=0)
    living = columns[:, 0].astype(jnp.float32) < EMPTY_ABOVE
    products = lax.dot_general(own, columns, (((1,), (1,)), ((), ())), preferred_element_type=jnp.float32)
    position = jnp.arange(2 * slots, dtype=jnp.int32)
    keep = living[None, :] & (position[:slots, None] != position[None, :])
    density = jnp.sum(jnp.where(keep, jnp.exp(products * SHARPNESS), 0.0), axis=1)
    scores = jnp.log(jnp.where(living[:slots], density, 1.0)).reshape(owners, capacity)
    returned = lax.all_to_all(scores, "blk", split_axis=0, concat_axis=0, tiled=True)
    return returned.reshape(slots)[target]


def solution(mesh):
    placed = (P(("groups", "blk", "pair"), None), P(("groups", "blk", "pair")))
    shards = direct_shards if mesh.shape["blk"] <= DIRECT_OWNERS else wide_shards
    return jax.shard_map(
        shards, mesh=mesh, in_specs=placed, out_specs=P(("groups", "blk", "pair")), check_vma=False
    )
```

time: 78.3 us -> 45.1 us (0.58)
  blocking collectives: 29.1 us -> 0 us
  starting transfers between devices: 6.92 us -> 30.4 us
  between operations: 13.5 us -> 0.06 us
  other arithmetic: 5.66 us -> 0 us
  local copies, waits for them, and re-layouts: 6.18 us -> 1.67 us
  matrix products: 3.88 us -> 0 us
  Pallas kernels: 0 us -> 3.14 us
  waiting for transfers between devices: 12.7 us -> 9.74 us
    ppermute x0 -> x22, starting transfers between devices: none -> 30.4 us  [swap(): return lax.ppermute(block, axis, [(i, i ^ step) for i in range(size)])]
    all_to_all x1 -> x0, blocking collectives: 27.3 us -> none  [shards(): lax.all_to_all(send_rows, 'blk', split_axis=0, concat_axis=0, tiled=True)]
    all_to_all x2 -> x0, waiting for transfers between devices: 12.7 us -> none  [the longest x1 6.39 us: shards(): lax.all_to_all(owned_scores, 'blk', split_axis=0, concat_axis=0, tiled=True)]
    ppermute x0 -> x22, waiting for transfers between devices: none -> 9.74 us  [swap(): return lax.ppermute(block, axis, [(i, i ^ step) for i in range(size)])]
    all_to_all x2 -> x0, starting transfers between devices: 6.92 us -> none  [the longest x1 3.59 us: shards(): lax.all_to_all(send_valid, 'blk', split_axis=0, concat_axis=0, tiled=True)]
    dot_general x2 -> x0, matrix products: 3.88 us -> none  [the longest x1 2.93 us: tile_pass(): lax.dot_general(left, right, (((1,), (1,)), ((), ())), preferred_element_...]
    pallas_call x0 -> x4, Pallas kernels: none -> 3.14 us  [the longest x1 0.89 us: prepare(): pl.pallas_call(functools.partial(prepare_kernel, owners, capacity), out_s...]
    gather x1 -> x0, local copies, waits for them, and re-layouts: 2.5 us -> none  [shards(): return returned.reshape(slots)[target]]
  transfers between devices with their start and end apart: 3 -> 22, of which waited for: 2 -> 5; matrix products, arithmetic and copies ran while one was open for 3% -> 0% of each run, Pallas kernels for 0% -> 2%
where the time goes in v1:
time: 45.1 us; the launch traced here: 45 us
  starting transfers between devices  30.4 us (67%)
  waiting for transfers between devices  9.74 us (22%)
  Pallas kernels  3.14 us (7%)
  local copies, waits for them, and re-layouts  1.67 us (4%)
    ppermute x22, starting transfers between devices, swap(): return lax.ppermute(block, axis, [(i, i ^ step) for i in range(size)])  30.4 us
    ppermute x22, waiting for transfers between devices, swap(): return lax.ppermute(block, axis, [(i, i ^ step) for i in range(size)])  9.74 us
    unnamed x4, local copies, waits for them, and re-layouts  1.67 us
  transfers between devices with their start and end apart: 22, of which 5 were waited for; matrix products, arithmetic and copies ran while one was open for 0% of the time, Pallas kernels for 2%

profile of v1, /device:TPU:0, one launch (start us, length us, event | category | flops | bytes accessed | tf_op | source)
XLA Modules:
  0.0 45.0 jit_solution(610585513194984097)
XLA Ops:
  0.0 0.7 %copy-done.1 = s32[256]{0:T(256)S(1)} copy-done((s32[256]{0:T(256)S(1)}, s32[256]{0:T(256)}, u32[]{:S(2)}) %copy-start.1) | copy-done | bytes 1048
  0.7 1.0 %copy-done = bf16[256,768]{1,0:T(8,128)(2,1)S(1)} copy-done((bf16[256,768]{1,0:T(8,128)(2,1)S(1)}, bf16[256,768]{1,0:T(8,128)(2,1)}, u32[]{:S(2)}) %copy-start) | copy-done | bytes 393240
  1.7 0.9 %shard_map.28 = (bf16[64,768]{1,0:T(8,128)(2,1)S(1)}, bf16[64,768]{1,0:T(8,128)(2,1)S(1)}, bf16[64,768]{1,0:T(8,128)(2,1)S(1)}, bf16[64,768]{1,0:T(8,128)(2,1)S(...) custom-call(s32[1]{0:T(128)} %bitcast.me_ref, ...), custom_call_target="tpu_custom_call" | custom-call | tf_op jit(solution)/shard_map/pallas_call | solution.py:63
  2.6 3.0 %collective-permute-start.1 = (bf16[64,768]{1,0:T(8,128)(2,1)S(1)}, bf16[64,768]{1,0:T(8,128)(2,1)S(1)}, u32[]{:S(2)}, u32[]{:S(2)}) collective-permute-start(bf16[64,768]{1,0:T(8,128)(2,1)S(1)} %get-tuple-element.25), channel_id=1, source_target_pairs={{0,2},{2,0},{4,6},{6,4},{8,10},{10,8},{12,14},{14,12},{1,3},{3,1},... | collective-permute-start | bytes 294920 | tf_op jit(solution)/shard_map/ppermute | solution.py:165
  5.6 3.6 %collective-permute-start.11 = (bf16[64,768]{1,0:T(8,128)(2,1)S(1)}, bf16[64,768]{1,0:T(8,128)(2,1)S(1)}, u32[]{:S(2)}, u32[]{:S(2)}) collective-permute-start(bf16[64,768]{1,0:T(8,128)(2,1)S(1)} %get-tuple-element.30), channel_id=1, source_target_pairs={{0,12},{2,14},{4,8},{6,10},{8,4},{10,6},{12,0},{14,2},{1,13},{3,15... | collective-permute-start | bytes 294920 | tf_op jit(solution)/shard_map/ppermute | solution.py:165
  9.2 1.9 %collective-permute-start.9 = (bf16[64,768]{1,0:T(8,128)(2,1)S(1)}, bf16[64,768]{1,0:T(8,128)(2,1)S(1)}, u32[]{:S(2)}, u32[]{:S(2)}) collective-permute-start(bf16[64,768]{1,0:T(8,128)(2,1)S(1)} %get-tuple-element.29), channel_id=1, source_target_pairs={{0,10},{2,8},{4,14},{6,12},{8,2},{10,0},{12,6},{14,4},{1,11},{3,9}... | collective-permute-start | bytes 294920 | tf_op jit(solution)/shard_map/ppermute | solution.py:165
  11.1 3.4 %collective-permute-start.3 = (bf16[64,768]{1,0:T(8,128)(2,1)S(1)}, bf16[64,768]{1,0:T(8,128)(2,1)S(1)}, u32[]{:S(2)}, u32[]{:S(2)}) collective-permute-start(bf16[64,768]{1,0:T(8,128)(2,1)S(1)} %get-tuple-element.26), channel_id=1, source_target_pairs={{0,4},{2,6},{4,0},{6,2},{8,12},{10,14},{12,8},{14,10},{1,5},{3,7},... | collective-permute-start | bytes 294920 | tf_op jit(solution)/shard_map/ppermute | solution.py:165
  14.5 5.7 %collective-permute-start.7 = (bf16[64,768]{1,0:T(8,128)(2,1)S(1)}, bf16[64,768]{1,0:T(8,128)(2,1)S(1)}, u32[]{:S(2)}, u32[]{:S(2)}) collective-permute-start(bf16[64,768]{1,0:T(8,128)(2,1)S(1)} %get-tuple-element.28), channel_id=1, source_target_pairs={{0,8},{2,10},{4,12},{6,14},{8,0},{10,2},{12,4},{14,6},{1,9},{3,11}... | collective-permute-start | bytes 294920 | tf_op jit(solution)/shard_map/ppermute | solution.py:165
  20.2 4.2 %collective-permute-done.9.refs_5_ = bf16[64,768]{1,0:T(8,128)(2,1)S(1)} collective-permute-done((bf16[64,768]{1,0:T(8,128)(2,1)S(1)}, bf16[64,768]{1,0:T(8,128)(2,1)S(1)}, u32[]{:S(2)}, u32[]{:S(2)}) %collective-permute-start.9) | collective-permute-done | bytes 98336 | tf_op jit(solution)/shard_map/ppermute | solution.py:165
  24.4 0.5 %collective-permute-start.12 = (bf16[64,768]{1,0:T(8,128)(2,1)S(1)}, bf16[64,768]{1,0:T(8,128)(2,1)S(1)}, u32[]{:S(2)}, u32[]{:S(2)}) collective-permute-start(bf16[64,768]{1,0:T(8,128)(2,1)S(1)} %collective-permute-done.11.refs_6_), channel_id=1, source_target_pairs={{0,1},{1,0},{2,3},{3,2},{4,5},{5,4},{6,7},{7,6},{8,9},{9,8},{10,11... | collective-permute-start | bytes 294920 | tf_op jit(solution)/shard_map/ppermute | solution.py:165
  25.0 0.5 %collective-permute-done.7.refs_4_ = bf16[64,768]{1,0:T(8,128)(2,1)S(1)} collective-permute-done((bf16[64,768]{1,0:T(8,128)(2,1)S(1)}, bf16[64,768]{1,0:T(8,128)(2,1)S(1)}, u32[]{:S(2)}, u32[]{:S(2)}) %collective-permute-start.7) | collective-permute-done | bytes 98336 | tf_op jit(solution)/shard_map/ppermute | solution.py:165
  25.6 0.5 %collective-permute-start.4 = (bf16[64,768]{1,0:T(8,128)(2,1)S(1)}, bf16[64,768]{1,0:T(8,128)(2,1)S(1)}, u32[]{:S(2)}, u32[]{:S(2)}) collective-permute-start(bf16[64,768]{1,0:T(8,128)(2,1)S(1)} %collective-permute-done.3.refs_2_), channel_id=1, source_target_pairs={{0,1},{1,0},{2,3},{3,2},{4,5},{5,4},{6,7},{7,6},{8,9},{9,8},{10,11... | collective-permute-start | bytes 294920 | tf_op jit(solution)/shard_map/ppermute | solution.py:165
  26.2 0.4 collective-permute-start.8
  26.6 0.7 %shard_map.29 = (bf16[512,768]{1,0:T(8,128)(2,1)S(1)}, f32[1,512]{1,0:T(1,128)S(1)}) custom-call(bf16[64,768]{1,0:T(8,128)(2,1)S(1)} %get-tuple-element.24.refs_0_, bf16[64,768]{1,0:T(8,128)(2,1)S(1)} %collective-permute-done.1.refs_1_, bf16[64,768]{1,0:T(8,128)(2,1)S(1)} %collective-permute-done.3.refs_2_, ...), custom_call_target="tpu_custom_call" | custom-call | flops 402653184 | bytes 1572864 | tf_op jit(solution)/shard_map/pallas_call | solution.py:99
  27.5 0.7 %shard_map.30 = (f32[1,64]{1,0:T(1,128)S(1)}, f32[1,64]{1,0:T(1,128)S(1)}, f32[1,64]{1,0:T(1,128)S(1)}, f32[1,64]{1,0:T(1,128)S(1)}, f32[1,64]{1,0:T(1,128)S(1)}...) custom-call(bf16[64,768]{1,0:T(8,128)(2,1)S(1)} %collective-permute-done.refs_0_, ...), custom_call_target="tpu_custom_call" | custom-call | tf_op jit(solution)/shard_map/pallas_call | solution.py:130
  28.3 1.2 %collective-permute-start.15 = (f32[1,64]{1,0:T(1,128)S(1)}, f32[1,64]{1,0:T(1,128)S(1)}, u32[]{:S(2)}, u32[]{:S(2)}) collective-permute-start(f32[1,64]{1,0:T(1,128)S(1)} %get-tuple-element.35), channel_id=1, source_target_pairs={{0,2},{2,0},{4,6},{6,4},{8,10},{10,8},{12,14},{14,12},{1,3},{3,1},... | collective-permute-start | bytes 776 | tf_op jit(solution)/shard_map/ppermute | solution.py:165
  29.5 2.3 %collective-permute-start.17 = (f32[1,64]{1,0:T(1,128)S(1)}, f32[1,64]{1,0:T(1,128)S(1)}, u32[]{:S(2)}, u32[]{:S(2)}) collective-permute-start(f32[1,64]{1,0:T(1,128)S(1)} %get-tuple-element.37), channel_id=1, source_target_pairs={{0,6},{2,4},{4,2},{6,0},{8,14},{10,12},{12,10},{14,8},{1,7},{3,5},... | collective-permute-start | bytes 776 | tf_op jit(solution)/shard_map/ppermute | solution.py:165
  31.8 1.0 %collective-permute-start.18 = (f32[1,64]{1,0:T(1,128)S(1)}, f32[1,64]{1,0:T(1,128)S(1)}, u32[]{:S(2)}, u32[]{:S(2)}) collective-permute-start(f32[1,64]{1,0:T(1,128)S(1)} %get-tuple-element.38), channel_id=1, source_target_pairs={{0,8},{2,10},{4,12},{6,14},{8,0},{10,2},{12,4},{14,6},{1,9},{3,11}... | collective-permute-start | bytes 776 | tf_op jit(solution)/shard_map/ppermute | solution.py:165
  32.8 2.6 %collective-permute-start.19 = (f32[1,64]{1,0:T(1,128)S(1)}, f32[1,64]{1,0:T(1,128)S(1)}, u32[]{:S(2)}, u32[]{:S(2)}) collective-permute-start(f32[1,64]{1,0:T(1,128)S(1)} %get-tuple-element.39), channel_id=1, source_target_pairs={{0,10},{2,8},{4,14},{6,12},{8,2},{10,0},{12,6},{14,4},{1,11},{3,9}... | collective-permute-start | bytes 776 | tf_op jit(solution)/shard_map/ppermute | solution.py:165
  35.4 2.5 %collective-permute-start.20 = (f32[1,64]{1,0:T(1,128)S(1)}, f32[1,64]{1,0:T(1,128)S(1)}, u32[]{:S(2)}, u32[]{:S(2)}) collective-permute-start(f32[1,64]{1,0:T(1,128)S(1)} %get-tuple-element.40), channel_id=1, source_target_pairs={{0,12},{2,14},{4,8},{6,10},{8,4},{10,6},{12,0},{14,2},{1,13},{3,15... | collective-permute-start | bytes 776 | tf_op jit(solution)/shard_map/ppermute | solution.py:165
  37.9 1.5 %collective-permute-start.21 = (f32[1,64]{1,0:T(1,128)S(1)}, f32[1,64]{1,0:T(1,128)S(1)}, u32[]{:S(2)}, u32[]{:S(2)}) collective-permute-start(f32[1,64]{1,0:T(1,128)S(1)} %get-tuple-element.41), channel_id=1, source_target_pairs={{0,14},{2,12},{4,10},{6,8},{8,6},{10,4},{12,2},{14,0},{1,15},{3,13... | collective-permute-start | bytes 776 | tf_op jit(solution)/shard_map/ppermute | solution.py:165
  39.4 1.3 %collective-permute-done.20.refs_6_ = f32[1,64]{1,0:T(1,128)S(1)} collective-permute-done((f32[1,64]{1,0:T(1,128)S(1)}, f32[1,64]{1,0:T(1,128)S(1)}, u32[]{:S(2)}, u32[]{:S(2)}) %collective-permute-start.20) | collective-permute-done | bytes 288 | tf_op jit(solution)/shard_map/ppermute | solution.py:165
  40.7 3.4 %collective-permute-done.21.refs_7_ = f32[1,64]{1,0:T(1,128)S(1)} collective-permute-done((f32[1,64]{1,0:T(1,128)S(1)}, f32[1,64]{1,0:T(1,128)S(1)}, u32[]{:S(2)}, u32[]{:S(2)}) %collective-permute-start.21) | collective-permute-done | bytes 288 | tf_op jit(solution)/shard_map/ppermute | solution.py:165
  44.1 0.8 %shard_map.31 = f32[256]{0:T(256)} custom-call(f32[1,64]{1,0:T(1,128)S(1)} %get-tuple-element.34.refs_0_, f32[1,64]{1,0:T(1,128)S(1)} %collective-permute-done.15.refs_1_, f32[1,64]{1,0:T(1,128)S(1)} %collective-permute-done.16.refs_2_, f32[1,64]{1,0:T(1,128)S(1)} %collective-permute-done.17.refs_3_, f32[1,64]{1,0:T(1,128)S(1)} %collective-permute-done.18.refs_4_, ...), custom_call_target="tpu_custom_call" | custom-call | tf_op jit(solution)/shard_map/pallas_call | solution.py:153
  (28 shorter events, 0.4 us)
Async XLA Ops:
  0.0 0.7 %copy-start.1 = (s32[256]{0:T(256)S(1)}, s32[256]{0:T(256)}, u32[]{:S(2)}) copy-start(s32[256]{0:T(256)} %ids_ref.1) | copy-start | bytes 3076
  0.7 1.0 %copy-start = (bf16[256,768]{1,0:T(8,128)(2,1)S(1)}, bf16[256,768]{1,0:T(8,128)(2,1)}, u32[]{:S(2)}) copy-start(bf16[256,768]{1,0:T(8,128)(2,1)} %rows_ref.1) | copy-start | bytes 1179652
  2.6 11.9 %collective-permute-start.1 = (bf16[64,768]{1,0:T(8,128)(2,1)S(1)}, bf16[64,768]{1,0:T(8,128)(2,1)S(1)}, u32[]{:S(2)}, u32[]{:S(2)}) collective-permute-start(bf16[64,768]{1,0:T(8,128)(2,1)S(1)} %get-tuple-element.25), channel_id=1, source_target_pairs={{0,2},{2,0},{4,6},{6,4},{8,10},{10,8},{12,14},{14,12},{1,3},{3,1},... | collective-permute-start | bytes 294920 | tf_op jit(solution)/shard_map/ppermute | solution.py:165
  5.6 8.9 %collective-permute-start.11 = (bf16[64,768]{1,0:T(8,128)(2,1)S(1)}, bf16[64,768]{1,0:T(8,128)(2,1)S(1)}, u32[]{:S(2)}, u32[]{:S(2)}) collective-permute-start(bf16[64,768]{1,0:T(8,128)(2,1)S(1)} %get-tuple-element.30), channel_id=1, source_target_pairs={{0,12},{2,14},{4,8},{6,10},{8,4},{10,6},{12,0},{14,2},{1,13},{3,15... | collective-permute-start | bytes 294920 | tf_op jit(solution)/shard_map/ppermute | solution.py:165
  9.2 11.0 %collective-permute-start.13 = (bf16[64,768]{1,0:T(8,128)(2,1)S(1)}, bf16[64,768]{1,0:T(8,128)(2,1)S(1)}, u32[]{:S(2)}, u32[]{:S(2)}) collective-permute-start(bf16[64,768]{1,0:T(8,128)(2,1)S(1)} %get-tuple-element.31), channel_id=1, source_target_pairs={{0,14},{2,12},{4,10},{6,8},{8,6},{10,4},{12,2},{14,0},{1,15},{3,13... | collective-permute-start | bytes 294920 | tf_op jit(solution)/shard_map/ppermute | solution.py:165
  9.2 15.3 %collective-permute-start.9 = (bf16[64,768]{1,0:T(8,128)(2,1)S(1)}, bf16[64,768]{1,0:T(8,128)(2,1)S(1)}, u32[]{:S(2)}, u32[]{:S(2)}) collective-permute-start(bf16[64,768]{1,0:T(8,128)(2,1)S(1)} %get-tuple-element.29), channel_id=1, source_target_pairs={{0,10},{2,8},{4,14},{6,12},{8,2},{10,0},{12,6},{14,4},{1,11},{3,9}... | collective-permute-start | bytes 294920 | tf_op jit(solution)/shard_map/ppermute | solution.py:165
  11.1 13.4 %collective-permute-start.3 = (bf16[64,768]{1,0:T(8,128)(2,1)S(1)}, bf16[64,768]{1,0:T(8,128)(2,1)S(1)}, u32[]{:S(2)}, u32[]{:S(2)}) collective-permute-start(bf16[64,768]{1,0:T(8,128)(2,1)S(1)} %get-tuple-element.26), channel_id=1, source_target_pairs={{0,4},{2,6},{4,0},{6,2},{8,12},{10,14},{12,8},{14,10},{1,5},{3,7},... | collective-permute-start | bytes 294920 | tf_op jit(solution)/shard_map/ppermute | solution.py:165
  14.4 10.5 %collective-permute-start.5 = (bf16[64,768]{1,0:T(8,128)(2,1)S(1)}, bf16[64,768]{1,0:T(8,128)(2,1)S(1)}, u32[]{:S(2)}, u32[]{:S(2)}) collective-permute-start(bf16[64,768]{1,0:T(8,128)(2,1)S(1)} %get-tuple-element.27), channel_id=1, source_target_pairs={{0,6},{2,4},{4,2},{6,0},{8,14},{10,12},{12,10},{14,8},{1,7},{3,5},... | collective-permute-start | bytes 294920 | tf_op jit(solution)/shard_map/ppermute | solution.py:165
  14.5 11.1 %collective-permute-start.7 = (bf16[64,768]{1,0:T(8,128)(2,1)S(1)}, bf16[64,768]{1,0:T(8,128)(2,1)S(1)}, u32[]{:S(2)}, u32[]{:S(2)}) collective-permute-start(bf16[64,768]{1,0:T(8,128)(2,1)S(1)} %get-tuple-element.28), channel_id=1, source_target_pairs={{0,8},{2,10},{4,12},{6,14},{8,0},{10,2},{12,4},{14,6},{1,9},{3,11}... | collective-permute-start | bytes 294920 | tf_op jit(solution)/shard_map/ppermute | solution.py:165
  20.2 5.4 %collective-permute-start = (bf16[64,768]{1,0:T(8,128)(2,1)S(1)}, bf16[64,768]{1,0:T(8,128)(2,1)S(1)}, u32[]{:S(2)}, u32[]{:S(2)}) collective-permute-start(bf16[64,768]{1,0:T(8,128)(2,1)S(1)} %get-tuple-element.24.refs_0_), channel_id=1, source_target_pairs={{0,1},{1,0},{2,3},{3,2},{4,5},{5,4},{6,7},{7,6},{8,9},{9,8},{10,11... | collective-permute-start | bytes 294920 | tf_op jit(solution)/shard_map/ppermute | solution.py:165
  24.4 1.7 %collective-permute-start.10 = (bf16[64,768]{1,0:T(8,128)(2,1)S(1)}, bf16[64,768]{1,0:T(8,128)(2,1)S(1)}, u32[]{:S(2)}, u32[]{:S(2)}) collective-permute-start(bf16[64,768]{1,0:T(8,128)(2,1)S(1)} %collective-permute-done.9.refs_5_), channel_id=1, source_target_pairs={{0,1},{1,0},{2,3},{3,2},{4,5},{5,4},{6,7},{7,6},{8,9},{9,8},{10,11... | collective-permute-start | bytes 294920 | tf_op jit(solution)/shard_map/ppermute | solution.py:165
  24.4 1.7 %collective-permute-start.12 = (bf16[64,768]{1,0:T(8,128)(2,1)S(1)}, bf16[64,768]{1,0:T(8,128)(2,1)S(1)}, u32[]{:S(2)}, u32[]{:S(2)}) collective-permute-start(bf16[64,768]{1,0:T(8,128)(2,1)S(1)} %collective-permute-done.11.refs_6_), channel_id=1, source_target_pairs={{0,1},{1,0},{2,3},{3,2},{4,5},{5,4},{6,7},{7,6},{8,9},{9,8},{10,11... | collective-permute-start | bytes 294920 | tf_op jit(solution)/shard_map/ppermute | solution.py:165
  25.0 2.4 %collective-permute-start.14 = (bf16[64,768]{1,0:T(8,128)(2,1)S(1)}, bf16[64,768]{1,0:T(8,128)(2,1)S(1)}, u32[]{:S(2)}, u32[]{:S(2)}) collective-permute-start(bf16[64,768]{1,0:T(8,128)(2,1)S(1)} %collective-permute-done.13.refs_7_), channel_id=1, source_target_pairs={{0,1},{1,0},{2,3},{3,2},{4,5},{5,4},{6,7},{7,6},{8,9},{9,8},{10,11... | collective-permute-start | bytes 294920 | tf_op jit(solution)/shard_map/ppermute | solution.py:165
  25.6 1.8 %collective-permute-start.2 = (bf16[64,768]{1,0:T(8,128)(2,1)S(1)}, bf16[64,768]{1,0:T(8,128)(2,1)S(1)}, u32[]{:S(2)}, u32[]{:S(2)}) collective-permute-start(bf16[64,768]{1,0:T(8,128)(2,1)S(1)} %collective-permute-done.1.refs_1_), channel_id=1, source_target_pairs={{0,1},{1,0},{2,3},{3,2},{4,5},{5,4},{6,7},{7,6},{8,9},{9,8},{10,11... | collective-permute-start | bytes 294920 | tf_op jit(solution)/shard_map/ppermute | solution.py:165
  25.6 1.8 %collective-permute-start.4 = (bf16[64,768]{1,0:T(8,128)(2,1)S(1)}, bf16[64,768]{1,0:T(8,128)(2,1)S(1)}, u32[]{:S(2)}, u32[]{:S(2)}) collective-permute-start(bf16[64,768]{1,0:T(8,128)(2,1)S(1)} %collective-permute-done.3.refs_2_), channel_id=1, source_target_pairs={{0,1},{1,0},{2,3},{3,2},{4,5},{5,4},{6,7},{7,6},{8,9},{9,8},{10,11... | collective-permute-start | bytes 294920 | tf_op jit(solution)/shard_map/ppermute | solution.py:165
  26.1 1.3 %collective-permute-start.6 = (bf16[64,768]{1,0:T(8,128)(2,1)S(1)}, bf16[64,768]{1,0:T(8,128)(2,1)S(1)}, u32[]{:S(2)}, u32[]{:S(2)}) collective-permute-start(bf16[64,768]{1,0:T(8,128)(2,1)S(1)} %collective-permute-done.5.refs_3_), channel_id=1, source_target_pairs={{0,1},{1,0},{2,3},{3,2},{4,5},{5,4},{6,7},{7,6},{8,9},{9,8},{10,11... | collective-permute-start | bytes 294920 | tf_op jit(solution)/shard_map/ppermute | solution.py:165
  26.2 1.4 %collective-permute-start.8 = (bf16[64,768]{1,0:T(8,128)(2,1)S(1)}, bf16[64,768]{1,0:T(8,128)(2,1)S(1)}, u32[]{:S(2)}, u32[]{:S(2)}) collective-permute-start(bf16[64,768]{1,0:T(8,128)(2,1)S(1)} %collective-permute-done.7.refs_4_), channel_id=1, source_target_pairs={{0,1},{1,0},{2,3},{3,2},{4,5},{5,4},{6,7},{7,6},{8,9},{9,8},{10,11... | collective-permute-start | bytes 294920 | tf_op jit(solution)/shard_map/ppermute | solution.py:165
  28.3 7.1 %collective-permute-start.15 = (f32[1,64]{1,0:T(1,128)S(1)}, f32[1,64]{1,0:T(1,128)S(1)}, u32[]{:S(2)}, u32[]{:S(2)}) collective-permute-start(f32[1,64]{1,0:T(1,128)S(1)} %get-tuple-element.35), channel_id=1, source_target_pairs={{0,2},{2,0},{4,6},{6,4},{8,10},{10,8},{12,14},{14,12},{1,3},{3,1},... | collective-permute-start | bytes 776 | tf_op jit(solution)/shard_map/ppermute | solution.py:165
  29.5 8.4 %collective-permute-start.16 = (f32[1,64]{1,0:T(1,128)S(1)}, f32[1,64]{1,0:T(1,128)S(1)}, u32[]{:S(2)}, u32[]{:S(2)}) collective-permute-start(f32[1,64]{1,0:T(1,128)S(1)} %get-tuple-element.36), channel_id=1, source_target_pairs={{0,4},{2,6},{4,0},{6,2},{8,12},{10,14},{12,8},{14,10},{1,5},{3,7},... | collective-permute-start | bytes 776 | tf_op jit(solution)/shard_map/ppermute | solution.py:165
  29.5 9.9 %collective-permute-start.17 = (f32[1,64]{1,0:T(1,128)S(1)}, f32[1,64]{1,0:T(1,128)S(1)}, u32[]{:S(2)}, u32[]{:S(2)}) collective-permute-start(f32[1,64]{1,0:T(1,128)S(1)} %get-tuple-element.37), channel_id=1, source_target_pairs={{0,6},{2,4},{4,2},{6,0},{8,14},{10,12},{12,10},{14,8},{1,7},{3,5},... | collective-permute-start | bytes 776 | tf_op jit(solution)/shard_map/ppermute | solution.py:165
  31.8 7.7 %collective-permute-start.18 = (f32[1,64]{1,0:T(1,128)S(1)}, f32[1,64]{1,0:T(1,128)S(1)}, u32[]{:S(2)}, u32[]{:S(2)}) collective-permute-start(f32[1,64]{1,0:T(1,128)S(1)} %get-tuple-element.38), channel_id=1, source_target_pairs={{0,8},{2,10},{4,12},{6,14},{8,0},{10,2},{12,4},{14,6},{1,9},{3,11}... | collective-permute-start | bytes 776 | tf_op jit(solution)/shard_map/ppermute | solution.py:165
  32.8 6.6 %collective-permute-start.19 = (f32[1,64]{1,0:T(1,128)S(1)}, f32[1,64]{1,0:T(1,128)S(1)}, u32[]{:S(2)}, u32[]{:S(2)}) collective-permute-start(f32[1,64]{1,0:T(1,128)S(1)} %get-tuple-element.39), channel_id=1, source_target_pairs={{0,10},{2,8},{4,14},{6,12},{8,2},{10,0},{12,6},{14,4},{1,11},{3,9}... | collective-permute-start | bytes 776 | tf_op jit(solution)/shard_map/ppermute | solution.py:165
  35.4 5.3 %collective-permute-start.20 = (f32[1,64]{1,0:T(1,128)S(1)}, f32[1,64]{1,0:T(1,128)S(1)}, u32[]{:S(2)}, u32[]{:S(2)}) collective-permute-start(f32[1,64]{1,0:T(1,128)S(1)} %get-tuple-element.40), channel_id=1, source_target_pairs={{0,12},{2,14},{4,8},{6,10},{8,4},{10,6},{12,0},{14,2},{1,13},{3,15... | collective-permute-start | bytes 776 | tf_op jit(solution)/shard_map/ppermute | solution.py:165
  37.9 6.2 %collective-permute-start.21 = (f32[1,64]{1,0:T(1,128)S(1)}, f32[1,64]{1,0:T(1,128)S(1)}, u32[]{:S(2)}, u32[]{:S(2)}) collective-permute-start(f32[1,64]{1,0:T(1,128)S(1)} %get-tuple-element.41), channel_id=1, source_target_pairs={{0,14},{2,12},{4,10},{6,8},{8,6},{10,4},{12,2},{14,0},{1,15},{3,13... | collective-permute-start | bytes 776 | tf_op jit(solution)/shard_map/ppermute | solution.py:165

commit v2 on v1

--- a/solution.py
+++ b/solution.py
@@ -12,6 +12,7 @@
 EMPTY_MARK = 2.0
 EMPTY_ABOVE = 1.5
 DIRECT_OWNERS = 8
+SCORE_LANES = 128
 
 
 def vmem(count):
@@ -111,35 +112,36 @@
     )(*blocks)
 
 
-def cross_kernel(owners, *refs):
-    block_refs, joined_ref, total_ref = refs[:owners], refs[owners], refs[owners + 1]
-    score_refs = refs[owners + 2:2 * owners + 2]
-    others_ref = refs[-1]
+def cross_kernel(owners, me_ref, *refs):
+    block_refs, joined_ref, total_ref, score_ref, others_ref = refs[:owners], *refs[owners:]
+    me = me_ref[0]
     capacity = block_refs[0].shape[0]
     for k, block_ref in enumerate(block_refs):
         others_ref[k * capacity:(k + 1) * capacity, :] = block_ref[...]
     total = total_ref[...] + partial_sums(joined_ref[...], others_ref[...], block_refs, False)
     scores = jnp.log(jnp.where(total > 0.0, total, 1.0))
-    for k, score_ref in enumerate(score_refs):
-        score_ref[...] = scores[:, k * capacity:(k + 1) * capacity]
-
-
-def cross_scores(blocks, joined, total):
+    for k in range(owners):
+        score_ref[pl.ds(me ^ k, 1), 0:capacity] = scores[:, k * capacity:(k + 1) * capacity]
+
+
+def cross_scores(me, blocks, joined, total):
     capacity, width = blocks[0].shape
     slots = len(blocks) * capacity
     return pl.pallas_call(
         functools.partial(cross_kernel, len(blocks)),
-        out_shape=[jax.ShapeDtypeStruct((1, capacity), jnp.float32)] * len(blocks),
-        in_specs=vmem(len(blocks) + 2),
-        out_specs=vmem(len(blocks)),
+        out_shape=jax.ShapeDtypeStruct((len(blocks), SCORE_LANES), jnp.float32),
+        in_specs=[pl.BlockSpec(memory_space=pltpu.SMEM)] + vmem(len(blocks) + 2),
+        out_specs=pl.BlockSpec(memory_space=pltpu.VMEM),
         scratch_shapes=[pltpu.VMEM((slots, width), jnp.bfloat16)],
         compiler_params=params(),
-    )(*blocks, joined, total)
-
-
-def collect_kernel(owners, *refs):
-    score_refs, pick_ref, out_ref = refs[:owners], refs[owners], refs[owners + 1]
-    scores = jnp.concatenate([score_ref[...] for score_ref in score_refs], axis=1)
+    )(me, *blocks, joined, total)
+
+
+def collect_kernel(capacity, me_ref, score_ref, pick_ref, out_ref):
+    me = me_ref[0]
+    scores = jnp.concatenate(
+        [score_ref[pl.ds(me ^ k, 1), 0:capacity] for k in range(score_ref.shape[0])], axis=1
+    )
     high = scores.astype(jnp.bfloat16)
     rest = scores - high.astype(jnp.float32)
     middle = rest.astype(jnp.bfloat16)
@@ -149,14 +151,14 @@
     out_ref[...] = jnp.reshape((parts[0] + parts[1]) + parts[2], out_ref.shape)
 
 
-def collect(scores, pick):
-    return pl.pallas_call(
-        functools.partial(collect_kernel, len(scores)),
+def collect(me, scores, pick, capacity):
+    return pl.pallas_call(
+        functools.partial(collect_kernel, capacity),
         out_shape=jax.ShapeDtypeStruct((pick.shape[1],), jnp.float32),
-        in_specs=vmem(len(scores) + 1),
+        in_specs=[pl.BlockSpec(memory_space=pltpu.SMEM)] + vmem(2),
         out_specs=pl.BlockSpec(memory_space=pltpu.VMEM),
         compiler_params=params(),
-    )(*scores, pick)
+    )(me, scores, pick)
 
 
 def swap(block, axis, step, size):
@@ -175,9 +177,9 @@
         own_blocks[k] = swap(blocks[k], "blk", k, owners)
     other_blocks = [swap(block, "pair", 1, 2) for block in own_blocks]
     joined, total = own_sums(own_blocks)
-    scores = cross_scores(other_blocks, joined, total)
-    returned = [swap(scores[k], "blk", k, owners) for k in range(owners)]
-    return collect(returned, pick)
+    scores = cross_scores(me, other_blocks, joined, total)
+    returned = lax.all_to_all(scores, "blk", split_axis=0, concat_axis=0, tiled=True)
+    return collect(me, returned, pick, capacity)
 
 
 def unit_vectors(values):

time: 45.1 us -> 40 us (0.89)
  starting transfers between devices: 30.4 us -> 19.2 us
  blocking collectives: 0 us -> 10.7 us
  waiting for transfers between devices: 9.74 us -> 5.03 us
    ppermute x22 -> x15, starting transfers between devices: 30.4 us -> 19.2 us  [swap(): return lax.ppermute(block, axis, [(i, i ^ step) for i in range(size)])]
    all_to_all x0 -> x1, blocking collectives: none -> 10.7 us  [direct_shards(): lax.all_to_all(scores, 'blk', split_axis=0, concat_axis=0, tiled=True)]
    ppermute x22 -> x15, waiting for transfers between devices: 9.74 us -> 5.03 us  [swap(): return lax.ppermute(block, axis, [(i, i ^ step) for i in range(size)])]
  transfers between devices with their start and end apart: 22 -> 15, of which waited for: 5 -> 4; matrix products, arithmetic and copies ran while one was open for 0% -> 0% of each run, Pallas kernels for 2% -> 2%
where the time goes in v2:
time: 40 us; the launch traced here: 39.8 us
  starting transfers between devices  19.2 us (48%)
  blocking collectives  10.7 us (27%)
  waiting for transfers between devices  5.03 us (13%)
  Pallas kernels  3.14 us (8%)
  local copies, waits for them, and re-layouts  1.67 us (4%)
    ppermute x15, starting transfers between devices, swap(): return lax.ppermute(block, axis, [(i, i ^ step) for i in range(size)])  19.2 us
    all_to_all x1, blocking collectives, direct_shards(): lax.all_to_all(scores, 'blk', split_axis=0, concat_axis=0, tiled=True)  10.7 us
    ppermute x15, waiting for transfers between devices, swap(): return lax.ppermute(block, axis, [(i, i ^ step) for i in range(size)])  5.03 us
    unnamed x4, local copies, waits for them, and re-layouts  1.67 us
    pallas_call x1, Pallas kernels, prepare(): pl.pallas_call(functools.partial(prepare_kernel, owners, capacity), out_s...  0.89 us
    pallas_call x1, Pallas kernels, collect(): pl.pallas_call(functools.partial(collect_kernel, capacity), out_shape=jax...  0.83 us
  transfers between devices with their start and end apart: 15, of which 4 were waited for; matrix products, arithmetic and copies ran while one was open for 0% of the time, Pallas kernels for 2%

profile of v2, /device:TPU:0, one launch (start us, length us, event | category | flops | bytes accessed | tf_op | source)
XLA Modules:
  0.0 39.8 jit_solution(4220978013347836320)
XLA Ops:
  0.0 0.7 %copy-done.1 = s32[256]{0:T(256)S(1)} copy-done((s32[256]{0:T(256)S(1)}, s32[256]{0:T(256)}, u32[]{:S(2)}) %copy-start.1) | copy-done | bytes 1048
  0.7 1.0 %copy-done = bf16[256,768]{1,0:T(8,128)(2,1)S(1)} copy-done((bf16[256,768]{1,0:T(8,128)(2,1)S(1)}, bf16[256,768]{1,0:T(8,128)(2,1)}, u32[]{:S(2)}) %copy-start) | copy-done | bytes 393240
  1.7 0.9 %shard_map.28 = (bf16[64,768]{1,0:T(8,128)(2,1)S(1)}, bf16[64,768]{1,0:T(8,128)(2,1)S(1)}, bf16[64,768]{1,0:T(8,128)(2,1)S(1)}, bf16[64,768]{1,0:T(8,128)(2,1)S(...) custom-call(s32[1]{0:T(128)} %bitcast.me_ref, ...), custom_call_target="tpu_custom_call" | custom-call | tf_op jit(solution)/shard_map/pallas_call | solution.py:64
  2.6 3.0 %collective-permute-start.1 = (bf16[64,768]{1,0:T(8,128)(2,1)S(1)}, bf16[64,768]{1,0:T(8,128)(2,1)S(1)}, u32[]{:S(2)}, u32[]{:S(2)}) collective-permute-start(bf16[64,768]{1,0:T(8,128)(2,1)S(1)} %get-tuple-element.17), channel_id=1, source_target_pairs={{0,2},{2,0},{4,6},{6,4},{8,10},{10,8},{12,14},{14,12},{1,3},{3,1},... | collective-permute-start | bytes 294920 | tf_op jit(solution)/shard_map/ppermute | solution.py:167
  5.6 3.6 %collective-permute-start.11 = (bf16[64,768]{1,0:T(8,128)(2,1)S(1)}, bf16[64,768]{1,0:T(8,128)(2,1)S(1)}, u32[]{:S(2)}, u32[]{:S(2)}) collective-permute-start(bf16[64,768]{1,0:T(8,128)(2,1)S(1)} %get-tuple-element.22), channel_id=1, source_target_pairs={{0,12},{2,14},{4,8},{6,10},{8,4},{10,6},{12,0},{14,2},{1,13},{3,15... | collective-permute-start | bytes 294920 | tf_op jit(solution)/shard_map/ppermute | solution.py:167
  9.2 1.9 %collective-permute-start.9 = (bf16[64,768]{1,0:T(8,128)(2,1)S(1)}, bf16[64,768]{1,0:T(8,128)(2,1)S(1)}, u32[]{:S(2)}, u32[]{:S(2)}) collective-permute-start(bf16[64,768]{1,0:T(8,128)(2,1)S(1)} %get-tuple-element.21), channel_id=1, source_target_pairs={{0,10},{2,8},{4,14},{6,12},{8,2},{10,0},{12,6},{14,4},{1,11},{3,9}... | collective-permute-start | bytes 294920 | tf_op jit(solution)/shard_map/ppermute | solution.py:167
  11.1 3.4 %collective-permute-start.3 = (bf16[64,768]{1,0:T(8,128)(2,1)S(1)}, bf16[64,768]{1,0:T(8,128)(2,1)S(1)}, u32[]{:S(2)}, u32[]{:S(2)}) collective-permute-start(bf16[64,768]{1,0:T(8,128)(2,1)S(1)} %get-tuple-element.18), channel_id=1, source_target_pairs={{0,4},{2,6},{4,0},{6,2},{8,12},{10,14},{12,8},{14,10},{1,5},{3,7},... | collective-permute-start | bytes 294920 | tf_op jit(solution)/shard_map/ppermute | solution.py:167
  14.4 0.0 collective-permute-done.1.refs_1_
  14.4 0.0 collective-permute-start.5
  14.5 0.0 collective-permute-done.11.refs_6_
  14.5 5.7 %collective-permute-start.7 = (bf16[64,768]{1,0:T(8,128)(2,1)S(1)}, bf16[64,768]{1,0:T(8,128)(2,1)S(1)}, u32[]{:S(2)}, u32[]{:S(2)}) collective-permute-start(bf16[64,768]{1,0:T(8,128)(2,1)S(1)} %get-tuple-element.20), channel_id=1, source_target_pairs={{0,8},{2,10},{4,12},{6,14},{8,0},{10,2},{12,4},{14,6},{1,9},{3,11}... | collective-permute-start | bytes 294920 | tf_op jit(solution)/shard_map/ppermute | solution.py:167
  20.2 4.2 %collective-permute-done.9.refs_5_ = bf16[64,768]{1,0:T(8,128)(2,1)S(1)} collective-permute-done((bf16[64,768]{1,0:T(8,128)(2,1)S(1)}, bf16[64,768]{1,0:T(8,128)(2,1)S(1)}, u32[]{:S(2)}, u32[]{:S(2)}) %collective-permute-start.9) | collective-permute-done | bytes 98336 | tf_op jit(solution)/shard_map/ppermute | solution.py:167
  24.4 0.5 %collective-permute-start.12 = (bf16[64,768]{1,0:T(8,128)(2,1)S(1)}, bf16[64,768]{1,0:T(8,128)(2,1)S(1)}, u32[]{:S(2)}, u32[]{:S(2)}) collective-permute-start(bf16[64,768]{1,0:T(8,128)(2,1)S(1)} %collective-permute-done.11.refs_6_), channel_id=1, source_target_pairs={{0,1},{1,0},{2,3},{3,2},{4,5},{5,4},{6,7},{7,6},{8,9},{9,8},{10,11... | collective-permute-start | bytes 294920 | tf_op jit(solution)/shard_map/ppermute | solution.py:167
  25.0 0.1 collective-permute-start.14
  25.0 0.5 %collective-permute-done.7.refs_4_ = bf16[64,768]{1,0:T(8,128)(2,1)S(1)} collective-permute-done((bf16[64,768]{1,0:T(8,128)(2,1)S(1)}, bf16[64,768]{1,0:T(8,128)(2,1)S(1)}, u32[]{:S(2)}, u32[]{:S(2)}) %collective-permute-start.7) | collective-permute-done | bytes 98336 | tf_op jit(solution)/shard_map/ppermute | solution.py:167
  25.6 0.5 %collective-permute-start.4 = (bf16[64,768]{1,0:T(8,128)(2,1)S(1)}, bf16[64,768]{1,0:T(8,128)(2,1)S(1)}, u32[]{:S(2)}, u32[]{:S(2)}) collective-permute-start(bf16[64,768]{1,0:T(8,128)(2,1)S(1)} %collective-permute-done.3.refs_2_), channel_id=1, source_target_pairs={{0,1},{1,0},{2,3},{3,2},{4,5},{5,4},{6,7},{7,6},{8,9},{9,8},{10,11... | collective-permute-start | bytes 294920 | tf_op jit(solution)/shard_map/ppermute | solution.py:167
  26.1 0.1 collective-permute-start.6
  26.2 0.4 %collective-permute-start.8 = (bf16[64,768]{1,0:T(8,128)(2,1)S(1)}, bf16[64,768]{1,0:T(8,128)(2,1)S(1)}, u32[]{:S(2)}, u32[]{:S(2)}) collective-permute-start(bf16[64,768]{1,0:T(8,128)(2,1)S(1)} %collective-permute-done.7.refs_4_), channel_id=1, source_target_pairs={{0,1},{1,0},{2,3},{3,2},{4,5},{5,4},{6,7},{7,6},{8,9},{9,8},{10,11... | collective-permute-start | bytes 294920 | tf_op jit(solution)/shard_map/ppermute | solution.py:167
  26.6 0.7 %shard_map.29 = (bf16[512,768]{1,0:T(8,128)(2,1)S(1)}, f32[1,512]{1,0:T(1,128)S(1)}) custom-call(bf16[64,768]{1,0:T(8,128)(2,1)S(1)} %get-tuple-element.16.refs_0_, bf16[64,768]{1,0:T(8,128)(2,1)S(1)} %collective-permute-done.1.refs_1_, bf16[64,768]{1,0:T(8,128)(2,1)S(1)} %collective-permute-done.3.refs_2_, ...), custom_call_target="tpu_custom_call" | custom-call | flops 402653184 | bytes 1572864 | tf_op jit(solution)/shard_map/pallas_call | solution.py:100
  27.3 0.1 collective-permute-done.6.refs_3_
  27.4 0.2 collective-permute-done.8.refs_4_
  27.5 0.7 %shard_map.30 = f32[8,128]{1,0:T(8,128)S(1)} custom-call(s32[1]{0:T(128)} %bitcast.me_ref, bf16[64,768]{1,0:T(8,128)(2,1)S(1)} %collective-permute-done.refs_0_, bf16[64,768]{1,0:T(8,128)(2,1)S(1)} %collective-permute-done.2.refs_1_, bf16[64,768]{1,0:T(8,128)(2,1)S(1)} %collective-permute-done.4.refs_2_, bf16[64,768]{1,0:T(8,128)(2,1)S(1)} %collective-permute-done.6.refs_3_, ...), custom_call_target="tpu_custom_call" | custom-call | tf_op jit(solution)/shard_map/pallas_call | solution.py:130
  28.3 10.7 %all_to_all.11 = f32[8,1,128]{2,1,0:T(1,128)S(1)} all-to-all(f32[8,1,128]{2,1,0:T(1,128)S(1)} %bitcast.5), channel_id=1, replica_groups=mesh['groups'=2,'blk'=8,'pair'=2] {'blk'}, dimensions={0} | all-to-all | bytes 8192 | tf_op jit(solution)/shard_map/all_to_all | solution.py:181
  39.0 0.8 %shard_map.31 = f32[256]{0:T(256)} custom-call(s32[1]{0:T(128)} %bitcast.me_ref, f32[8,128]{1,0:T(8,128)S(1)} %bitcast.6, bf16[512,256]{1,0:T(8,128)(2,1)S(1)} %get-tuple-element.26.pick_ref), custom_call_target="tpu_custom_call" | custom-call | tf_op jit(solution)/shard_map/pallas_call | solution.py:155
  (15 shorter events, 0.0 us)
Async XLA Ops:
  0.0 0.7 %copy-start.1 = (s32[256]{0:T(256)S(1)}, s32[256]{0:T(256)}, u32[]{:S(2)}) copy-start(s32[256]{0:T(256)} %ids_ref.1) | copy-start | bytes 3076
  0.7 1.0 %copy-start = (bf16[256,768]{1,0:T(8,128)(2,1)S(1)}, bf16[256,768]{1,0:T(8,128)(2,1)}, u32[]{:S(2)}) copy-start(bf16[256,768]{1,0:T(8,128)(2,1)} %rows_ref.1) | copy-start | bytes 1179652
  2.6 11.9 %collective-permute-start.1 = (bf16[64,768]{1,0:T(8,128)(2,1)S(1)}, bf16[64,768]{1,0:T(8,128)(2,1)S(1)}, u32[]{:S(2)}, u32[]{:S(2)}) collective-permute-start(bf16[64,768]{1,0:T(8,128)(2,1)S(1)} %get-tuple-element.17), channel_id=1, source_target_pairs={{0,2},{2,0},{4,6},{6,4},{8,10},{10,8},{12,14},{14,12},{1,3},{3,1},... | collective-permute-start | bytes 294920 | tf_op jit(solution)/shard_map/ppermute | solution.py:167
  5.6 8.9 %collective-permute-start.11 = (bf16[64,768]{1,0:T(8,128)(2,1)S(1)}, bf16[64,768]{1,0:T(8,128)(2,1)S(1)}, u32[]{:S(2)}, u32[]{:S(2)}) collective-permute-start(bf16[64,768]{1,0:T(8,128)(2,1)S(1)} %get-tuple-element.22), channel_id=1, source_target_pairs={{0,12},{2,14},{4,8},{6,10},{8,4},{10,6},{12,0},{14,2},{1,13},{3,15... | collective-permute-start | bytes 294920 | tf_op jit(solution)/shard_map/ppermute | solution.py:167
  9.2 11.0 %collective-permute-start.13 = (bf16[64,768]{1,0:T(8,128)(2,1)S(1)}, bf16[64,768]{1,0:T(8,128)(2,1)S(1)}, u32[]{:S(2)}, u32[]{:S(2)}) collective-permute-start(bf16[64,768]{1,0:T(8,128)(2,1)S(1)} %get-tuple-element.23), channel_id=1, source_target_pairs={{0,14},{2,12},{4,10},{6,8},{8,6},{10,4},{12,2},{14,0},{1,15},{3,13... | collective-permute-start | bytes 294920 | tf_op jit(solution)/shard_map/ppermute | solution.py:167
  9.2 15.3 %collective-permute-start.9 = (bf16[64,768]{1,0:T(8,128)(2,1)S(1)}, bf16[64,768]{1,0:T(8,128)(2,1)S(1)}, u32[]{:S(2)}, u32[]{:S(2)}) collective-permute-start(bf16[64,768]{1,0:T(8,128)(2,1)S(1)} %get-tuple-element.21), channel_id=1, source_target_pairs={{0,10},{2,8},{4,14},{6,12},{8,2},{10,0},{12,6},{14,4},{1,11},{3,9}... | collective-permute-start | bytes 294920 | tf_op jit(solution)/shard_map/ppermute | solution.py:167
  11.1 13.4 %collective-permute-start.3 = (bf16[64,768]{1,0:T(8,128)(2,1)S(1)}, bf16[64,768]{1,0:T(8,128)(2,1)S(1)}, u32[]{:S(2)}, u32[]{:S(2)}) collective-permute-start(bf16[64,768]{1,0:T(8,128)(2,1)S(1)} %get-tuple-element.18), channel_id=1, source_target_pairs={{0,4},{2,6},{4,0},{6,2},{8,12},{10,14},{12,8},{14,10},{1,5},{3,7},... | collective-permute-start | bytes 294920 | tf_op jit(solution)/shard_map/ppermute | solution.py:167
  14.4 10.5 %collective-permute-start.5 = (bf16[64,768]{1,0:T(8,128)(2,1)S(1)}, bf16[64,768]{1,0:T(8,128)(2,1)S(1)}, u32[]{:S(2)}, u32[]{:S(2)}) collective-permute-start(bf16[64,768]{1,0:T(8,128)(2,1)S(1)} %get-tuple-element.19), channel_id=1, source_target_pairs={{0,6},{2,4},{4,2},{6,0},{8,14},{10,12},{12,10},{14,8},{1,7},{3,5},... | collective-permute-start | bytes 294920 | tf_op jit(solution)/shard_map/ppermute | solution.py:167
  14.5 11.1 %collective-permute-start.7 = (bf16[64,768]{1,0:T(8,128)(2,1)S(1)}, bf16[64,768]{1,0:T(8,128)(2,1)S(1)}, u32[]{:S(2)}, u32[]{:S(2)}) collective-permute-start(bf16[64,768]{1,0:T(8,128)(2,1)S(1)} %get-tuple-element.20), channel_id=1, source_target_pairs={{0,8},{2,10},{4,12},{6,14},{8,0},{10,2},{12,4},{14,6},{1,9},{3,11}... | collective-permute-start | bytes 294920 | tf_op jit(solution)/shard_map/ppermute | solution.py:167
  20.2 5.4 %collective-permute-start = (bf16[64,768]{1,0:T(8,128)(2,1)S(1)}, bf16[64,768]{1,0:T(8,128)(2,1)S(1)}, u32[]{:S(2)}, u32[]{:S(2)}) collective-permute-start(bf16[64,768]{1,0:T(8,128)(2,1)S(1)} %get-tuple-element.16.refs_0_), channel_id=1, source_target_pairs={{0,1},{1,0},{2,3},{3,2},{4,5},{5,4},{6,7},{7,6},{8,9},{9,8},{10,11... | collective-permute-start | bytes 294920 | tf_op jit(solution)/shard_map/ppermute | solution.py:167
  24.4 1.7 %collective-permute-start.10 = (bf16[64,768]{1,0:T(8,128)(2,1)S(1)}, bf16[64,768]{1,0:T(8,128)(2,1)S(1)}, u32[]{:S(2)}, u32[]{:S(2)}) collective-permute-start(bf16[64,768]{1,0:T(8,128)(2,1)S(1)} %collective-permute-done.9.refs_5_), channel_id=1, source_target_pairs={{0,1},{1,0},{2,3},{3,2},{4,5},{5,4},{6,7},{7,6},{8,9},{9,8},{10,11... | collective-permute-start | bytes 294920 | tf_op jit(solution)/shard_map/ppermute | solution.py:167
  24.4 1.7 %collective-permute-start.12 = (bf16[64,768]{1,0:T(8,128)(2,1)S(1)}, bf16[64,768]{1,0:T(8,128)(2,1)S(1)}, u32[]{:S(2)}, u32[]{:S(2)}) collective-permute-start(bf16[64,768]{1,0:T(8,128)(2,1)S(1)} %collective-permute-done.11.refs_6_), channel_id=1, source_target_pairs={{0,1},{1,0},{2,3},{3,2},{4,5},{5,4},{6,7},{7,6},{8,9},{9,8},{10,11... | collective-permute-start | bytes 294920 | tf_op jit(solution)/shard_map/ppermute | solution.py:167
  25.0 2.4 %collective-permute-start.14 = (bf16[64,768]{1,0:T(8,128)(2,1)S(1)}, bf16[64,768]{1,0:T(8,128)(2,1)S(1)}, u32[]{:S(2)}, u32[]{:S(2)}) collective-permute-start(bf16[64,768]{1,0:T(8,128)(2,1)S(1)} %collective-permute-done.13.refs_7_), channel_id=1, source_target_pairs={{0,1},{1,0},{2,3},{3,2},{4,5},{5,4},{6,7},{7,6},{8,9},{9,8},{10,11... | collective-permute-start | bytes 294920 | tf_op jit(solution)/shard_map/ppermute | solution.py:167
  25.6 1.7 %collective-permute-start.2 = (bf16[64,768]{1,0:T(8,128)(2,1)S(1)}, bf16[64,768]{1,0:T(8,128)(2,1)S(1)}, u32[]{:S(2)}, u32[]{:S(2)}) collective-permute-start(bf16[64,768]{1,0:T(8,128)(2,1)S(1)} %collective-permute-done.1.refs_1_), channel_id=1, source_target_pairs={{0,1},{1,0},{2,3},{3,2},{4,5},{5,4},{6,7},{7,6},{8,9},{9,8},{10,11... | collective-permute-start | bytes 294920 | tf_op jit(solution)/shard_map/ppermute | solution.py:167
  25.6 1.7 %collective-permute-start.4 = (bf16[64,768]{1,0:T(8,128)(2,1)S(1)}, bf16[64,768]{1,0:T(8,128)(2,1)S(1)}, u32[]{:S(2)}, u32[]{:S(2)}) collective-permute-start(bf16[64,768]{1,0:T(8,128)(2,1)S(1)} %collective-permute-done.3.refs_2_), channel_id=1, source_target_pairs={{0,1},{1,0},{2,3},{3,2},{4,5},{5,4},{6,7},{7,6},{8,9},{9,8},{10,11... | collective-permute-start | bytes 294920 | tf_op jit(solution)/shard_map/ppermute | solution.py:167
  26.1 1.3 %collective-permute-start.6 = (bf16[64,768]{1,0:T(8,128)(2,1)S(1)}, bf16[64,768]{1,0:T(8,128)(2,1)S(1)}, u32[]{:S(2)}, u32[]{:S(2)}) collective-permute-start(bf16[64,768]{1,0:T(8,128)(2,1)S(1)} %collective-permute-done.5.refs_3_), channel_id=1, source_target_pairs={{0,1},{1,0},{2,3},{3,2},{4,5},{5,4},{6,7},{7,6},{8,9},{9,8},{10,11... | collective-permute-start | bytes 294920 | tf_op jit(solution)/shard_map/ppermute | solution.py:167
  26.2 1.4 %collective-permute-start.8 = (bf16[64,768]{1,0:T(8,128)(2,1)S(1)}, bf16[64,768]{1,0:T(8,128)(2,1)S(1)}, u32[]{:S(2)}, u32[]{:S(2)}) collective-permute-start(bf16[64,768]{1,0:T(8,128)(2,1)S(1)} %collective-permute-done.7.refs_4_), channel_id=1, source_target_pairs={{0,1},{1,0},{2,3},{3,2},{4,5},{5,4},{6,7},{7,6},{8,9},{9,8},{10,11... | collective-permute-start | bytes 294920 | tf_op jit(solution)/shard_map/ppermute | solution.py:167

commit v3 on v2

--- a/solution.py
+++ b/solution.py
@@ -23,14 +23,10 @@
     return pltpu.CompilerParams(vmem_limit_bytes=mib * 1024 * 1024)
 
 
-def prepare_kernel(owners, capacity, me_ref, rows_ref, ids_ref, *outs):
-    block_refs, pick_ref = outs[:-1], outs[-1]
-    me = me_ref[0]
-    row_count, width = rows_ref.shape
-    values = rows_ref[...].astype(jnp.float32)
-    scale = lax.rsqrt(jnp.sum(values * values, axis=1, keepdims=True) + EPSILON)
-    units = (values * scale).astype(jnp.bfloat16)
-    relative = jnp.reshape(ids_ref[...], (1, row_count)) ^ me
+def pick_kernel(owners, capacity, me_ref, ids_ref, pick_ref, empty_ref):
+    row_count = ids_ref.shape[0]
+    step = jnp.reshape(ids_ref[...], (1, row_count)) ^ me_ref[0]
+    relative = sum(jnp.where(step == value, k, 0) for k, value in enumerate(steps_of(owners)))
     labels = lax.broadcasted_iota(jnp.int32, (owners, row_count), 0)
     inside = (labels == relative).astype(jnp.float32)
     above = lax.broadcasted_iota(jnp.int32, (row_count, row_count), 0)
@@ -40,34 +36,46 @@
     rank = jnp.sum(before * inside, axis=0, keepdims=True).astype(jnp.int32)
     slot = relative * capacity + rank
     slots = owners * capacity
-    pick = jnp.where(lax.broadcasted_iota(jnp.int32, (slots, row_count), 0) == slot, 1.0, 0.0).astype(
-        jnp.bfloat16
-    )
-    pick_ref[...] = pick
-    counts = jnp.sum(inside, axis=1, keepdims=True)
-    first = lax.broadcasted_iota(jnp.int32, (capacity, 128), 1) == 0
+    pick_ref[...] = jnp.where(
+        lax.broadcasted_iota(jnp.int32, (slots, row_count), 0) == slot, 1.0, 0.0
+    ).astype(jnp.bfloat16)
+    counts = jnp.broadcast_to(jnp.sum(inside, axis=1, keepdims=True), empty_ref.shape)
+    first = lax.broadcasted_iota(jnp.int32, empty_ref.shape, 1) == 0
+    empty_ref[...] = jnp.where(first & (counts == 0.0), EMPTY_MARK, 0.0)
+
+
+def prepare_kernel(owners, capacity, rows_ref, pick_ref, empty_ref, *block_refs):
+    values = rows_ref[...].astype(jnp.float32)
+    scale = lax.rsqrt(jnp.sum(values * values, axis=1, keepdims=True) + EPSILON)
+    units = (values * scale).astype(jnp.bfloat16)
     for k, block_ref in enumerate(block_refs):
         block = jnp.dot(
-            pick[k * capacity:(k + 1) * capacity], units, preferred_element_type=jnp.float32
-        ).astype(jnp.bfloat16)
-        block_ref[...] = block
-        empty = counts[k:k + 1] == 0.0
-        block_ref[:, 0:128] = jnp.where(
-            first & empty, EMPTY_MARK, block[:, 0:128].astype(jnp.float32)
-        ).astype(jnp.bfloat16)
+            pick_ref[k * capacity:(k + 1) * capacity, :], units, preferred_element_type=jnp.float32
+        )
+        block_ref[...] = block.astype(jnp.bfloat16)
+        block_ref[:, 0:128] = (block[:, 0:128] + empty_ref[k:k + 1, :]).astype(jnp.bfloat16)
 
 
 def prepare(me, rows, ids, owners, capacity):
     row_count, width = rows.shape
-    shapes = [jax.ShapeDtypeStruct((capacity, width), jnp.bfloat16)] * owners
-    shapes.append(jax.ShapeDtypeStruct((owners * capacity, row_count), jnp.bfloat16))
-    return pl.pallas_call(
+    pick, empty = pl.pallas_call(
+        functools.partial(pick_kernel, owners, capacity),
+        out_shape=[
+            jax.ShapeDtypeStruct((owners * capacity, row_count), jnp.bfloat16),
+            jax.ShapeDtypeStruct((owners, 128), jnp.float32),
+        ],
+        in_specs=[pl.BlockSpec(memory_space=pltpu.SMEM)] + vmem(1),
+        out_specs=vmem(2),
+        compiler_params=params(),
+    )(me, ids)
+    blocks = pl.pallas_call(
         functools.partial(prepare_kernel, owners, capacity),
-        out_shape=shapes,
-        in_specs=[pl.BlockSpec(memory_space=pltpu.SMEM)] + vmem(2),
-        out_specs=vmem(len(shapes)),
-        compiler_params=params(),
-    )(me, rows, ids)
+        out_shape=[jax.ShapeDtypeStruct((capacity, width), jnp.bfloat16)] * owners,
+        in_specs=vmem(3),
+        out_specs=vmem(owners),
+        compiler_params=params(),
+    )(rows, pick, empty)
+    return blocks, pick
 
 
 def partial_sums(own, others, others_refs, own_block):
@@ -120,8 +128,8 @@
         others_ref[k * capacity:(k + 1) * capacity, :] = block_ref[...]
     total = total_ref[...] + partial_sums(joined_ref[...], others_ref[...], block_refs, False)
     scores = jnp.log(jnp.where(total > 0.0, total, 1.0))
-    for k in range(owners):
-        score_ref[pl.ds(me ^ k, 1), 0:capacity] = scores[:, k * capacity:(k + 1) * capacity]
+    for k, step in enumerate(steps_of(owners)):
+        score_ref[pl.ds(me ^ step, 1), 0:capacity] = scores[:, k * capacity:(k + 1) * capacity]
 
 
 def cross_scores(me, blocks, joined, total):
@@ -140,15 +148,16 @@
 def collect_kernel(capacity, me_ref, score_ref, pick_ref, out_ref):
     me = me_ref[0]
     scores = jnp.concatenate(
-        [score_ref[pl.ds(me ^ k, 1), 0:capacity] for k in range(score_ref.shape[0])], axis=1
+        [score_ref[pl.ds(me ^ step, 1), 0:capacity] for step in steps_of(score_ref.shape[0])], axis=1
     )
     high = scores.astype(jnp.bfloat16)
     rest = scores - high.astype(jnp.float32)
     middle = rest.astype(jnp.bfloat16)
     low = (rest - middle.astype(jnp.float32)).astype(jnp.bfloat16)
-    pick = pick_ref[...]
-    parts = [jnp.dot(part, pick, preferred_element_type=jnp.float32) for part in (high, middle, low)]
-    out_ref[...] = jnp.reshape((parts[0] + parts[1]) + parts[2], out_ref.shape)
+    parts = jnp.dot(
+        jnp.concatenate([high, middle, low], axis=0), pick_ref[...], preferred_element_type=jnp.float32
+    )
+    out_ref[...] = jnp.reshape((parts[0:1] + parts[1:2]) + parts[2:3], out_ref.shape)
 
 
 def collect(me, scores, pick, capacity):
@@ -161,6 +170,12 @@
     )(me, scores, pick)
 
 
+def steps_of(owners):
+    if owners == 8:
+        return (0, 6, 5, 7, 3, 1, 2, 4)
+    return tuple(range(owners))
+
+
 def swap(block, axis, step, size):
     if step == 0:
         return block
@@ -171,10 +186,10 @@
     owners = lax.axis_size("blk")
     capacity = 2 * embeddings.shape[0] // owners
     me = jnp.reshape(lax.axis_index("blk").astype(jnp.int32), (1,))
-    *blocks, pick = prepare(me, embeddings, cluster_ids, owners, capacity)
+    blocks, pick = prepare(me, embeddings, cluster_ids, owners, capacity)
     own_blocks = [None] * owners
-    for k in reversed(range(owners)):
-        own_blocks[k] = swap(blocks[k], "blk", k, owners)
+    for k, step in enumerate(steps_of(owners)):
+        own_blocks[k] = swap(blocks[k], "blk", step, owners)
     other_blocks = [swap(block, "pair", 1, 2) for block in own_blocks]
     joined, total = own_sums(own_blocks)
     scores = cross_scores(me, other_blocks, joined, total)

time: 40 us -> 38.7 us (0.968)
  starting transfers between devices: 19.2 us -> 15.8 us
  waiting for transfers between devices: 5.03 us -> 7.28 us
    ppermute x15, starting transfers between devices: 19.2 us -> 15.8 us  [swap(): return lax.ppermute(block, axis, [(i, i ^ step) for i in range(size)])]
    ppermute x15, waiting for transfers between devices: 5.03 us -> 7.28 us  [swap(): return lax.ppermute(block, axis, [(i, i ^ step) for i in range(size)])]
  transfers between devices with their start and end apart: 15 -> 15, of which waited for: 4 -> 5; matrix products, arithmetic and copies ran while one was open for 0% -> 0% of each run, Pallas kernels for 2% -> 2%
where the time goes in v3:
time: 38.7 us; the launch traced here: 38.5 us
  starting transfers between devices  15.8 us (41%)
  blocking collectives  10.5 us (27%)
  waiting for transfers between devices  7.28 us (19%)
  Pallas kernels  3.23 us (8%)
  local copies, waits for them, and re-layouts  1.67 us (4%)
    ppermute x15, starting transfers between devices, swap(): return lax.ppermute(block, axis, [(i, i ^ step) for i in range(size)])  15.8 us
    all_to_all x1, blocking collectives, direct_shards(): lax.all_to_all(scores, 'blk', split_axis=0, concat_axis=0, tiled=True)  10.5 us
    ppermute x15, waiting for transfers between devices, swap(): return lax.ppermute(block, axis, [(i, i ^ step) for i in range(size)])  7.28 us
    unnamed x4, local copies, waits for them, and re-layouts  1.67 us
    pallas_call x1, Pallas kernels, prepare(): pl.pallas_call(functools.partial(prepare_kernel, owners, capacity), out_s...  0.79 us
  transfers between devices with their start and end apart: 15, of which 5 were waited for; matrix products, arithmetic and copies ran while one was open for 0% of the time, Pallas kernels for 2%

profile of v3, /device:TPU:0, one launch (start us, length us, event | category | flops | bytes accessed | tf_op | source)
XLA Modules:
  0.0 38.5 jit_solution(3308984652522930609)
XLA Ops:
  0.0 0.7 %copy-done.1 = s32[256]{0:T(256)S(1)} copy-done((s32[256]{0:T(256)S(1)}, s32[256]{0:T(256)}, u32[]{:S(2)}) %copy-start.1) | copy-done | bytes 1048
  0.7 0.3 shard_map.28
  1.0 1.0 %copy-done = bf16[256,768]{1,0:T(8,128)(2,1)S(1)} copy-done((bf16[256,768]{1,0:T(8,128)(2,1)S(1)}, bf16[256,768]{1,0:T(8,128)(2,1)}, u32[]{:S(2)}) %copy-start) | copy-done | bytes 393240
  1.9 0.8 %shard_map.29 = (bf16[64,768]{1,0:T(8,128)(2,1)S(1)}, bf16[64,768]{1,0:T(8,128)(2,1)S(1)}, bf16[64,768]{1,0:T(8,128)(2,1)S(1)}, bf16[64,768]{1,0:T(8,128)(2,1)S(...) custom-call(bf16[256,768]{1,0:T(8,128)(2,1)S(1)} %copy-done, ...), custom_call_target="tpu_custom_call" | custom-call | tf_op jit(solution)/shard_map/pallas_call | solution.py:71
  2.7 5.1 %collective-permute-start.1 = (bf16[64,768]{1,0:T(8,128)(2,1)S(1)}, bf16[64,768]{1,0:T(8,128)(2,1)S(1)}, u32[]{:S(2)}, u32[]{:S(2)}) collective-permute-start(bf16[64,768]{1,0:T(8,128)(2,1)S(1)} %get-tuple-element.20), channel_id=1, source_target_pairs={{0,12},{2,14},{4,8},{6,10},{8,4},{10,6},{12,0},{14,2},{1,13},{3,15... | collective-permute-start | bytes 294920 | tf_op jit(solution)/shard_map/ppermute | solution.py:182
  7.9 0.6 %collective-permute-start.13 = (bf16[64,768]{1,0:T(8,128)(2,1)S(1)}, bf16[64,768]{1,0:T(8,128)(2,1)S(1)}, u32[]{:S(2)}, u32[]{:S(2)}) collective-permute-start(bf16[64,768]{1,0:T(8,128)(2,1)S(1)} %get-tuple-element.26), channel_id=1, source_target_pairs={{0,8},{2,10},{4,12},{6,14},{8,0},{10,2},{12,4},{14,6},{1,9},{3,11}... | collective-permute-start | bytes 294920 | tf_op jit(solution)/shard_map/ppermute | solution.py:182
  8.5 1.6 %collective-permute-start.9 = (bf16[64,768]{1,0:T(8,128)(2,1)S(1)}, bf16[64,768]{1,0:T(8,128)(2,1)S(1)}, u32[]{:S(2)}, u32[]{:S(2)}) collective-permute-start(bf16[64,768]{1,0:T(8,128)(2,1)S(1)} %get-tuple-element.24), channel_id=1, source_target_pairs={{0,2},{2,0},{4,6},{6,4},{8,10},{10,8},{12,14},{14,12},{1,3},{3,1},... | collective-permute-start | bytes 294920 | tf_op jit(solution)/shard_map/ppermute | solution.py:182
  10.1 2.1 %collective-permute-start.3 = (bf16[64,768]{1,0:T(8,128)(2,1)S(1)}, bf16[64,768]{1,0:T(8,128)(2,1)S(1)}, u32[]{:S(2)}, u32[]{:S(2)}) collective-permute-start(bf16[64,768]{1,0:T(8,128)(2,1)S(1)} %get-tuple-element.21), channel_id=1, source_target_pairs={{0,10},{2,8},{4,14},{6,12},{8,2},{10,0},{12,6},{14,4},{1,11},{3,9}... | collective-permute-start | bytes 294920 | tf_op jit(solution)/shard_map/ppermute | solution.py:182
  12.3 4.0 %collective-permute-start.5 = (bf16[64,768]{1,0:T(8,128)(2,1)S(1)}, bf16[64,768]{1,0:T(8,128)(2,1)S(1)}, u32[]{:S(2)}, u32[]{:S(2)}) collective-permute-start(bf16[64,768]{1,0:T(8,128)(2,1)S(1)} %get-tuple-element.22), channel_id=1, source_target_pairs={{0,14},{2,12},{4,10},{6,8},{8,6},{10,4},{12,2},{14,0},{1,15},{3,13... | collective-permute-start | bytes 294920 | tf_op jit(solution)/shard_map/ppermute | solution.py:182
  16.3 0.3 collective-permute-start.7
  16.6 4.5 %collective-permute-done.13.refs_7_ = bf16[64,768]{1,0:T(8,128)(2,1)S(1)} collective-permute-done((bf16[64,768]{1,0:T(8,128)(2,1)S(1)}, bf16[64,768]{1,0:T(8,128)(2,1)S(1)}, u32[]{:S(2)}, u32[]{:S(2)}) %collective-permute-start.13) | collective-permute-done | bytes 98336 | tf_op jit(solution)/shard_map/ppermute | solution.py:182
  21.1 0.5 %collective-permute-start.10 = (bf16[64,768]{1,0:T(8,128)(2,1)S(1)}, bf16[64,768]{1,0:T(8,128)(2,1)S(1)}, u32[]{:S(2)}, u32[]{:S(2)}) collective-permute-start(bf16[64,768]{1,0:T(8,128)(2,1)S(1)} %collective-permute-done.9.refs_5_), channel_id=1, source_target_pairs={{0,1},{1,0},{2,3},{3,2},{4,5},{5,4},{6,7},{7,6},{8,9},{9,8},{10,11... | collective-permute-start | bytes 294920 | tf_op jit(solution)/shard_map/ppermute | solution.py:182
  21.6 2.4 %collective-permute-done.3.refs_2_ = bf16[64,768]{1,0:T(8,128)(2,1)S(1)} collective-permute-done((bf16[64,768]{1,0:T(8,128)(2,1)S(1)}, bf16[64,768]{1,0:T(8,128)(2,1)S(1)}, u32[]{:S(2)}, u32[]{:S(2)}) %collective-permute-start.3) | collective-permute-done | bytes 98336 | tf_op jit(solution)/shard_map/ppermute | solution.py:182
  23.9 0.5 %collective-permute-start.14 = (bf16[64,768]{1,0:T(8,128)(2,1)S(1)}, bf16[64,768]{1,0:T(8,128)(2,1)S(1)}, u32[]{:S(2)}, u32[]{:S(2)}) collective-permute-start(bf16[64,768]{1,0:T(8,128)(2,1)S(1)} %collective-permute-done.13.refs_7_), channel_id=1, source_target_pairs={{0,1},{1,0},{2,3},{3,2},{4,5},{5,4},{6,7},{7,6},{8,9},{9,8},{10,11... | collective-permute-start | bytes 294920 | tf_op jit(solution)/shard_map/ppermute | solution.py:182
  24.4 0.2 collective-permute-done.7.refs_4_
  24.6 0.5 %collective-permute-start.4 = (bf16[64,768]{1,0:T(8,128)(2,1)S(1)}, bf16[64,768]{1,0:T(8,128)(2,1)S(1)}, u32[]{:S(2)}, u32[]{:S(2)}) collective-permute-start(bf16[64,768]{1,0:T(8,128)(2,1)S(1)} %collective-permute-done.3.refs_2_), channel_id=1, source_target_pairs={{0,1},{1,0},{2,3},{3,2},{4,5},{5,4},{6,7},{7,6},{8,9},{9,8},{10,11... | collective-permute-start | bytes 294920 | tf_op jit(solution)/shard_map/ppermute | solution.py:182
  25.1 0.1 collective-permute-start.6
  25.2 0.4 %collective-permute-start.8 = (bf16[64,768]{1,0:T(8,128)(2,1)S(1)}, bf16[64,768]{1,0:T(8,128)(2,1)S(1)}, u32[]{:S(2)}, u32[]{:S(2)}) collective-permute-start(bf16[64,768]{1,0:T(8,128)(2,1)S(1)} %collective-permute-done.7.refs_4_), channel_id=1, source_target_pairs={{0,1},{1,0},{2,3},{3,2},{4,5},{5,4},{6,7},{7,6},{8,9},{9,8},{10,11... | collective-permute-start | bytes 294920 | tf_op jit(solution)/shard_map/ppermute | solution.py:182
  25.6 0.7 %shard_map.30 = (bf16[512,768]{1,0:T(8,128)(2,1)S(1)}, f32[1,512]{1,0:T(1,128)S(1)}) custom-call(bf16[64,768]{1,0:T(8,128)(2,1)S(1)} %get-tuple-element.19.refs_0_, bf16[64,768]{1,0:T(8,128)(2,1)S(1)} %collective-permute-done.1.refs_1_, bf16[64,768]{1,0:T(8,128)(2,1)S(1)} %collective-permute-done.3.refs_2_, ...), custom_call_target="tpu_custom_call" | custom-call | flops 402653184 | bytes 1572864 | tf_op jit(solution)/shard_map/pallas_call | solution.py:108
  26.4 0.1 collective-permute-done.6.refs_3_
  26.4 0.2 collective-permute-done.8.refs_4_
  26.6 0.7 %shard_map.31 = f32[8,128]{1,0:T(8,128)S(1)} custom-call(s32[1]{0:T(128)} %bitcast.me_ref, bf16[64,768]{1,0:T(8,128)(2,1)S(1)} %collective-permute-done.refs_0_, bf16[64,768]{1,0:T(8,128)(2,1)S(1)} %collective-permute-done.2.refs_1_, bf16[64,768]{1,0:T(8,128)(2,1)S(1)} %collective-permute-done.4.refs_2_, bf16[64,768]{1,0:T(8,128)(2,1)S(1)} %collective-permute-done.6.refs_3_, ...), custom_call_target="tpu_custom_call" | custom-call | tf_op jit(solution)/shard_map/pallas_call | solution.py:138
  27.3 10.5 %all_to_all.11 = f32[8,1,128]{2,1,0:T(1,128)S(1)} all-to-all(f32[8,1,128]{2,1,0:T(1,128)S(1)} %bitcast.5), channel_id=1, replica_groups=mesh['groups'=2,'blk'=8,'pair'=2] {'blk'}, dimensions={0} | all-to-all | bytes 8192 | tf_op jit(solution)/shard_map/all_to_all | solution.py:196
  37.8 0.8 %shard_map.32 = f32[256]{0:T(256)} custom-call(s32[1]{0:T(128)} %bitcast.me_ref, f32[8,128]{1,0:T(8,128)S(1)} %bitcast.6, bf16[512,256]{1,0:T(8,128)(2,1)S(1)} %get-tuple-element.17.pick_ref), custom_call_target="tpu_custom_call" | custom-call | tf_op jit(solution)/shard_map/pallas_call | solution.py:164
  (16 shorter events, 0.1 us)
Async XLA Ops:
  0.0 0.7 %copy-start.1 = (s32[256]{0:T(256)S(1)}, s32[256]{0:T(256)}, u32[]{:S(2)}) copy-start(s32[256]{0:T(256)} %ids_ref.1) | copy-start | bytes 3076
  0.9 1.0 %copy-start = (bf16[256,768]{1,0:T(8,128)(2,1)S(1)}, bf16[256,768]{1,0:T(8,128)(2,1)}, u32[]{:S(2)}) copy-start(bf16[256,768]{1,0:T(8,128)(2,1)} %rows_ref.1) | copy-start | bytes 1179652
  2.7 9.5 %collective-permute-start.1 = (bf16[64,768]{1,0:T(8,128)(2,1)S(1)}, bf16[64,768]{1,0:T(8,128)(2,1)S(1)}, u32[]{:S(2)}, u32[]{:S(2)}) collective-permute-start(bf16[64,768]{1,0:T(8,128)(2,1)S(1)} %get-tuple-element.20), channel_id=1, source_target_pairs={{0,12},{2,14},{4,8},{6,10},{8,4},{10,6},{12,0},{14,2},{1,13},{3,15... | collective-permute-start | bytes 294920 | tf_op jit(solution)/shard_map/ppermute | solution.py:182
  7.9 8.4 %collective-permute-start.11 = (bf16[64,768]{1,0:T(8,128)(2,1)S(1)}, bf16[64,768]{1,0:T(8,128)(2,1)S(1)}, u32[]{:S(2)}, u32[]{:S(2)}) collective-permute-start(bf16[64,768]{1,0:T(8,128)(2,1)S(1)} %get-tuple-element.25), channel_id=1, source_target_pairs={{0,4},{2,6},{4,0},{6,2},{8,12},{10,14},{12,8},{14,10},{1,5},{3,7},... | collective-permute-start | bytes 294920 | tf_op jit(solution)/shard_map/ppermute | solution.py:182
  7.9 13.2 %collective-permute-start.13 = (bf16[64,768]{1,0:T(8,128)(2,1)S(1)}, bf16[64,768]{1,0:T(8,128)(2,1)S(1)}, u32[]{:S(2)}, u32[]{:S(2)}) collective-permute-start(bf16[64,768]{1,0:T(8,128)(2,1)S(1)} %get-tuple-element.26), channel_id=1, source_target_pairs={{0,8},{2,10},{4,12},{6,14},{8,0},{10,2},{12,4},{14,6},{1,9},{3,11}... | collective-permute-start | bytes 294920 | tf_op jit(solution)/shard_map/ppermute | solution.py:182
  8.5 12.6 %collective-permute-start.9 = (bf16[64,768]{1,0:T(8,128)(2,1)S(1)}, bf16[64,768]{1,0:T(8,128)(2,1)S(1)}, u32[]{:S(2)}, u32[]{:S(2)}) collective-permute-start(bf16[64,768]{1,0:T(8,128)(2,1)S(1)} %get-tuple-element.24), channel_id=1, source_target_pairs={{0,2},{2,0},{4,6},{6,4},{8,10},{10,8},{12,14},{14,12},{1,3},{3,1},... | collective-permute-start | bytes 294920 | tf_op jit(solution)/shard_map/ppermute | solution.py:182
  10.1 13.8 %collective-permute-start.3 = (bf16[64,768]{1,0:T(8,128)(2,1)S(1)}, bf16[64,768]{1,0:T(8,128)(2,1)S(1)}, u32[]{:S(2)}, u32[]{:S(2)}) collective-permute-start(bf16[64,768]{1,0:T(8,128)(2,1)S(1)} %get-tuple-element.21), channel_id=1, source_target_pairs={{0,10},{2,8},{4,14},{6,12},{8,2},{10,0},{12,6},{14,4},{1,11},{3,9}... | collective-permute-start | bytes 294920 | tf_op jit(solution)/shard_map/ppermute | solution.py:182
  12.3 11.7 %collective-permute-start.5 = (bf16[64,768]{1,0:T(8,128)(2,1)S(1)}, bf16[64,768]{1,0:T(8,128)(2,1)S(1)}, u32[]{:S(2)}, u32[]{:S(2)}) collective-permute-start(bf16[64,768]{1,0:T(8,128)(2,1)S(1)} %get-tuple-element.22), channel_id=1, source_target_pairs={{0,14},{2,12},{4,10},{6,8},{8,6},{10,4},{12,2},{14,0},{1,15},{3,13... | collective-permute-start | bytes 294920 | tf_op jit(solution)/shard_map/ppermute | solution.py:182
  16.3 8.3 %collective-permute-start.7 = (bf16[64,768]{1,0:T(8,128)(2,1)S(1)}, bf16[64,768]{1,0:T(8,128)(2,1)S(1)}, u32[]{:S(2)}, u32[]{:S(2)}) collective-permute-start(bf16[64,768]{1,0:T(8,128)(2,1)S(1)} %get-tuple-element.23), channel_id=1, source_target_pairs={{0,6},{2,4},{4,2},{6,0},{8,14},{10,12},{12,10},{14,8},{1,7},{3,5},... | collective-permute-start | bytes 294920 | tf_op jit(solution)/shard_map/ppermute | solution.py:182
  21.1 3.5 %collective-permute-start = (bf16[64,768]{1,0:T(8,128)(2,1)S(1)}, bf16[64,768]{1,0:T(8,128)(2,1)S(1)}, u32[]{:S(2)}, u32[]{:S(2)}) collective-permute-start(bf16[64,768]{1,0:T(8,128)(2,1)S(1)} %get-tuple-element.19.refs_0_), channel_id=1, source_target_pairs={{0,1},{1,0},{2,3},{3,2},{4,5},{5,4},{6,7},{7,6},{8,9},{9,8},{10,11... | collective-permute-start | bytes 294920 | tf_op jit(solution)/shard_map/ppermute | solution.py:182
  21.1 4.1 %collective-permute-start.10 = (bf16[64,768]{1,0:T(8,128)(2,1)S(1)}, bf16[64,768]{1,0:T(8,128)(2,1)S(1)}, u32[]{:S(2)}, u32[]{:S(2)}) collective-permute-start(bf16[64,768]{1,0:T(8,128)(2,1)S(1)} %collective-permute-done.9.refs_5_), channel_id=1, source_target_pairs={{0,1},{1,0},{2,3},{3,2},{4,5},{5,4},{6,7},{7,6},{8,9},{9,8},{10,11... | collective-permute-start | bytes 294920 | tf_op jit(solution)/shard_map/ppermute | solution.py:182
  23.9 1.3 %collective-permute-start.12 = (bf16[64,768]{1,0:T(8,128)(2,1)S(1)}, bf16[64,768]{1,0:T(8,128)(2,1)S(1)}, u32[]{:S(2)}, u32[]{:S(2)}) collective-permute-start(bf16[64,768]{1,0:T(8,128)(2,1)S(1)} %collective-permute-done.11.refs_6_), channel_id=1, source_target_pairs={{0,1},{1,0},{2,3},{3,2},{4,5},{5,4},{6,7},{7,6},{8,9},{9,8},{10,11... | collective-permute-start | bytes 294920 | tf_op jit(solution)/shard_map/ppermute | solution.py:182
  23.9 2.4 %collective-permute-start.14 = (bf16[64,768]{1,0:T(8,128)(2,1)S(1)}, bf16[64,768]{1,0:T(8,128)(2,1)S(1)}, u32[]{:S(2)}, u32[]{:S(2)}) collective-permute-start(bf16[64,768]{1,0:T(8,128)(2,1)S(1)} %collective-permute-done.13.refs_7_), channel_id=1, source_target_pairs={{0,1},{1,0},{2,3},{3,2},{4,5},{5,4},{6,7},{7,6},{8,9},{9,8},{10,11... | collective-permute-start | bytes 294920 | tf_op jit(solution)/shard_map/ppermute | solution.py:182
  24.6 1.7 %collective-permute-start.2 = (bf16[64,768]{1,0:T(8,128)(2,1)S(1)}, bf16[64,768]{1,0:T(8,128)(2,1)S(1)}, u32[]{:S(2)}, u32[]{:S(2)}) collective-permute-start(bf16[64,768]{1,0:T(8,128)(2,1)S(1)} %collective-permute-done.1.refs_1_), channel_id=1, source_target_pairs={{0,1},{1,0},{2,3},{3,2},{4,5},{5,4},{6,7},{7,6},{8,9},{9,8},{10,11... | collective-permute-start | bytes 294920 | tf_op jit(solution)/shard_map/ppermute | solution.py:182
  24.6 1.7 %collective-permute-start.4 = (bf16[64,768]{1,0:T(8,128)(2,1)S(1)}, bf16[64,768]{1,0:T(8,128)(2,1)S(1)}, u32[]{:S(2)}, u32[]{:S(2)}) collective-permute-start(bf16[64,768]{1,0:T(8,128)(2,1)S(1)} %collective-permute-done.3.refs_2_), channel_id=1, source_target_pairs={{0,1},{1,0},{2,3},{3,2},{4,5},{5,4},{6,7},{7,6},{8,9},{9,8},{10,11... | collective-permute-start | bytes 294920 | tf_op jit(solution)/shard_map/ppermute | solution.py:182
  25.1 1.3 %collective-permute-start.6 = (bf16[64,768]{1,0:T(8,128)(2,1)S(1)}, bf16[64,768]{1,0:T(8,128)(2,1)S(1)}, u32[]{:S(2)}, u32[]{:S(2)}) collective-permute-start(bf16[64,768]{1,0:T(8,128)(2,1)S(1)} %collective-permute-done.5.refs_3_), channel_id=1, source_target_pairs={{0,1},{1,0},{2,3},{3,2},{4,5},{5,4},{6,7},{7,6},{8,9},{9,8},{10,11... | collective-permute-start | bytes 294920 | tf_op jit(solution)/shard_map/ppermute | solution.py:182
  25.2 1.4 %collective-permute-start.8 = (bf16[64,768]{1,0:T(8,128)(2,1)S(1)}, bf16[64,768]{1,0:T(8,128)(2,1)S(1)}, u32[]{:S(2)}, u32[]{:S(2)}) collective-permute-start(bf16[64,768]{1,0:T(8,128)(2,1)S(1)} %collective-permute-done.7.refs_4_), channel_id=1, source_target_pairs={{0,1},{1,0},{2,3},{3,2},{4,5},{5,4},{6,7},{7,6},{8,9},{9,8},{10,11... | collective-permute-start | bytes 294920 | tf_op jit(solution)/shard_map/ppermute | solution.py:182

commit v4 on v3

--- a/solution.py
+++ b/solution.py
@@ -23,15 +23,22 @@
     return pltpu.CompilerParams(vmem_limit_bytes=mib * 1024 * 1024)
 
 
-def pick_kernel(owners, capacity, me_ref, ids_ref, pick_ref, empty_ref):
+def prepare_kernel(owners, capacity, me_ref, rows_hbm, ids_hbm, *refs):
+    block_refs = refs[:owners]
+    pick_ref, rows_ref, ids_ref, sems = refs[owners:]
+    ids_copy = pltpu.make_async_copy(ids_hbm, ids_ref, sems.at[0])
+    rows_copy = pltpu.make_async_copy(rows_hbm, rows_ref, sems.at[1])
+    ids_copy.start()
+    rows_copy.start()
     row_count = ids_ref.shape[0]
-    step = jnp.reshape(ids_ref[...], (1, row_count)) ^ me_ref[0]
-    relative = sum(jnp.where(step == value, k, 0) for k, value in enumerate(steps_of(owners)))
-    labels = lax.broadcasted_iota(jnp.int32, (owners, row_count), 0)
-    inside = (labels == relative).astype(jnp.float32)
     above = lax.broadcasted_iota(jnp.int32, (row_count, row_count), 0)
     right = lax.broadcasted_iota(jnp.int32, (row_count, row_count), 1)
     earlier = jnp.where(above < right, 1.0, 0.0).astype(jnp.bfloat16)
+    labels = lax.broadcasted_iota(jnp.int32, (owners, row_count), 0)
+    ids_copy.wait()
+    step = jnp.reshape(ids_ref[...], (1, row_count)) ^ me_ref[0]
+    relative = sum(jnp.where(step == value, k, 0) for k, value in enumerate(steps_of(owners)))
+    inside = (labels == relative).astype(jnp.float32)
     before = jnp.dot(inside.astype(jnp.bfloat16), earlier, preferred_element_type=jnp.float32)
     rank = jnp.sum(before * inside, axis=0, keepdims=True).astype(jnp.int32)
     slot = relative * capacity + rank
@@ -39,12 +46,10 @@
     pick_ref[...] = jnp.where(
         lax.broadcasted_iota(jnp.int32, (slots, row_count), 0) == slot, 1.0, 0.0
     ).astype(jnp.bfloat16)
-    counts = jnp.broadcast_to(jnp.sum(inside, axis=1, keepdims=True), empty_ref.shape)
-    first = lax.broadcasted_iota(jnp.int32, empty_ref.shape, 1) == 0
-    empty_ref[...] = jnp.where(first & (counts == 0.0), EMPTY_MARK, 0.0)
-
-
-def prepare_kernel(owners, capacity, rows_ref, pick_ref, empty_ref, *block_refs):
+    counts = jnp.broadcast_to(jnp.sum(inside, axis=1, keepdims=True), (owners, 128))
+    first = lax.broadcasted_iota(jnp.int32, (owners, 128), 1) == 0
+    marks = jnp.where(first & (counts == 0.0), EMPTY_MARK, 0.0)
+    rows_copy.wait()
     values = rows_ref[...].astype(jnp.float32)
     scale = lax.rsqrt(jnp.sum(values * values, axis=1, keepdims=True) + EPSILON)
     units = (values * scale).astype(jnp.bfloat16)
@@ -53,28 +58,28 @@
             pick_ref[k * capacity:(k + 1) * capacity, :], units, preferred_element_type=jnp.float32
         )
         block_ref[...] = block.astype(jnp.bfloat16)
-        block_ref[:, 0:128] = (block[:, 0:128] + empty_ref[k:k + 1, :]).astype(jnp.bfloat16)
+        block_ref[:, 0:128] = (block[:, 0:128] + marks[k:k + 1, :]).astype(jnp.bfloat16)
 
 
 def prepare(me, rows, ids, owners, capacity):
     row_count, width = rows.shape
-    pick, empty = pl.pallas_call(
-        functools.partial(pick_kernel, owners, capacity),
-        out_shape=[
-            jax.ShapeDtypeStruct((owners * capacity, row_count), jnp.bfloat16),
-            jax.ShapeDtypeStruct((owners, 128), jnp.float32),
+    *blocks, pick = pl.pallas_call(
+        functools.partial(prepare_kernel, owners, capacity),
+        out_shape=[jax.ShapeDtypeStruct((capacity, width), jnp.bfloat16)] * owners
+        + [jax.ShapeDtypeStruct((owners * capacity, row_count), jnp.bfloat16)],
+        in_specs=[pl.BlockSpec(memory_space=pltpu.SMEM)] + [pl.BlockSpec(memory_space=pltpu.HBM)] * 2,
+        out_specs=vmem(owners + 1),
+        scratch_shapes=[
+            pltpu.VMEM(rows.shape, rows.dtype),
+            pltpu.VMEM(ids.shape, ids.dtype),
+            pltpu.SemaphoreType.DMA((2,)),
         ],
-        in_specs=[pl.BlockSpec(memory_space=pltpu.SMEM)] + vmem(1),
-        out_specs=vmem(2),
-        compiler_params=params(),
-    )(me, ids)
-    blocks = pl.pallas_call(
-        functools.partial(prepare_kernel, owners, capacity),
-        out_shape=[jax.ShapeDtypeStruct((capacity, width), jnp.bfloat16)] * owners,
-        in_specs=vmem(3),
-        out_specs=vmem(owners),
-        compiler_params=params(),
-    )(rows, pick, empty)
+        compiler_params=params(),
+    )(
+        me,
+        pltpu.with_memory_space_constraint(rows, pltpu.HBM),
+        pltpu.with_memory_space_constraint(ids, pltpu.HBM),
+    )
     return blocks, pick
 
 

time: 38.7 us -> 37.8 us (0.977)
  local copies, waits for them, and re-layouts: 1.67 us -> 0 us
  Pallas kernels: 3.23 us -> 4.03 us
    unnamed x4 -> x0, local copies, waits for them, and re-layouts: 1.67 us -> none
    pallas_call x1, Pallas kernels: 0.79 us -> 1.85 us  [prepare(): pl.pallas_call(functools.partial(prepare_kernel, owners, capacity), out_s...]
where the time goes in v4:
time: 37.8 us; the launch traced here: 37.7 us
  starting transfers between devices  15.8 us (42%)
  blocking collectives  10.5 us (28%)
  waiting for transfers between devices  7.29 us (19%)
  Pallas kernels  4.03 us (11%)
    ppermute x15, starting transfers between devices, swap(): return lax.ppermute(block, axis, [(i, i ^ step) for i in range(size)])  15.8 us
    all_to_all x1, blocking collectives, direct_shards(): lax.all_to_all(scores, 'blk', split_axis=0, concat_axis=0, tiled=True)  10.5 us
    ppermute x15, waiting for transfers between devices, swap(): return lax.ppermute(block, axis, [(i, i ^ step) for i in range(size)])  7.29 us
    pallas_call x1, Pallas kernels, prepare(): pl.pallas_call(functools.partial(prepare_kernel, owners, capacity), out_s...  1.85 us
    pallas_call x1, Pallas kernels, collect(): pl.pallas_call(functools.partial(collect_kernel, capacity), out_shape=jax...  0.77 us
  transfers between devices with their start and end apart: 15, of which 5 were waited for; matrix products, arithmetic and copies ran while one was open for 0% of the time, Pallas kernels for 2%

profile of v4, /device:TPU:0, one launch (start us, length us, event | category | flops | bytes accessed | tf_op | source)
XLA Modules:
  0.0 37.7 jit_solution(10426397288315791181)
XLA Ops:
  0.0 1.8 %shard_map.28 = (bf16[64,768]{1,0:T(8,128)(2,1)S(1)}, bf16[64,768]{1,0:T(8,128)(2,1)S(1)}, bf16[64,768]{1,0:T(8,128)(2,1)S(1)}, bf16[64,768]{1,0:T(8,128)(2,1)S(...) custom-call(s32[1]{0:T(128)} %bitcast.me_ref, ...), custom_call_target="tpu_custom_call" | custom-call | tf_op jit(solution)/shard_map/pallas_call | solution.py:66
  1.9 5.1 %collective-permute-start.1 = (bf16[64,768]{1,0:T(8,128)(2,1)S(1)}, bf16[64,768]{1,0:T(8,128)(2,1)S(1)}, u32[]{:S(2)}, u32[]{:S(2)}) collective-permute-start(bf16[64,768]{1,0:T(8,128)(2,1)S(1)} %get-tuple-element.17), channel_id=1, source_target_pairs={{0,12},{2,14},{4,8},{6,10},{8,4},{10,6},{12,0},{14,2},{1,13},{3,15... | collective-permute-start | bytes 294920 | tf_op jit(solution)/shard_map/ppermute | solution.py:187
  7.0 0.0 collective-permute-start.11
  7.0 0.6 %collective-permute-start.13 = (bf16[64,768]{1,0:T(8,128)(2,1)S(1)}, bf16[64,768]{1,0:T(8,128)(2,1)S(1)}, u32[]{:S(2)}, u32[]{:S(2)}) collective-permute-start(bf16[64,768]{1,0:T(8,128)(2,1)S(1)} %get-tuple-element.23), channel_id=1, source_target_pairs={{0,8},{2,10},{4,12},{6,14},{8,0},{10,2},{12,4},{14,6},{1,9},{3,11}... | collective-permute-start | bytes 294920 | tf_op jit(solution)/shard_map/ppermute | solution.py:187
  7.6 1.6 %collective-permute-start.9 = (bf16[64,768]{1,0:T(8,128)(2,1)S(1)}, bf16[64,768]{1,0:T(8,128)(2,1)S(1)}, u32[]{:S(2)}, u32[]{:S(2)}) collective-permute-start(bf16[64,768]{1,0:T(8,128)(2,1)S(1)} %get-tuple-element.21), channel_id=1, source_target_pairs={{0,2},{2,0},{4,6},{6,4},{8,10},{10,8},{12,14},{14,12},{1,3},{3,1},... | collective-permute-start | bytes 294920 | tf_op jit(solution)/shard_map/ppermute | solution.py:187
  9.3 2.1 %collective-permute-start.3 = (bf16[64,768]{1,0:T(8,128)(2,1)S(1)}, bf16[64,768]{1,0:T(8,128)(2,1)S(1)}, u32[]{:S(2)}, u32[]{:S(2)}) collective-permute-start(bf16[64,768]{1,0:T(8,128)(2,1)S(1)} %get-tuple-element.18), channel_id=1, source_target_pairs={{0,10},{2,8},{4,14},{6,12},{8,2},{10,0},{12,6},{14,4},{1,11},{3,9}... | collective-permute-start | bytes 294920 | tf_op jit(solution)/shard_map/ppermute | solution.py:187
  11.4 0.0 collective-permute-done.1.refs_1_
  11.4 4.0 %collective-permute-start.5 = (bf16[64,768]{1,0:T(8,128)(2,1)S(1)}, bf16[64,768]{1,0:T(8,128)(2,1)S(1)}, u32[]{:S(2)}, u32[]{:S(2)}) collective-permute-start(bf16[64,768]{1,0:T(8,128)(2,1)S(1)} %get-tuple-element.19), channel_id=1, source_target_pairs={{0,14},{2,12},{4,10},{6,8},{8,6},{10,4},{12,2},{14,0},{1,15},{3,13... | collective-permute-start | bytes 294920 | tf_op jit(solution)/shard_map/ppermute | solution.py:187
  15.4 0.3 collective-permute-start.7
  15.7 4.5 %collective-permute-done.13.refs_7_ = bf16[64,768]{1,0:T(8,128)(2,1)S(1)} collective-permute-done((bf16[64,768]{1,0:T(8,128)(2,1)S(1)}, bf16[64,768]{1,0:T(8,128)(2,1)S(1)}, u32[]{:S(2)}, u32[]{:S(2)}) %collective-permute-start.13) | collective-permute-done | bytes 98336 | tf_op jit(solution)/shard_map/ppermute | solution.py:187
  20.2 0.5 %collective-permute-start.10 = (bf16[64,768]{1,0:T(8,128)(2,1)S(1)}, bf16[64,768]{1,0:T(8,128)(2,1)S(1)}, u32[]{:S(2)}, u32[]{:S(2)}) collective-permute-start(bf16[64,768]{1,0:T(8,128)(2,1)S(1)} %collective-permute-done.9.refs_5_), channel_id=1, source_target_pairs={{0,1},{1,0},{2,3},{3,2},{4,5},{5,4},{6,7},{7,6},{8,9},{9,8},{10,11... | collective-permute-start | bytes 294920 | tf_op jit(solution)/shard_map/ppermute | solution.py:187
  20.7 2.4 %collective-permute-done.3.refs_2_ = bf16[64,768]{1,0:T(8,128)(2,1)S(1)} collective-permute-done((bf16[64,768]{1,0:T(8,128)(2,1)S(1)}, bf16[64,768]{1,0:T(8,128)(2,1)S(1)}, u32[]{:S(2)}, u32[]{:S(2)}) %collective-permute-start.3) | collective-permute-done | bytes 98336 | tf_op jit(solution)/shard_map/ppermute | solution.py:187
  23.1 0.5 %collective-permute-start.14 = (bf16[64,768]{1,0:T(8,128)(2,1)S(1)}, bf16[64,768]{1,0:T(8,128)(2,1)S(1)}, u32[]{:S(2)}, u32[]{:S(2)}) collective-permute-start(bf16[64,768]{1,0:T(8,128)(2,1)S(1)} %collective-permute-done.13.refs_7_), channel_id=1, source_target_pairs={{0,1},{1,0},{2,3},{3,2},{4,5},{5,4},{6,7},{7,6},{8,9},{9,8},{10,11... | collective-permute-start | bytes 294920 | tf_op jit(solution)/shard_map/ppermute | solution.py:187
  23.6 0.2 collective-permute-done.7.refs_4_
  23.7 0.5 %collective-permute-start.4 = (bf16[64,768]{1,0:T(8,128)(2,1)S(1)}, bf16[64,768]{1,0:T(8,128)(2,1)S(1)}, u32[]{:S(2)}, u32[]{:S(2)}) collective-permute-start(bf16[64,768]{1,0:T(8,128)(2,1)S(1)} %collective-permute-done.3.refs_2_), channel_id=1, source_target_pairs={{0,1},{1,0},{2,3},{3,2},{4,5},{5,4},{6,7},{7,6},{8,9},{9,8},{10,11... | collective-permute-start | bytes 294920 | tf_op jit(solution)/shard_map/ppermute | solution.py:187
  24.2 0.1 collective-permute-start.6
  24.3 0.0 collective-permute-done.12.refs_6_
  24.4 0.4 %collective-permute-start.8 = (bf16[64,768]{1,0:T(8,128)(2,1)S(1)}, bf16[64,768]{1,0:T(8,128)(2,1)S(1)}, u32[]{:S(2)}, u32[]{:S(2)}) collective-permute-start(bf16[64,768]{1,0:T(8,128)(2,1)S(1)} %collective-permute-done.7.refs_4_), channel_id=1, source_target_pairs={{0,1},{1,0},{2,3},{3,2},{4,5},{5,4},{6,7},{7,6},{8,9},{9,8},{10,11... | collective-permute-start | bytes 294920 | tf_op jit(solution)/shard_map/ppermute | solution.py:187
  24.8 0.7 %shard_map.29 = (bf16[512,768]{1,0:T(8,128)(2,1)S(1)}, f32[1,512]{1,0:T(1,128)S(1)}) custom-call(bf16[64,768]{1,0:T(8,128)(2,1)S(1)} %get-tuple-element.16.refs_0_, bf16[64,768]{1,0:T(8,128)(2,1)S(1)} %collective-permute-done.1.refs_1_, bf16[64,768]{1,0:T(8,128)(2,1)S(1)} %collective-permute-done.3.refs_2_, ...), custom_call_target="tpu_custom_call" | custom-call | flops 402653184 | bytes 1572864 | tf_op jit(solution)/shard_map/pallas_call | solution.py:113
  25.5 0.1 collective-permute-done.6.refs_3_
  25.5 0.2 collective-permute-done.8.refs_4_
  25.7 0.7 %shard_map.30 = f32[8,128]{1,0:T(8,128)S(1)} custom-call(s32[1]{0:T(128)} %bitcast.me_ref, bf16[64,768]{1,0:T(8,128)(2,1)S(1)} %collective-permute-done.refs_0_, bf16[64,768]{1,0:T(8,128)(2,1)S(1)} %collective-permute-done.2.refs_1_, bf16[64,768]{1,0:T(8,128)(2,1)S(1)} %collective-permute-done.4.refs_2_, bf16[64,768]{1,0:T(8,128)(2,1)S(1)} %collective-permute-done.6.refs_3_, ...), custom_call_target="tpu_custom_call" | custom-call | tf_op jit(solution)/shard_map/pallas_call | solution.py:143
  26.4 10.5 %all_to_all.11 = f32[8,1,128]{2,1,0:T(1,128)S(1)} all-to-all(f32[8,1,128]{2,1,0:T(1,128)S(1)} %bitcast.5), channel_id=1, replica_groups=mesh['groups'=2,'blk'=8,'pair'=2] {'blk'}, dimensions={0} | all-to-all | bytes 8192 | tf_op jit(solution)/shard_map/all_to_all | solution.py:201
  36.9 0.8 %shard_map.31 = f32[256]{0:T(256)} custom-call(s32[1]{0:T(128)} %bitcast.me_ref, f32[8,128]{1,0:T(8,128)S(1)} %bitcast.6, bf16[512,256]{1,0:T(8,128)(2,1)S(1)} %get-tuple-element.26.pick_ref), custom_call_target="tpu_custom_call" | custom-call | tf_op jit(solution)/shard_map/pallas_call | solution.py:169
  (11 shorter events, 0.0 us)
Async XLA Ops:
  1.9 9.5 %collective-permute-start.1 = (bf16[64,768]{1,0:T(8,128)(2,1)S(1)}, bf16[64,768]{1,0:T(8,128)(2,1)S(1)}, u32[]{:S(2)}, u32[]{:S(2)}) collective-permute-start(bf16[64,768]{1,0:T(8,128)(2,1)S(1)} %get-tuple-element.17), channel_id=1, source_target_pairs={{0,12},{2,14},{4,8},{6,10},{8,4},{10,6},{12,0},{14,2},{1,13},{3,15... | collective-permute-start | bytes 294920 | tf_op jit(solution)/shard_map/ppermute | solution.py:187
  7.0 8.4 %collective-permute-start.11 = (bf16[64,768]{1,0:T(8,128)(2,1)S(1)}, bf16[64,768]{1,0:T(8,128)(2,1)S(1)}, u32[]{:S(2)}, u32[]{:S(2)}) collective-permute-start(bf16[64,768]{1,0:T(8,128)(2,1)S(1)} %get-tuple-element.22), channel_id=1, source_target_pairs={{0,4},{2,6},{4,0},{6,2},{8,12},{10,14},{12,8},{14,10},{1,5},{3,7},... | collective-permute-start | bytes 294920 | tf_op jit(solution)/shard_map/ppermute | solution.py:187
  7.0 13.2 %collective-permute-start.13 = (bf16[64,768]{1,0:T(8,128)(2,1)S(1)}, bf16[64,768]{1,0:T(8,128)(2,1)S(1)}, u32[]{:S(2)}, u32[]{:S(2)}) collective-permute-start(bf16[64,768]{1,0:T(8,128)(2,1)S(1)} %get-tuple-element.23), channel_id=1, source_target_pairs={{0,8},{2,10},{4,12},{6,14},{8,0},{10,2},{12,4},{14,6},{1,9},{3,11}... | collective-permute-start | bytes 294920 | tf_op jit(solution)/shard_map/ppermute | solution.py:187
  7.6 12.6 %collective-permute-start.9 = (bf16[64,768]{1,0:T(8,128)(2,1)S(1)}, bf16[64,768]{1,0:T(8,128)(2,1)S(1)}, u32[]{:S(2)}, u32[]{:S(2)}) collective-permute-start(bf16[64,768]{1,0:T(8,128)(2,1)S(1)} %get-tuple-element.21), channel_id=1, source_target_pairs={{0,2},{2,0},{4,6},{6,4},{8,10},{10,8},{12,14},{14,12},{1,3},{3,1},... | collective-permute-start | bytes 294920 | tf_op jit(solution)/shard_map/ppermute | solution.py:187
  9.3 13.8 %collective-permute-start.3 = (bf16[64,768]{1,0:T(8,128)(2,1)S(1)}, bf16[64,768]{1,0:T(8,128)(2,1)S(1)}, u32[]{:S(2)}, u32[]{:S(2)}) collective-permute-start(bf16[64,768]{1,0:T(8,128)(2,1)S(1)} %get-tuple-element.18), channel_id=1, source_target_pairs={{0,10},{2,8},{4,14},{6,12},{8,2},{10,0},{12,6},{14,4},{1,11},{3,9}... | collective-permute-start | bytes 294920 | tf_op jit(solution)/shard_map/ppermute | solution.py:187
  11.4 11.7 %collective-permute-start.5 = (bf16[64,768]{1,0:T(8,128)(2,1)S(1)}, bf16[64,768]{1,0:T(8,128)(2,1)S(1)}, u32[]{:S(2)}, u32[]{:S(2)}) collective-permute-start(bf16[64,768]{1,0:T(8,128)(2,1)S(1)} %get-tuple-element.19), channel_id=1, source_target_pairs={{0,14},{2,12},{4,10},{6,8},{8,6},{10,4},{12,2},{14,0},{1,15},{3,13... | collective-permute-start | bytes 294920 | tf_op jit(solution)/shard_map/ppermute | solution.py:187
  15.4 8.3 %collective-permute-start.7 = (bf16[64,768]{1,0:T(8,128)(2,1)S(1)}, bf16[64,768]{1,0:T(8,128)(2,1)S(1)}, u32[]{:S(2)}, u32[]{:S(2)}) collective-permute-start(bf16[64,768]{1,0:T(8,128)(2,1)S(1)} %get-tuple-element.20), channel_id=1, source_target_pairs={{0,6},{2,4},{4,2},{6,0},{8,14},{10,12},{12,10},{14,8},{1,7},{3,5},... | collective-permute-start | bytes 294920 | tf_op jit(solution)/shard_map/ppermute | solution.py:187
  20.2 3.5 %collective-permute-start = (bf16[64,768]{1,0:T(8,128)(2,1)S(1)}, bf16[64,768]{1,0:T(8,128)(2,1)S(1)}, u32[]{:S(2)}, u32[]{:S(2)}) collective-permute-start(bf16[64,768]{1,0:T(8,128)(2,1)S(1)} %get-tuple-element.16.refs_0_), channel_id=1, source_target_pairs={{0,1},{1,0},{2,3},{3,2},{4,5},{5,4},{6,7},{7,6},{8,9},{9,8},{10,11... | collective-permute-start | bytes 294920 | tf_op jit(solution)/shard_map/ppermute | solution.py:187
  20.2 4.1 %collective-permute-start.10 = (bf16[64,768]{1,0:T(8,128)(2,1)S(1)}, bf16[64,768]{1,0:T(8,128)(2,1)S(1)}, u32[]{:S(2)}, u32[]{:S(2)}) collective-permute-start(bf16[64,768]{1,0:T(8,128)(2,1)S(1)} %collective-permute-done.9.refs_5_), channel_id=1, source_target_pairs={{0,1},{1,0},{2,3},{3,2},{4,5},{5,4},{6,7},{7,6},{8,9},{9,8},{10,11... | collective-permute-start | bytes 294920 | tf_op jit(solution)/shard_map/ppermute | solution.py:187
  23.1 1.3 %collective-permute-start.12 = (bf16[64,768]{1,0:T(8,128)(2,1)S(1)}, bf16[64,768]{1,0:T(8,128)(2,1)S(1)}, u32[]{:S(2)}, u32[]{:S(2)}) collective-permute-start(bf16[64,768]{1,0:T(8,128)(2,1)S(1)} %collective-permute-done.11.refs_6_), channel_id=1, source_target_pairs={{0,1},{1,0},{2,3},{3,2},{4,5},{5,4},{6,7},{7,6},{8,9},{9,8},{10,11... | collective-permute-start | bytes 294920 | tf_op jit(solution)/shard_map/ppermute | solution.py:187
  23.1 2.4 %collective-permute-start.14 = (bf16[64,768]{1,0:T(8,128)(2,1)S(1)}, bf16[64,768]{1,0:T(8,128)(2,1)S(1)}, u32[]{:S(2)}, u32[]{:S(2)}) collective-permute-start(bf16[64,768]{1,0:T(8,128)(2,1)S(1)} %collective-permute-done.13.refs_7_), channel_id=1, source_target_pairs={{0,1},{1,0},{2,3},{3,2},{4,5},{5,4},{6,7},{7,6},{8,9},{9,8},{10,11... | collective-permute-start | bytes 294920 | tf_op jit(solution)/shard_map/ppermute | solution.py:187
  23.7 1.7 %collective-permute-start.2 = (bf16[64,768]{1,0:T(8,128)(2,1)S(1)}, bf16[64,768]{1,0:T(8,128)(2,1)S(1)}, u32[]{:S(2)}, u32[]{:S(2)}) collective-permute-start(bf16[64,768]{1,0:T(8,128)(2,1)S(1)} %collective-permute-done.1.refs_1_), channel_id=1, source_target_pairs={{0,1},{1,0},{2,3},{3,2},{4,5},{5,4},{6,7},{7,6},{8,9},{9,8},{10,11... | collective-permute-start | bytes 294920 | tf_op jit(solution)/shard_map/ppermute | solution.py:187
  23.7 1.7 %collective-permute-start.4 = (bf16[64,768]{1,0:T(8,128)(2,1)S(1)}, bf16[64,768]{1,0:T(8,128)(2,1)S(1)}, u32[]{:S(2)}, u32[]{:S(2)}) collective-permute-start(bf16[64,768]{1,0:T(8,128)(2,1)S(1)} %collective-permute-done.3.refs_2_), channel_id=1, source_target_pairs={{0,1},{1,0},{2,3},{3,2},{4,5},{5,4},{6,7},{7,6},{8,9},{9,8},{10,11... | collective-permute-start | bytes 294920 | tf_op jit(solution)/shard_map/ppermute | solution.py:187
  24.2 1.3 %collective-permute-start.6 = (bf16[64,768]{1,0:T(8,128)(2,1)S(1)}, bf16[64,768]{1,0:T(8,128)(2,1)S(1)}, u32[]{:S(2)}, u32[]{:S(2)}) collective-permute-start(bf16[64,768]{1,0:T(8,128)(2,1)S(1)} %collective-permute-done.5.refs_3_), channel_id=1, source_target_pairs={{0,1},{1,0},{2,3},{3,2},{4,5},{5,4},{6,7},{7,6},{8,9},{9,8},{10,11... | collective-permute-start | bytes 294920 | tf_op jit(solution)/shard_map/ppermute | solution.py:187
  24.4 1.3 %collective-permute-start.8 = (bf16[64,768]{1,0:T(8,128)(2,1)S(1)}, bf16[64,768]{1,0:T(8,128)(2,1)S(1)}, u32[]{:S(2)}, u32[]{:S(2)}) collective-permute-start(bf16[64,768]{1,0:T(8,128)(2,1)S(1)} %collective-permute-done.7.refs_4_), channel_id=1, source_target_pairs={{0,1},{1,0},{2,3},{3,2},{4,5},{5,4},{6,7},{7,6},{8,9},{9,8},{10,11... | collective-permute-start | bytes 294920 | tf_op jit(solution)/shard_map/ppermute | solution.py:187

commit v5 on v4

--- a/solution.py
+++ b/solution.py
@@ -177,7 +177,7 @@
 
 def steps_of(owners):
     if owners == 8:
-        return (0, 6, 5, 7, 3, 1, 2, 4)
+        return (0, 6, 5, 3, 7, 1, 2, 4)
     return tuple(range(owners))
 
 

time: 37.8 us -> 37.5 us (level)
  no operation moved by 1% of the time
where the time goes in v5:
time: 37.5 us; the launch traced here: 37.3 us
  starting transfers between devices  16 us (43%)
  blocking collectives  10.2 us (27%)
  waiting for transfers between devices  6.99 us (19%)
  Pallas kernels  4.03 us (11%)
    ppermute x15, starting transfers between devices, swap(): return lax.ppermute(block, axis, [(i, i ^ step) for i in range(size)])  16 us
    all_to_all x1, blocking collectives, direct_shards(): lax.all_to_all(scores, 'blk', split_axis=0, concat_axis=0, tiled=True)  10.2 us
    ppermute x15, waiting for transfers between devices, swap(): return lax.ppermute(block, axis, [(i, i ^ step) for i in range(size)])  6.99 us
    pallas_call x1, Pallas kernels, prepare(): pl.pallas_call(functools.partial(prepare_kernel, owners, capacity), out_s...  1.85 us
    pallas_call x1, Pallas kernels, collect(): pl.pallas_call(functools.partial(collect_kernel, capacity), out_shape=jax...  0.76 us
  transfers between devices with their start and end apart: 15, of which 5 were waited for; matrix products, arithmetic and copies ran while one was open for 0% of the time, Pallas kernels for 2%

profile of v5, /device:TPU:0, one launch (start us, length us, event | category | flops | bytes accessed | tf_op | source)
XLA Modules:
  0.0 37.3 jit_solution(15839045148344971046)
XLA Ops:
  0.0 1.8 %shard_map.28 = (bf16[64,768]{1,0:T(8,128)(2,1)S(1)}, bf16[64,768]{1,0:T(8,128)(2,1)S(1)}, bf16[64,768]{1,0:T(8,128)(2,1)S(1)}, bf16[64,768]{1,0:T(8,128)(2,1)S(...) custom-call(s32[1]{0:T(128)} %bitcast.me_ref, ...), custom_call_target="tpu_custom_call" | custom-call | tf_op jit(solution)/shard_map/pallas_call | solution.py:66
  1.9 5.1 %collective-permute-start.1 = (bf16[64,768]{1,0:T(8,128)(2,1)S(1)}, bf16[64,768]{1,0:T(8,128)(2,1)S(1)}, u32[]{:S(2)}, u32[]{:S(2)}) collective-permute-start(bf16[64,768]{1,0:T(8,128)(2,1)S(1)} %get-tuple-element.17), channel_id=1, source_target_pairs={{0,12},{2,14},{4,8},{6,10},{8,4},{10,6},{12,0},{14,2},{1,13},{3,15... | collective-permute-start | bytes 294920 | tf_op jit(solution)/shard_map/ppermute | solution.py:187
  7.0 0.6 %collective-permute-start.13 = (bf16[64,768]{1,0:T(8,128)(2,1)S(1)}, bf16[64,768]{1,0:T(8,128)(2,1)S(1)}, u32[]{:S(2)}, u32[]{:S(2)}) collective-permute-start(bf16[64,768]{1,0:T(8,128)(2,1)S(1)} %get-tuple-element.23), channel_id=1, source_target_pairs={{0,8},{2,10},{4,12},{6,14},{8,0},{10,2},{12,4},{14,6},{1,9},{3,11}... | collective-permute-start | bytes 294920 | tf_op jit(solution)/shard_map/ppermute | solution.py:187
  7.6 1.6 %collective-permute-start.9 = (bf16[64,768]{1,0:T(8,128)(2,1)S(1)}, bf16[64,768]{1,0:T(8,128)(2,1)S(1)}, u32[]{:S(2)}, u32[]{:S(2)}) collective-permute-start(bf16[64,768]{1,0:T(8,128)(2,1)S(1)} %get-tuple-element.21), channel_id=1, source_target_pairs={{0,2},{2,0},{4,6},{6,4},{8,10},{10,8},{12,14},{14,12},{1,3},{3,1},... | collective-permute-start | bytes 294920 | tf_op jit(solution)/shard_map/ppermute | solution.py:187
  9.3 2.1 %collective-permute-start.3 = (bf16[64,768]{1,0:T(8,128)(2,1)S(1)}, bf16[64,768]{1,0:T(8,128)(2,1)S(1)}, u32[]{:S(2)}, u32[]{:S(2)}) collective-permute-start(bf16[64,768]{1,0:T(8,128)(2,1)S(1)} %get-tuple-element.18), channel_id=1, source_target_pairs={{0,10},{2,8},{4,14},{6,12},{8,2},{10,0},{12,6},{14,4},{1,11},{3,9}... | collective-permute-start | bytes 294920 | tf_op jit(solution)/shard_map/ppermute | solution.py:187
  11.4 3.0 %collective-permute-start.5 = (bf16[64,768]{1,0:T(8,128)(2,1)S(1)}, bf16[64,768]{1,0:T(8,128)(2,1)S(1)}, u32[]{:S(2)}, u32[]{:S(2)}) collective-permute-start(bf16[64,768]{1,0:T(8,128)(2,1)S(1)} %get-tuple-element.19), channel_id=1, source_target_pairs={{0,6},{2,4},{4,2},{6,0},{8,14},{10,12},{12,10},{14,8},{1,7},{3,5},... | collective-permute-start | bytes 294920 | tf_op jit(solution)/shard_map/ppermute | solution.py:187
  14.3 0.0 collective-permute-done.11.refs_6_
  14.3 1.7 %collective-permute-start.7 = (bf16[64,768]{1,0:T(8,128)(2,1)S(1)}, bf16[64,768]{1,0:T(8,128)(2,1)S(1)}, u32[]{:S(2)}, u32[]{:S(2)}) collective-permute-start(bf16[64,768]{1,0:T(8,128)(2,1)S(1)} %get-tuple-element.20), channel_id=1, source_target_pairs={{0,14},{2,12},{4,10},{6,8},{8,6},{10,4},{12,2},{14,0},{1,15},{3,13... | collective-permute-start | bytes 294920 | tf_op jit(solution)/shard_map/ppermute | solution.py:187
  16.0 2.5 %collective-permute-done.13.refs_7_ = bf16[64,768]{1,0:T(8,128)(2,1)S(1)} collective-permute-done((bf16[64,768]{1,0:T(8,128)(2,1)S(1)}, bf16[64,768]{1,0:T(8,128)(2,1)S(1)}, u32[]{:S(2)}, u32[]{:S(2)}) %collective-permute-start.13) | collective-permute-done | bytes 98336 | tf_op jit(solution)/shard_map/ppermute | solution.py:187
  18.6 0.0 collective-permute-start
  18.6 0.5 %collective-permute-start.10 = (bf16[64,768]{1,0:T(8,128)(2,1)S(1)}, bf16[64,768]{1,0:T(8,128)(2,1)S(1)}, u32[]{:S(2)}, u32[]{:S(2)}) collective-permute-start(bf16[64,768]{1,0:T(8,128)(2,1)S(1)} %collective-permute-done.9.refs_5_), channel_id=1, source_target_pairs={{0,1},{1,0},{2,3},{3,2},{4,5},{5,4},{6,7},{7,6},{8,9},{9,8},{10,11... | collective-permute-start | bytes 294920 | tf_op jit(solution)/shard_map/ppermute | solution.py:187
  19.1 3.9 %collective-permute-done.3.refs_2_ = bf16[64,768]{1,0:T(8,128)(2,1)S(1)} collective-permute-done((bf16[64,768]{1,0:T(8,128)(2,1)S(1)}, bf16[64,768]{1,0:T(8,128)(2,1)S(1)}, u32[]{:S(2)}, u32[]{:S(2)}) %collective-permute-start.3) | collective-permute-done | bytes 98336 | tf_op jit(solution)/shard_map/ppermute | solution.py:187
  23.0 0.5 %collective-permute-start.14 = (bf16[64,768]{1,0:T(8,128)(2,1)S(1)}, bf16[64,768]{1,0:T(8,128)(2,1)S(1)}, u32[]{:S(2)}, u32[]{:S(2)}) collective-permute-start(bf16[64,768]{1,0:T(8,128)(2,1)S(1)} %collective-permute-done.13.refs_7_), channel_id=1, source_target_pairs={{0,1},{1,0},{2,3},{3,2},{4,5},{5,4},{6,7},{7,6},{8,9},{9,8},{10,11... | collective-permute-start | bytes 294920 | tf_op jit(solution)/shard_map/ppermute | solution.py:187
  23.5 0.1 collective-permute-start.2
  23.6 0.4 %collective-permute-start.4 = (bf16[64,768]{1,0:T(8,128)(2,1)S(1)}, bf16[64,768]{1,0:T(8,128)(2,1)S(1)}, u32[]{:S(2)}, u32[]{:S(2)}) collective-permute-start(bf16[64,768]{1,0:T(8,128)(2,1)S(1)} %collective-permute-done.3.refs_2_), channel_id=1, source_target_pairs={{0,1},{1,0},{2,3},{3,2},{4,5},{5,4},{6,7},{7,6},{8,9},{9,8},{10,11... | collective-permute-start | bytes 294920 | tf_op jit(solution)/shard_map/ppermute | solution.py:187
  24.0 0.1 collective-permute-start.6
  24.1 0.2 collective-permute-done.12.refs_6_
  24.3 0.2 collective-permute-start.8
  24.6 0.7 %shard_map.29 = (bf16[512,768]{1,0:T(8,128)(2,1)S(1)}, f32[1,512]{1,0:T(1,128)S(1)}) custom-call(bf16[64,768]{1,0:T(8,128)(2,1)S(1)} %get-tuple-element.16.refs_0_, bf16[64,768]{1,0:T(8,128)(2,1)S(1)} %collective-permute-done.1.refs_1_, bf16[64,768]{1,0:T(8,128)(2,1)S(1)} %collective-permute-done.3.refs_2_, ...), custom_call_target="tpu_custom_call" | custom-call | flops 402653184 | bytes 1572864 | tf_op jit(solution)/shard_map/pallas_call | solution.py:113
  25.3 0.1 collective-permute-done.6.refs_3_
  25.3 0.3 collective-permute-done.8.refs_4_
  25.6 0.7 %shard_map.30 = f32[8,128]{1,0:T(8,128)S(1)} custom-call(s32[1]{0:T(128)} %bitcast.me_ref, bf16[64,768]{1,0:T(8,128)(2,1)S(1)} %collective-permute-done.refs_0_, bf16[64,768]{1,0:T(8,128)(2,1)S(1)} %collective-permute-done.2.refs_1_, bf16[64,768]{1,0:T(8,128)(2,1)S(1)} %collective-permute-done.4.refs_2_, bf16[64,768]{1,0:T(8,128)(2,1)S(1)} %collective-permute-done.6.refs_3_, ...), custom_call_target="tpu_custom_call" | custom-call | tf_op jit(solution)/shard_map/pallas_call | solution.py:143
  26.3 10.2 %all_to_all.11 = f32[8,1,128]{2,1,0:T(1,128)S(1)} all-to-all(f32[8,1,128]{2,1,0:T(1,128)S(1)} %bitcast.5), channel_id=1, replica_groups=mesh['groups'=2,'blk'=8,'pair'=2] {'blk'}, dimensions={0} | all-to-all | bytes 8192 | tf_op jit(solution)/shard_map/all_to_all | solution.py:201
  36.5 0.8 %shard_map.31 = f32[256]{0:T(256)} custom-call(s32[1]{0:T(128)} %bitcast.me_ref, f32[8,128]{1,0:T(8,128)S(1)} %bitcast.6, bf16[512,256]{1,0:T(8,128)(2,1)S(1)} %get-tuple-element.26.pick_ref), custom_call_target="tpu_custom_call" | custom-call | tf_op jit(solution)/shard_map/pallas_call | solution.py:169
  (11 shorter events, 0.0 us)
Async XLA Ops:
  1.9 9.5 %collective-permute-start.1 = (bf16[64,768]{1,0:T(8,128)(2,1)S(1)}, bf16[64,768]{1,0:T(8,128)(2,1)S(1)}, u32[]{:S(2)}, u32[]{:S(2)}) collective-permute-start(bf16[64,768]{1,0:T(8,128)(2,1)S(1)} %get-tuple-element.17), channel_id=1, source_target_pairs={{0,12},{2,14},{4,8},{6,10},{8,4},{10,6},{12,0},{14,2},{1,13},{3,15... | collective-permute-start | bytes 294920 | tf_op jit(solution)/shard_map/ppermute | solution.py:187
  7.0 7.3 %collective-permute-start.11 = (bf16[64,768]{1,0:T(8,128)(2,1)S(1)}, bf16[64,768]{1,0:T(8,128)(2,1)S(1)}, u32[]{:S(2)}, u32[]{:S(2)}) collective-permute-start(bf16[64,768]{1,0:T(8,128)(2,1)S(1)} %get-tuple-element.22), channel_id=1, source_target_pairs={{0,4},{2,6},{4,0},{6,2},{8,12},{10,14},{12,8},{14,10},{1,5},{3,7},... | collective-permute-start | bytes 294920 | tf_op jit(solution)/shard_map/ppermute | solution.py:187
  7.0 11.6 %collective-permute-start.13 = (bf16[64,768]{1,0:T(8,128)(2,1)S(1)}, bf16[64,768]{1,0:T(8,128)(2,1)S(1)}, u32[]{:S(2)}, u32[]{:S(2)}) collective-permute-start(bf16[64,768]{1,0:T(8,128)(2,1)S(1)} %get-tuple-element.23), channel_id=1, source_target_pairs={{0,8},{2,10},{4,12},{6,14},{8,0},{10,2},{12,4},{14,6},{1,9},{3,11}... | collective-permute-start | bytes 294920 | tf_op jit(solution)/shard_map/ppermute | solution.py:187
  7.6 11.0 %collective-permute-start.9 = (bf16[64,768]{1,0:T(8,128)(2,1)S(1)}, bf16[64,768]{1,0:T(8,128)(2,1)S(1)}, u32[]{:S(2)}, u32[]{:S(2)}) collective-permute-start(bf16[64,768]{1,0:T(8,128)(2,1)S(1)} %get-tuple-element.21), channel_id=1, source_target_pairs={{0,2},{2,0},{4,6},{6,4},{8,10},{10,8},{12,14},{14,12},{1,3},{3,1},... | collective-permute-start | bytes 294920 | tf_op jit(solution)/shard_map/ppermute | solution.py:187
  9.3 13.8 %collective-permute-start.3 = (bf16[64,768]{1,0:T(8,128)(2,1)S(1)}, bf16[64,768]{1,0:T(8,128)(2,1)S(1)}, u32[]{:S(2)}, u32[]{:S(2)}) collective-permute-start(bf16[64,768]{1,0:T(8,128)(2,1)S(1)} %get-tuple-element.18), channel_id=1, source_target_pairs={{0,10},{2,8},{4,14},{6,12},{8,2},{10,0},{12,6},{14,4},{1,11},{3,9}... | collective-permute-start | bytes 294920 | tf_op jit(solution)/shard_map/ppermute | solution.py:187
  11.4 11.6 %collective-permute-start.5 = (bf16[64,768]{1,0:T(8,128)(2,1)S(1)}, bf16[64,768]{1,0:T(8,128)(2,1)S(1)}, u32[]{:S(2)}, u32[]{:S(2)}) collective-permute-start(bf16[64,768]{1,0:T(8,128)(2,1)S(1)} %get-tuple-element.19), channel_id=1, source_target_pairs={{0,6},{2,4},{4,2},{6,0},{8,14},{10,12},{12,10},{14,8},{1,7},{3,5},... | collective-permute-start | bytes 294920 | tf_op jit(solution)/shard_map/ppermute | solution.py:187
  14.3 9.2 %collective-permute-start.7 = (bf16[64,768]{1,0:T(8,128)(2,1)S(1)}, bf16[64,768]{1,0:T(8,128)(2,1)S(1)}, u32[]{:S(2)}, u32[]{:S(2)}) collective-permute-start(bf16[64,768]{1,0:T(8,128)(2,1)S(1)} %get-tuple-element.20), channel_id=1, source_target_pairs={{0,14},{2,12},{4,10},{6,8},{8,6},{10,4},{12,2},{14,0},{1,15},{3,13... | collective-permute-start | bytes 294920 | tf_op jit(solution)/shard_map/ppermute | solution.py:187
  18.6 5.0 %collective-permute-start = (bf16[64,768]{1,0:T(8,128)(2,1)S(1)}, bf16[64,768]{1,0:T(8,128)(2,1)S(1)}, u32[]{:S(2)}, u32[]{:S(2)}) collective-permute-start(bf16[64,768]{1,0:T(8,128)(2,1)S(1)} %get-tuple-element.16.refs_0_), channel_id=1, source_target_pairs={{0,1},{1,0},{2,3},{3,2},{4,5},{5,4},{6,7},{7,6},{8,9},{9,8},{10,11... | collective-permute-start | bytes 294920 | tf_op jit(solution)/shard_map/ppermute | solution.py:187
  18.6 5.5 %collective-permute-start.10 = (bf16[64,768]{1,0:T(8,128)(2,1)S(1)}, bf16[64,768]{1,0:T(8,128)(2,1)S(1)}, u32[]{:S(2)}, u32[]{:S(2)}) collective-permute-start(bf16[64,768]{1,0:T(8,128)(2,1)S(1)} %collective-permute-done.9.refs_5_), channel_id=1, source_target_pairs={{0,1},{1,0},{2,3},{3,2},{4,5},{5,4},{6,7},{7,6},{8,9},{9,8},{10,11... | collective-permute-start | bytes 294920 | tf_op jit(solution)/shard_map/ppermute | solution.py:187
  23.0 1.3 %collective-permute-start.12 = (bf16[64,768]{1,0:T(8,128)(2,1)S(1)}, bf16[64,768]{1,0:T(8,128)(2,1)S(1)}, u32[]{:S(2)}, u32[]{:S(2)}) collective-permute-start(bf16[64,768]{1,0:T(8,128)(2,1)S(1)} %collective-permute-done.11.refs_6_), channel_id=1, source_target_pairs={{0,1},{1,0},{2,3},{3,2},{4,5},{5,4},{6,7},{7,6},{8,9},{9,8},{10,11... | collective-permute-start | bytes 294920 | tf_op jit(solution)/shard_map/ppermute | solution.py:187
  23.0 2.2 %collective-permute-start.14 = (bf16[64,768]{1,0:T(8,128)(2,1)S(1)}, bf16[64,768]{1,0:T(8,128)(2,1)S(1)}, u32[]{:S(2)}, u32[]{:S(2)}) collective-permute-start(bf16[64,768]{1,0:T(8,128)(2,1)S(1)} %collective-permute-done.13.refs_7_), channel_id=1, source_target_pairs={{0,1},{1,0},{2,3},{3,2},{4,5},{5,4},{6,7},{7,6},{8,9},{9,8},{10,11... | collective-permute-start | bytes 294920 | tf_op jit(solution)/shard_map/ppermute | solution.py:187
  23.5 1.7 %collective-permute-start.2 = (bf16[64,768]{1,0:T(8,128)(2,1)S(1)}, bf16[64,768]{1,0:T(8,128)(2,1)S(1)}, u32[]{:S(2)}, u32[]{:S(2)}) collective-permute-start(bf16[64,768]{1,0:T(8,128)(2,1)S(1)} %collective-permute-done.1.refs_1_), channel_id=1, source_target_pairs={{0,1},{1,0},{2,3},{3,2},{4,5},{5,4},{6,7},{7,6},{8,9},{9,8},{10,11... | collective-permute-start | bytes 294920 | tf_op jit(solution)/shard_map/ppermute | solution.py:187
  23.6 1.7 %collective-permute-start.4 = (bf16[64,768]{1,0:T(8,128)(2,1)S(1)}, bf16[64,768]{1,0:T(8,128)(2,1)S(1)}, u32[]{:S(2)}, u32[]{:S(2)}) collective-permute-start(bf16[64,768]{1,0:T(8,128)(2,1)S(1)} %collective-permute-done.3.refs_2_), channel_id=1, source_target_pairs={{0,1},{1,0},{2,3},{3,2},{4,5},{5,4},{6,7},{7,6},{8,9},{9,8},{10,11... | collective-permute-start | bytes 294920 | tf_op jit(solution)/shard_map/ppermute | solution.py:187
  24.0 1.3 %collective-permute-start.6 = (bf16[64,768]{1,0:T(8,128)(2,1)S(1)}, bf16[64,768]{1,0:T(8,128)(2,1)S(1)}, u32[]{:S(2)}, u32[]{:S(2)}) collective-permute-start(bf16[64,768]{1,0:T(8,128)(2,1)S(1)} %collective-permute-done.5.refs_3_), channel_id=1, source_target_pairs={{0,1},{1,0},{2,3},{3,2},{4,5},{5,4},{6,7},{7,6},{8,9},{9,8},{10,11... | collective-permute-start | bytes 294920 | tf_op jit(solution)/shard_map/ppermute | solution.py:187
  24.3 1.3 %collective-permute-start.8 = (bf16[64,768]{1,0:T(8,128)(2,1)S(1)}, bf16[64,768]{1,0:T(8,128)(2,1)S(1)}, u32[]{:S(2)}, u32[]{:S(2)}) collective-permute-start(bf16[64,768]{1,0:T(8,128)(2,1)S(1)} %collective-permute-done.7.refs_4_), channel_id=1, source_target_pairs={{0,1},{1,0},{2,3},{3,2},{4,5},{5,4},{6,7},{7,6},{8,9},{9,8},{10,11... | collective-permute-start | bytes 294920 | tf_op jit(solution)/shard_map/ppermute | solution.py:187

commit v6 on v5

--- a/solution.py
+++ b/solution.py
@@ -13,6 +13,7 @@
 EMPTY_ABOVE = 1.5
 DIRECT_OWNERS = 8
 SCORE_LANES = 128
+COLUMNS = 256
 
 
 def vmem(count):
@@ -53,12 +54,17 @@
     values = rows_ref[...].astype(jnp.float32)
     scale = lax.rsqrt(jnp.sum(values * values, axis=1, keepdims=True) + EPSILON)
     units = (values * scale).astype(jnp.bfloat16)
-    for k, block_ref in enumerate(block_refs):
-        block = jnp.dot(
-            pick_ref[k * capacity:(k + 1) * capacity, :], units, preferred_element_type=jnp.float32
-        )
-        block_ref[...] = block.astype(jnp.bfloat16)
-        block_ref[:, 0:128] = (block[:, 0:128] + marks[k:k + 1, :]).astype(jnp.bfloat16)
+    width = units.shape[1]
+    for left in range(0, width, COLUMNS):
+        right = min(left + COLUMNS, width)
+        columns = jnp.dot(pick_ref[...], units[:, left:right], preferred_element_type=jnp.float32)
+        for k, block_ref in enumerate(block_refs):
+            block = columns[k * capacity:(k + 1) * capacity]
+            if left == 0:
+                block_ref[:, 0:128] = (block[:, 0:128] + marks[k:k + 1, :]).astype(jnp.bfloat16)
+                block_ref[:, 128:right] = block[:, 128:].astype(jnp.bfloat16)
+            else:
+                block_ref[:, left:right] = block.astype(jnp.bfloat16)
 
 
 def prepare(me, rows, ids, owners, capacity):

time: 37.5 us -> 37.2 us (level)
  no operation moved by 1% of the time
where the time goes in v6:
time: 37.2 us; the launch traced here: 37 us
  starting transfers between devices  16 us (43%)
  blocking collectives  10.2 us (27%)
  waiting for transfers between devices  7.02 us (19%)
  Pallas kernels  3.72 us (10%)
    ppermute x15, starting transfers between devices, swap(): return lax.ppermute(block, axis, [(i, i ^ step) for i in range(size)])  16 us
    all_to_all x1, blocking collectives, direct_shards(): lax.all_to_all(scores, 'blk', split_axis=0, concat_axis=0, tiled=True)  10.2 us
    ppermute x15, waiting for transfers between devices, swap(): return lax.ppermute(block, axis, [(i, i ^ step) for i in range(size)])  7.02 us
    pallas_call x1, Pallas kernels, prepare(): pl.pallas_call(functools.partial(prepare_kernel, owners, capacity), out_s...  1.55 us
    pallas_call x1, Pallas kernels, collect(): pl.pallas_call(functools.partial(collect_kernel, capacity), out_shape=jax...  0.76 us
  transfers between devices with their start and end apart: 15, of which 5 were waited for; matrix products, arithmetic and copies ran while one was open for 0% of the time, Pallas kernels for 2%

profile of v6, /device:TPU:0, one launch (start us, length us, event | category | flops | bytes accessed | tf_op | source)
XLA Modules:
  0.0 37.0 jit_solution(9829846013638838028)
XLA Ops:
  0.0 1.5 %shard_map.28 = (bf16[64,768]{1,0:T(8,128)(2,1)S(1)}, bf16[64,768]{1,0:T(8,128)(2,1)S(1)}, bf16[64,768]{1,0:T(8,128)(2,1)S(1)}, bf16[64,768]{1,0:T(8,128)(2,1)S(...) custom-call(s32[1]{0:T(128)} %bitcast.me_ref, ...), custom_call_target="tpu_custom_call" | custom-call | tf_op jit(solution)/shard_map/pallas_call | solution.py:72
  1.6 5.1 %collective-permute-start.1 = (bf16[64,768]{1,0:T(8,128)(2,1)S(1)}, bf16[64,768]{1,0:T(8,128)(2,1)S(1)}, u32[]{:S(2)}, u32[]{:S(2)}) collective-permute-start(bf16[64,768]{1,0:T(8,128)(2,1)S(1)} %get-tuple-element.17), channel_id=1, source_target_pairs={{0,12},{2,14},{4,8},{6,10},{8,4},{10,6},{12,0},{14,2},{1,13},{3,15... | collective-permute-start | bytes 294920 | tf_op jit(solution)/shard_map/ppermute | solution.py:193
  6.7 0.0 collective-permute-start.11
  6.7 0.6 %collective-permute-start.13 = (bf16[64,768]{1,0:T(8,128)(2,1)S(1)}, bf16[64,768]{1,0:T(8,128)(2,1)S(1)}, u32[]{:S(2)}, u32[]{:S(2)}) collective-permute-start(bf16[64,768]{1,0:T(8,128)(2,1)S(1)} %get-tuple-element.23), channel_id=1, source_target_pairs={{0,8},{2,10},{4,12},{6,14},{8,0},{10,2},{12,4},{14,6},{1,9},{3,11}... | collective-permute-start | bytes 294920 | tf_op jit(solution)/shard_map/ppermute | solution.py:193
  7.3 1.6 %collective-permute-start.9 = (bf16[64,768]{1,0:T(8,128)(2,1)S(1)}, bf16[64,768]{1,0:T(8,128)(2,1)S(1)}, u32[]{:S(2)}, u32[]{:S(2)}) collective-permute-start(bf16[64,768]{1,0:T(8,128)(2,1)S(1)} %get-tuple-element.21), channel_id=1, source_target_pairs={{0,2},{2,0},{4,6},{6,4},{8,10},{10,8},{12,14},{14,12},{1,3},{3,1},... | collective-permute-start | bytes 294920 | tf_op jit(solution)/shard_map/ppermute | solution.py:193
  8.9 2.1 %collective-permute-start.3 = (bf16[64,768]{1,0:T(8,128)(2,1)S(1)}, bf16[64,768]{1,0:T(8,128)(2,1)S(1)}, u32[]{:S(2)}, u32[]{:S(2)}) collective-permute-start(bf16[64,768]{1,0:T(8,128)(2,1)S(1)} %get-tuple-element.18), channel_id=1, source_target_pairs={{0,10},{2,8},{4,14},{6,12},{8,2},{10,0},{12,6},{14,4},{1,11},{3,9}... | collective-permute-start | bytes 294920 | tf_op jit(solution)/shard_map/ppermute | solution.py:193
  11.1 0.0 collective-permute-done.1.refs_1_
  11.1 3.0 %collective-permute-start.5 = (bf16[64,768]{1,0:T(8,128)(2,1)S(1)}, bf16[64,768]{1,0:T(8,128)(2,1)S(1)}, u32[]{:S(2)}, u32[]{:S(2)}) collective-permute-start(bf16[64,768]{1,0:T(8,128)(2,1)S(1)} %get-tuple-element.19), channel_id=1, source_target_pairs={{0,6},{2,4},{4,2},{6,0},{8,14},{10,12},{12,10},{14,8},{1,7},{3,5},... | collective-permute-start | bytes 294920 | tf_op jit(solution)/shard_map/ppermute | solution.py:193
  14.0 1.7 %collective-permute-start.7 = (bf16[64,768]{1,0:T(8,128)(2,1)S(1)}, bf16[64,768]{1,0:T(8,128)(2,1)S(1)}, u32[]{:S(2)}, u32[]{:S(2)}) collective-permute-start(bf16[64,768]{1,0:T(8,128)(2,1)S(1)} %get-tuple-element.20), channel_id=1, source_target_pairs={{0,14},{2,12},{4,10},{6,8},{8,6},{10,4},{12,2},{14,0},{1,15},{3,13... | collective-permute-start | bytes 294920 | tf_op jit(solution)/shard_map/ppermute | solution.py:193
  15.7 2.5 %collective-permute-done.13.refs_7_ = bf16[64,768]{1,0:T(8,128)(2,1)S(1)} collective-permute-done((bf16[64,768]{1,0:T(8,128)(2,1)S(1)}, bf16[64,768]{1,0:T(8,128)(2,1)S(1)}, u32[]{:S(2)}, u32[]{:S(2)}) %collective-permute-start.13) | collective-permute-done | bytes 98336 | tf_op jit(solution)/shard_map/ppermute | solution.py:193
  18.3 0.5 %collective-permute-start.10 = (bf16[64,768]{1,0:T(8,128)(2,1)S(1)}, bf16[64,768]{1,0:T(8,128)(2,1)S(1)}, u32[]{:S(2)}, u32[]{:S(2)}) collective-permute-start(bf16[64,768]{1,0:T(8,128)(2,1)S(1)} %collective-permute-done.9.refs_5_), channel_id=1, source_target_pairs={{0,1},{1,0},{2,3},{3,2},{4,5},{5,4},{6,7},{7,6},{8,9},{9,8},{10,11... | collective-permute-start | bytes 294920 | tf_op jit(solution)/shard_map/ppermute | solution.py:193
  18.8 3.9 %collective-permute-done.3.refs_2_ = bf16[64,768]{1,0:T(8,128)(2,1)S(1)} collective-permute-done((bf16[64,768]{1,0:T(8,128)(2,1)S(1)}, bf16[64,768]{1,0:T(8,128)(2,1)S(1)}, u32[]{:S(2)}, u32[]{:S(2)}) %collective-permute-start.3) | collective-permute-done | bytes 98336 | tf_op jit(solution)/shard_map/ppermute | solution.py:193
  22.7 0.5 %collective-permute-start.14 = (bf16[64,768]{1,0:T(8,128)(2,1)S(1)}, bf16[64,768]{1,0:T(8,128)(2,1)S(1)}, u32[]{:S(2)}, u32[]{:S(2)}) collective-permute-start(bf16[64,768]{1,0:T(8,128)(2,1)S(1)} %collective-permute-done.13.refs_7_), channel_id=1, source_target_pairs={{0,1},{1,0},{2,3},{3,2},{4,5},{5,4},{6,7},{7,6},{8,9},{9,8},{10,11... | collective-permute-start | bytes 294920 | tf_op jit(solution)/shard_map/ppermute | solution.py:193
  23.2 0.1 collective-permute-start.2
  23.3 0.4 %collective-permute-start.4 = (bf16[64,768]{1,0:T(8,128)(2,1)S(1)}, bf16[64,768]{1,0:T(8,128)(2,1)S(1)}, u32[]{:S(2)}, u32[]{:S(2)}) collective-permute-start(bf16[64,768]{1,0:T(8,128)(2,1)S(1)} %collective-permute-done.3.refs_2_), channel_id=1, source_target_pairs={{0,1},{1,0},{2,3},{3,2},{4,5},{5,4},{6,7},{7,6},{8,9},{9,8},{10,11... | collective-permute-start | bytes 294920 | tf_op jit(solution)/shard_map/ppermute | solution.py:193
  23.7 0.1 collective-permute-start.6
  23.8 0.2 collective-permute-done.12.refs_6_
  24.0 0.2 collective-permute-start.8
  24.3 0.7 %shard_map.29 = (bf16[512,768]{1,0:T(8,128)(2,1)S(1)}, f32[1,512]{1,0:T(1,128)S(1)}) custom-call(bf16[64,768]{1,0:T(8,128)(2,1)S(1)} %get-tuple-element.16.refs_0_, bf16[64,768]{1,0:T(8,128)(2,1)S(1)} %collective-permute-done.1.refs_1_, bf16[64,768]{1,0:T(8,128)(2,1)S(1)} %collective-permute-done.3.refs_2_, ...), custom_call_target="tpu_custom_call" | custom-call | flops 402653184 | bytes 1572864 | tf_op jit(solution)/shard_map/pallas_call | solution.py:119
  25.0 0.1 collective-permute-done.6.refs_3_
  25.0 0.3 collective-permute-done.8.refs_4_
  25.3 0.7 %shard_map.30 = f32[8,128]{1,0:T(8,128)S(1)} custom-call(s32[1]{0:T(128)} %bitcast.me_ref, bf16[64,768]{1,0:T(8,128)(2,1)S(1)} %collective-permute-done.refs_0_, bf16[64,768]{1,0:T(8,128)(2,1)S(1)} %collective-permute-done.2.refs_1_, bf16[64,768]{1,0:T(8,128)(2,1)S(1)} %collective-permute-done.4.refs_2_, bf16[64,768]{1,0:T(8,128)(2,1)S(1)} %collective-permute-done.6.refs_3_, ...), custom_call_target="tpu_custom_call" | custom-call | tf_op jit(solution)/shard_map/pallas_call | solution.py:149
  26.0 10.2 %all_to_all.11 = f32[8,1,128]{2,1,0:T(1,128)S(1)} all-to-all(f32[8,1,128]{2,1,0:T(1,128)S(1)} %bitcast.5), channel_id=1, replica_groups=mesh['groups'=2,'blk'=8,'pair'=2] {'blk'}, dimensions={0} | all-to-all | bytes 8192 | tf_op jit(solution)/shard_map/all_to_all | solution.py:207
  36.2 0.8 %shard_map.31 = f32[256]{0:T(256)} custom-call(s32[1]{0:T(128)} %bitcast.me_ref, f32[8,128]{1,0:T(8,128)S(1)} %bitcast.6, bf16[512,256]{1,0:T(8,128)(2,1)S(1)} %get-tuple-element.26.pick_ref), custom_call_target="tpu_custom_call" | custom-call | tf_op jit(solution)/shard_map/pallas_call | solution.py:175
  (11 shorter events, 0.0 us)
Async XLA Ops:
  1.6 9.5 %collective-permute-start.1 = (bf16[64,768]{1,0:T(8,128)(2,1)S(1)}, bf16[64,768]{1,0:T(8,128)(2,1)S(1)}, u32[]{:S(2)}, u32[]{:S(2)}) collective-permute-start(bf16[64,768]{1,0:T(8,128)(2,1)S(1)} %get-tuple-element.17), channel_id=1, source_target_pairs={{0,12},{2,14},{4,8},{6,10},{8,4},{10,6},{12,0},{14,2},{1,13},{3,15... | collective-permute-start | bytes 294920 | tf_op jit(solution)/shard_map/ppermute | solution.py:193
  6.7 7.3 %collective-permute-start.11 = (bf16[64,768]{1,0:T(8,128)(2,1)S(1)}, bf16[64,768]{1,0:T(8,128)(2,1)S(1)}, u32[]{:S(2)}, u32[]{:S(2)}) collective-permute-start(bf16[64,768]{1,0:T(8,128)(2,1)S(1)} %get-tuple-element.22), channel_id=1, source_target_pairs={{0,4},{2,6},{4,0},{6,2},{8,12},{10,14},{12,8},{14,10},{1,5},{3,7},... | collective-permute-start | bytes 294920 | tf_op jit(solution)/shard_map/ppermute | solution.py:193
  6.7 11.6 %collective-permute-start.13 = (bf16[64,768]{1,0:T(8,128)(2,1)S(1)}, bf16[64,768]{1,0:T(8,128)(2,1)S(1)}, u32[]{:S(2)}, u32[]{:S(2)}) collective-permute-start(bf16[64,768]{1,0:T(8,128)(2,1)S(1)} %get-tuple-element.23), channel_id=1, source_target_pairs={{0,8},{2,10},{4,12},{6,14},{8,0},{10,2},{12,4},{14,6},{1,9},{3,11}... | collective-permute-start | bytes 294920 | tf_op jit(solution)/shard_map/ppermute | solution.py:193
  7.3 11.0 %collective-permute-start.9 = (bf16[64,768]{1,0:T(8,128)(2,1)S(1)}, bf16[64,768]{1,0:T(8,128)(2,1)S(1)}, u32[]{:S(2)}, u32[]{:S(2)}) collective-permute-start(bf16[64,768]{1,0:T(8,128)(2,1)S(1)} %get-tuple-element.21), channel_id=1, source_target_pairs={{0,2},{2,0},{4,6},{6,4},{8,10},{10,8},{12,14},{14,12},{1,3},{3,1},... | collective-permute-start | bytes 294920 | tf_op jit(solution)/shard_map/ppermute | solution.py:193
  8.9 13.8 %collective-permute-start.3 = (bf16[64,768]{1,0:T(8,128)(2,1)S(1)}, bf16[64,768]{1,0:T(8,128)(2,1)S(1)}, u32[]{:S(2)}, u32[]{:S(2)}) collective-permute-start(bf16[64,768]{1,0:T(8,128)(2,1)S(1)} %get-tuple-element.18), channel_id=1, source_target_pairs={{0,10},{2,8},{4,14},{6,12},{8,2},{10,0},{12,6},{14,4},{1,11},{3,9}... | collective-permute-start | bytes 294920 | tf_op jit(solution)/shard_map/ppermute | solution.py:193
  11.1 11.7 %collective-permute-start.5 = (bf16[64,768]{1,0:T(8,128)(2,1)S(1)}, bf16[64,768]{1,0:T(8,128)(2,1)S(1)}, u32[]{:S(2)}, u32[]{:S(2)}) collective-permute-start(bf16[64,768]{1,0:T(8,128)(2,1)S(1)} %get-tuple-element.19), channel_id=1, source_target_pairs={{0,6},{2,4},{4,2},{6,0},{8,14},{10,12},{12,10},{14,8},{1,7},{3,5},... | collective-permute-start | bytes 294920 | tf_op jit(solution)/shard_map/ppermute | solution.py:193
  14.0 9.2 %collective-permute-start.7 = (bf16[64,768]{1,0:T(8,128)(2,1)S(1)}, bf16[64,768]{1,0:T(8,128)(2,1)S(1)}, u32[]{:S(2)}, u32[]{:S(2)}) collective-permute-start(bf16[64,768]{1,0:T(8,128)(2,1)S(1)} %get-tuple-element.20), channel_id=1, source_target_pairs={{0,14},{2,12},{4,10},{6,8},{8,6},{10,4},{12,2},{14,0},{1,15},{3,13... | collective-permute-start | bytes 294920 | tf_op jit(solution)/shard_map/ppermute | solution.py:193
  18.3 5.0 %collective-permute-start = (bf16[64,768]{1,0:T(8,128)(2,1)S(1)}, bf16[64,768]{1,0:T(8,128)(2,1)S(1)}, u32[]{:S(2)}, u32[]{:S(2)}) collective-permute-start(bf16[64,768]{1,0:T(8,128)(2,1)S(1)} %get-tuple-element.16.refs_0_), channel_id=1, source_target_pairs={{0,1},{1,0},{2,3},{3,2},{4,5},{5,4},{6,7},{7,6},{8,9},{9,8},{10,11... | collective-permute-start | bytes 294920 | tf_op jit(solution)/shard_map/ppermute | solution.py:193
  18.3 5.5 %collective-permute-start.10 = (bf16[64,768]{1,0:T(8,128)(2,1)S(1)}, bf16[64,768]{1,0:T(8,128)(2,1)S(1)}, u32[]{:S(2)}, u32[]{:S(2)}) collective-permute-start(bf16[64,768]{1,0:T(8,128)(2,1)S(1)} %collective-permute-done.9.refs_5_), channel_id=1, source_target_pairs={{0,1},{1,0},{2,3},{3,2},{4,5},{5,4},{6,7},{7,6},{8,9},{9,8},{10,11... | collective-permute-start | bytes 294920 | tf_op jit(solution)/shard_map/ppermute | solution.py:193
  22.7 1.3 %collective-permute-start.12 = (bf16[64,768]{1,0:T(8,128)(2,1)S(1)}, bf16[64,768]{1,0:T(8,128)(2,1)S(1)}, u32[]{:S(2)}, u32[]{:S(2)}) collective-permute-start(bf16[64,768]{1,0:T(8,128)(2,1)S(1)} %collective-permute-done.11.refs_6_), channel_id=1, source_target_pairs={{0,1},{1,0},{2,3},{3,2},{4,5},{5,4},{6,7},{7,6},{8,9},{9,8},{10,11... | collective-permute-start | bytes 294920 | tf_op jit(solution)/shard_map/ppermute | solution.py:193
  22.7 2.2 %collective-permute-start.14 = (bf16[64,768]{1,0:T(8,128)(2,1)S(1)}, bf16[64,768]{1,0:T(8,128)(2,1)S(1)}, u32[]{:S(2)}, u32[]{:S(2)}) collective-permute-start(bf16[64,768]{1,0:T(8,128)(2,1)S(1)} %collective-permute-done.13.refs_7_), channel_id=1, source_target_pairs={{0,1},{1,0},{2,3},{3,2},{4,5},{5,4},{6,7},{7,6},{8,9},{9,8},{10,11... | collective-permute-start | bytes 294920 | tf_op jit(solution)/shard_map/ppermute | solution.py:193
  23.2 1.7 %collective-permute-start.2 = (bf16[64,768]{1,0:T(8,128)(2,1)S(1)}, bf16[64,768]{1,0:T(8,128)(2,1)S(1)}, u32[]{:S(2)}, u32[]{:S(2)}) collective-permute-start(bf16[64,768]{1,0:T(8,128)(2,1)S(1)} %collective-permute-done.1.refs_1_), channel_id=1, source_target_pairs={{0,1},{1,0},{2,3},{3,2},{4,5},{5,4},{6,7},{7,6},{8,9},{9,8},{10,11... | collective-permute-start | bytes 294920 | tf_op jit(solution)/shard_map/ppermute | solution.py:193
  23.3 1.7 %collective-permute-start.4 = (bf16[64,768]{1,0:T(8,128)(2,1)S(1)}, bf16[64,768]{1,0:T(8,128)(2,1)S(1)}, u32[]{:S(2)}, u32[]{:S(2)}) collective-permute-start(bf16[64,768]{1,0:T(8,128)(2,1)S(1)} %collective-permute-done.3.refs_2_), channel_id=1, source_target_pairs={{0,1},{1,0},{2,3},{3,2},{4,5},{5,4},{6,7},{7,6},{8,9},{9,8},{10,11... | collective-permute-start | bytes 294920 | tf_op jit(solution)/shard_map/ppermute | solution.py:193
  23.7 1.3 %collective-permute-start.6 = (bf16[64,768]{1,0:T(8,128)(2,1)S(1)}, bf16[64,768]{1,0:T(8,128)(2,1)S(1)}, u32[]{:S(2)}, u32[]{:S(2)}) collective-permute-start(bf16[64,768]{1,0:T(8,128)(2,1)S(1)} %collective-permute-done.5.refs_3_), channel_id=1, source_target_pairs={{0,1},{1,0},{2,3},{3,2},{4,5},{5,4},{6,7},{7,6},{8,9},{9,8},{10,11... | collective-permute-start | bytes 294920 | tf_op jit(solution)/shard_map/ppermute | solution.py:193
  24.0 1.3 %collective-permute-start.8 = (bf16[64,768]{1,0:T(8,128)(2,1)S(1)}, bf16[64,768]{1,0:T(8,128)(2,1)S(1)}, u32[]{:S(2)}, u32[]{:S(2)}) collective-permute-start(bf16[64,768]{1,0:T(8,128)(2,1)S(1)} %collective-permute-done.7.refs_4_), channel_id=1, source_target_pairs={{0,1},{1,0},{2,3},{3,2},{4,5},{5,4},{6,7},{7,6},{8,9},{9,8},{10,11... | collective-permute-start | bytes 294920 | tf_op jit(solution)/shard_map/ppermute | solution.py:193

commit v7 on v6

--- a/solution.py
+++ b/solution.py
@@ -1,4 +1,5 @@
 import functools
+import math
 
 import jax
 import jax.numpy as jnp
@@ -8,6 +9,7 @@
 from jax.sharding import PartitionSpec as P
 
 SHARPNESS = 10.0
+SHARPNESS_LOG2 = SHARPNESS * math.log2(math.e)
 EPSILON = 1e-06
 EMPTY_MARK = 2.0
 EMPTY_ABOVE = 1.5
@@ -26,7 +28,7 @@
 
 def prepare_kernel(owners, capacity, me_ref, rows_hbm, ids_hbm, *refs):
     block_refs = refs[:owners]
-    pick_ref, rows_ref, ids_ref, sems = refs[owners:]
+    ranks_ref, ids_row_ref, pick_ref, rows_ref, ids_ref, sems = refs[owners:]
     ids_copy = pltpu.make_async_copy(ids_hbm, ids_ref, sems.at[0])
     rows_copy = pltpu.make_async_copy(rows_hbm, rows_ref, sems.at[1])
     ids_copy.start()
@@ -37,7 +39,9 @@
     earlier = jnp.where(above < right, 1.0, 0.0).astype(jnp.bfloat16)
     labels = lax.broadcasted_iota(jnp.int32, (owners, row_count), 0)
     ids_copy.wait()
-    step = jnp.reshape(ids_ref[...], (1, row_count)) ^ me_ref[0]
+    ids = jnp.reshape(ids_ref[...], (1, row_count))
+    ids_row_ref[...] = ids
+    step = ids ^ me_ref[0]
     relative = sum(jnp.where(step == value, k, 0) for k, value in enumerate(steps_of(owners)))
     inside = (labels == relative).astype(jnp.float32)
     before = jnp.dot(inside.astype(jnp.bfloat16), earlier, preferred_element_type=jnp.float32)
@@ -46,6 +50,9 @@
     slots = owners * capacity
     pick_ref[...] = jnp.where(
         lax.broadcasted_iota(jnp.int32, (slots, row_count), 0) == slot, 1.0, 0.0
+    ).astype(jnp.bfloat16)
+    ranks_ref[...] = jnp.where(
+        lax.broadcasted_iota(jnp.int32, (capacity, row_count), 0) == rank, 1.0, 0.0
     ).astype(jnp.bfloat16)
     counts = jnp.broadcast_to(jnp.sum(inside, axis=1, keepdims=True), (owners, 128))
     first = lax.broadcasted_iota(jnp.int32, (owners, 128), 1) == 0
@@ -69,13 +76,17 @@
 
 def prepare(me, rows, ids, owners, capacity):
     row_count, width = rows.shape
-    *blocks, pick = pl.pallas_call(
+    *blocks, ranks, ids_row = pl.pallas_call(
         functools.partial(prepare_kernel, owners, capacity),
         out_shape=[jax.ShapeDtypeStruct((capacity, width), jnp.bfloat16)] * owners
-        + [jax.ShapeDtypeStruct((owners * capacity, row_count), jnp.bfloat16)],
+        + [
+            jax.ShapeDtypeStruct((capacity, row_count), jnp.bfloat16),
+            jax.ShapeDtypeStruct((1, row_count), jnp.int32),
+        ],
         in_specs=[pl.BlockSpec(memory_space=pltpu.SMEM)] + [pl.BlockSpec(memory_space=pltpu.HBM)] * 2,
-        out_specs=vmem(owners + 1),
+        out_specs=vmem(owners + 2),
         scratch_shapes=[
+            pltpu.VMEM((owners * capacity, row_count), jnp.bfloat16),
             pltpu.VMEM(rows.shape, rows.dtype),
             pltpu.VMEM(ids.shape, ids.dtype),
             pltpu.SemaphoreType.DMA((2,)),
@@ -86,7 +97,7 @@
         pltpu.with_memory_space_constraint(rows, pltpu.HBM),
         pltpu.with_memory_space_constraint(ids, pltpu.HBM),
     )
-    return blocks, pick
+    return blocks, ranks, ids_row
 
 
 def partial_sums(own, others, others_refs, own_block):
@@ -95,7 +106,7 @@
     total = jnp.zeros((1, count), jnp.float32)
     products = lax.dot_general(others, own, (((1,), (1,)), ((), ())), preferred_element_type=jnp.float32)
     for k, block_ref in enumerate(others_refs):
-        powers = jnp.exp(products[k * capacity:(k + 1) * capacity] * SHARPNESS)
+        powers = jnp.exp2(products[k * capacity:(k + 1) * capacity] * SHARPNESS_LOG2)
         if own_block:
             row = lax.broadcasted_iota(jnp.int32, powers.shape, 0) + k * capacity
             powers = jnp.where(row == lax.broadcasted_iota(jnp.int32, powers.shape, 1), 0.0, powers)
@@ -156,29 +167,31 @@
     )(me, *blocks, joined, total)
 
 
-def collect_kernel(capacity, me_ref, score_ref, pick_ref, out_ref):
-    me = me_ref[0]
-    scores = jnp.concatenate(
-        [score_ref[pl.ds(me ^ step, 1), 0:capacity] for step in steps_of(score_ref.shape[0])], axis=1
-    )
+def collect_kernel(score_ref, ranks_ref, ids_ref, out_ref):
+    owners = score_ref.shape[0]
+    capacity, row_count = ranks_ref.shape
+    scores = score_ref[:, 0:capacity]
     high = scores.astype(jnp.bfloat16)
     rest = scores - high.astype(jnp.float32)
     middle = rest.astype(jnp.bfloat16)
     low = (rest - middle.astype(jnp.float32)).astype(jnp.bfloat16)
-    parts = jnp.dot(
-        jnp.concatenate([high, middle, low], axis=0), pick_ref[...], preferred_element_type=jnp.float32
-    )
-    out_ref[...] = jnp.reshape((parts[0:1] + parts[1:2]) + parts[2:3], out_ref.shape)
-
-
-def collect(me, scores, pick, capacity):
+    ranks = ranks_ref[...]
+    by_rank = (
+        jnp.dot(high, ranks, preferred_element_type=jnp.float32)
+        + jnp.dot(middle, ranks, preferred_element_type=jnp.float32)
+    ) + jnp.dot(low, ranks, preferred_element_type=jnp.float32)
+    own = lax.broadcasted_iota(jnp.int32, (owners, row_count), 0) == ids_ref[...]
+    out_ref[...] = jnp.reshape(jnp.sum(jnp.where(own, by_rank, 0.0), axis=0, keepdims=True), out_ref.shape)
+
+
+def collect(scores, ranks, ids):
     return pl.pallas_call(
-        functools.partial(collect_kernel, capacity),
-        out_shape=jax.ShapeDtypeStruct((pick.shape[1],), jnp.float32),
-        in_specs=[pl.BlockSpec(memory_space=pltpu.SMEM)] + vmem(2),
+        collect_kernel,
+        out_shape=jax.ShapeDtypeStruct((ranks.shape[1],), jnp.float32),
+        in_specs=vmem(3),
         out_specs=pl.BlockSpec(memory_space=pltpu.VMEM),
         compiler_params=params(),
-    )(me, scores, pick)
+    )(scores, ranks, ids)
 
 
 def steps_of(owners):
@@ -197,7 +210,7 @@
     owners = lax.axis_size("blk")
     capacity = 2 * embeddings.shape[0] // owners
     me = jnp.reshape(lax.axis_index("blk").astype(jnp.int32), (1,))
-    blocks, pick = prepare(me, embeddings, cluster_ids, owners, capacity)
+    blocks, ranks, ids = prepare(me, embeddings, cluster_ids, owners, capacity)
     own_blocks = [None] * owners
     for k, step in enumerate(steps_of(owners)):
         own_blocks[k] = swap(blocks[k], "blk", step, owners)
@@ -205,7 +218,7 @@
     joined, total = own_sums(own_blocks)
     scores = cross_scores(me, other_blocks, joined, total)
     returned = lax.all_to_all(scores, "blk", split_axis=0, concat_axis=0, tiled=True)
-    return collect(me, returned, pick, capacity)
+    return collect(returned, ranks, ids)
 
 
 def unit_vectors(values):

time: 37.2 us -> 37.1 us (level)
  no operation moved by 1% of the time
where the time goes in v7:
time: 37.1 us; the launch traced here: 36.9 us
  starting transfers between devices  16 us (43%)
  blocking collectives  10.2 us (27%)
  waiting for transfers between devices  7.05 us (19%)
  Pallas kernels  3.62 us (10%)
    ppermute x15, starting transfers between devices, swap(): return lax.ppermute(block, axis, [(i, i ^ step) for i in range(size)])  16 us
    all_to_all x1, blocking collectives, direct_shards(): lax.all_to_all(scores, 'blk', split_axis=0, concat_axis=0, tiled=True)  10.2 us
    ppermute x15, waiting for transfers between devices, swap(): return lax.ppermute(block, axis, [(i, i ^ step) for i in range(size)])  7.05 us
    pallas_call x1, Pallas kernels, prepare(): pl.pallas_call(functools.partial(prepare_kernel, owners, capacity), out_s...  1.55 us
  transfers between devices with their start and end apart: 15, of which 5 were waited for; matrix products, arithmetic and copies ran while one was open for 0% of the time, Pallas kernels for 2%

profile of v7, /device:TPU:0, one launch (start us, length us, event | category | flops | bytes accessed | tf_op | source)
XLA Modules:
  0.0 36.9 jit_solution(16825418820240456756)
XLA Ops:
  0.0 1.5 %shard_map.28 = (bf16[64,768]{1,0:T(8,128)(2,1)S(1)}, bf16[64,768]{1,0:T(8,128)(2,1)S(1)}, bf16[64,768]{1,0:T(8,128)(2,1)S(1)}, bf16[64,768]{1,0:T(8,128)(2,1)S(...) custom-call(s32[1]{0:T(128)} %bitcast.me_ref, ...), custom_call_target="tpu_custom_call" | custom-call | tf_op jit(solution)/shard_map/pallas_call | solution.py:79
  1.6 5.1 %collective-permute-start.1 = (bf16[64,768]{1,0:T(8,128)(2,1)S(1)}, bf16[64,768]{1,0:T(8,128)(2,1)S(1)}, u32[]{:S(2)}, u32[]{:S(2)}) collective-permute-start(bf16[64,768]{1,0:T(8,128)(2,1)S(1)} %get-tuple-element.18), channel_id=1, source_target_pairs={{0,12},{2,14},{4,8},{6,10},{8,4},{10,6},{12,0},{14,2},{1,13},{3,15... | collective-permute-start | bytes 294920 | tf_op jit(solution)/shard_map/ppermute | solution.py:206
  6.7 0.0 collective-permute-start.11
  6.7 0.6 %collective-permute-start.13 = (bf16[64,768]{1,0:T(8,128)(2,1)S(1)}, bf16[64,768]{1,0:T(8,128)(2,1)S(1)}, u32[]{:S(2)}, u32[]{:S(2)}) collective-permute-start(bf16[64,768]{1,0:T(8,128)(2,1)S(1)} %get-tuple-element.24), channel_id=1, source_target_pairs={{0,8},{2,10},{4,12},{6,14},{8,0},{10,2},{12,4},{14,6},{1,9},{3,11}... | collective-permute-start | bytes 294920 | tf_op jit(solution)/shard_map/ppermute | solution.py:206
  7.3 1.6 %collective-permute-start.9 = (bf16[64,768]{1,0:T(8,128)(2,1)S(1)}, bf16[64,768]{1,0:T(8,128)(2,1)S(1)}, u32[]{:S(2)}, u32[]{:S(2)}) collective-permute-start(bf16[64,768]{1,0:T(8,128)(2,1)S(1)} %get-tuple-element.22), channel_id=1, source_target_pairs={{0,2},{2,0},{4,6},{6,4},{8,10},{10,8},{12,14},{14,12},{1,3},{3,1},... | collective-permute-start | bytes 294920 | tf_op jit(solution)/shard_map/ppermute | solution.py:206
  8.9 2.1 %collective-permute-start.3 = (bf16[64,768]{1,0:T(8,128)(2,1)S(1)}, bf16[64,768]{1,0:T(8,128)(2,1)S(1)}, u32[]{:S(2)}, u32[]{:S(2)}) collective-permute-start(bf16[64,768]{1,0:T(8,128)(2,1)S(1)} %get-tuple-element.19), channel_id=1, source_target_pairs={{0,10},{2,8},{4,14},{6,12},{8,2},{10,0},{12,6},{14,4},{1,11},{3,9}... | collective-permute-start | bytes 294920 | tf_op jit(solution)/shard_map/ppermute | solution.py:206
  11.1 0.0 collective-permute-done.1.refs_1_
  11.1 3.0 %collective-permute-start.5 = (bf16[64,768]{1,0:T(8,128)(2,1)S(1)}, bf16[64,768]{1,0:T(8,128)(2,1)S(1)}, u32[]{:S(2)}, u32[]{:S(2)}) collective-permute-start(bf16[64,768]{1,0:T(8,128)(2,1)S(1)} %get-tuple-element.20), channel_id=1, source_target_pairs={{0,6},{2,4},{4,2},{6,0},{8,14},{10,12},{12,10},{14,8},{1,7},{3,5},... | collective-permute-start | bytes 294920 | tf_op jit(solution)/shard_map/ppermute | solution.py:206
  14.0 1.7 %collective-permute-start.7 = (bf16[64,768]{1,0:T(8,128)(2,1)S(1)}, bf16[64,768]{1,0:T(8,128)(2,1)S(1)}, u32[]{:S(2)}, u32[]{:S(2)}) collective-permute-start(bf16[64,768]{1,0:T(8,128)(2,1)S(1)} %get-tuple-element.21), channel_id=1, source_target_pairs={{0,14},{2,12},{4,10},{6,8},{8,6},{10,4},{12,2},{14,0},{1,15},{3,13... | collective-permute-start | bytes 294920 | tf_op jit(solution)/shard_map/ppermute | solution.py:206
  15.7 2.5 %collective-permute-done.13.refs_7_ = bf16[64,768]{1,0:T(8,128)(2,1)S(1)} collective-permute-done((bf16[64,768]{1,0:T(8,128)(2,1)S(1)}, bf16[64,768]{1,0:T(8,128)(2,1)S(1)}, u32[]{:S(2)}, u32[]{:S(2)}) %collective-permute-start.13) | collective-permute-done | bytes 98336 | tf_op jit(solution)/shard_map/ppermute | solution.py:206
  18.3 0.5 %collective-permute-start.10 = (bf16[64,768]{1,0:T(8,128)(2,1)S(1)}, bf16[64,768]{1,0:T(8,128)(2,1)S(1)}, u32[]{:S(2)}, u32[]{:S(2)}) collective-permute-start(bf16[64,768]{1,0:T(8,128)(2,1)S(1)} %collective-permute-done.9.refs_5_), channel_id=1, source_target_pairs={{0,1},{1,0},{2,3},{3,2},{4,5},{5,4},{6,7},{7,6},{8,9},{9,8},{10,11... | collective-permute-start | bytes 294920 | tf_op jit(solution)/shard_map/ppermute | solution.py:206
  18.8 3.9 %collective-permute-done.3.refs_2_ = bf16[64,768]{1,0:T(8,128)(2,1)S(1)} collective-permute-done((bf16[64,768]{1,0:T(8,128)(2,1)S(1)}, bf16[64,768]{1,0:T(8,128)(2,1)S(1)}, u32[]{:S(2)}, u32[]{:S(2)}) %collective-permute-start.3) | collective-permute-done | bytes 98336 | tf_op jit(solution)/shard_map/ppermute | solution.py:206
  22.7 0.5 %collective-permute-start.14 = (bf16[64,768]{1,0:T(8,128)(2,1)S(1)}, bf16[64,768]{1,0:T(8,128)(2,1)S(1)}, u32[]{:S(2)}, u32[]{:S(2)}) collective-permute-start(bf16[64,768]{1,0:T(8,128)(2,1)S(1)} %collective-permute-done.13.refs_7_), channel_id=1, source_target_pairs={{0,1},{1,0},{2,3},{3,2},{4,5},{5,4},{6,7},{7,6},{8,9},{9,8},{10,11... | collective-permute-start | bytes 294920 | tf_op jit(solution)/shard_map/ppermute | solution.py:206
  23.2 0.1 collective-permute-start.2
  23.3 0.4 %collective-permute-start.4 = (bf16[64,768]{1,0:T(8,128)(2,1)S(1)}, bf16[64,768]{1,0:T(8,128)(2,1)S(1)}, u32[]{:S(2)}, u32[]{:S(2)}) collective-permute-start(bf16[64,768]{1,0:T(8,128)(2,1)S(1)} %collective-permute-done.3.refs_2_), channel_id=1, source_target_pairs={{0,1},{1,0},{2,3},{3,2},{4,5},{5,4},{6,7},{7,6},{8,9},{9,8},{10,11... | collective-permute-start | bytes 294920 | tf_op jit(solution)/shard_map/ppermute | solution.py:206
  23.7 0.1 collective-permute-start.6
  23.8 0.2 collective-permute-done.12.refs_6_
  24.0 0.2 collective-permute-start.8
  24.3 0.7 %shard_map.29 = (bf16[512,768]{1,0:T(8,128)(2,1)S(1)}, f32[1,512]{1,0:T(1,128)S(1)}) custom-call(bf16[64,768]{1,0:T(8,128)(2,1)S(1)} %get-tuple-element.17.refs_0_, bf16[64,768]{1,0:T(8,128)(2,1)S(1)} %collective-permute-done.1.refs_1_, bf16[64,768]{1,0:T(8,128)(2,1)S(1)} %collective-permute-done.3.refs_2_, ...), custom_call_target="tpu_custom_call" | custom-call | flops 402653184 | bytes 1572864 | tf_op jit(solution)/shard_map/pallas_call | solution.py:130
  25.0 0.1 collective-permute-done.6.refs_3_
  25.1 0.3 collective-permute-done.8.refs_4_
  25.3 0.7 %shard_map.30 = f32[8,128]{1,0:T(8,128)S(1)} custom-call(s32[1]{0:T(128)} %bitcast.me_ref, bf16[64,768]{1,0:T(8,128)(2,1)S(1)} %collective-permute-done.refs_0_, bf16[64,768]{1,0:T(8,128)(2,1)S(1)} %collective-permute-done.2.refs_1_, bf16[64,768]{1,0:T(8,128)(2,1)S(1)} %collective-permute-done.4.refs_2_, bf16[64,768]{1,0:T(8,128)(2,1)S(1)} %collective-permute-done.6.refs_3_, ...), custom_call_target="tpu_custom_call" | custom-call | tf_op jit(solution)/shard_map/pallas_call | solution.py:160
  26.0 10.2 %all_to_all.11 = f32[8,1,128]{2,1,0:T(1,128)S(1)} all-to-all(f32[8,1,128]{2,1,0:T(1,128)S(1)} %bitcast.5), channel_id=1, replica_groups=mesh['groups'=2,'blk'=8,'pair'=2] {'blk'}, dimensions={0} | all-to-all | bytes 8192 | tf_op jit(solution)/shard_map/all_to_all | solution.py:220
  36.2 0.7 %shard_map.31 = f32[256]{0:T(256)} custom-call(f32[8,128]{1,0:T(8,128)S(1)} %bitcast.6, bf16[64,256]{1,0:T(8,128)(2,1)S(1)} %get-tuple-element.27.ranks_ref, s32[1,256]{1,0:T(1,128)S(1)} %get-tuple-element.28.ids_ref), custom_call_target="tpu_custom_call" | custom-call | tf_op jit(solution)/shard_map/pallas_call | solution.py:188
  (11 shorter events, 0.0 us)
Async XLA Ops:
  1.6 9.5 %collective-permute-start.1 = (bf16[64,768]{1,0:T(8,128)(2,1)S(1)}, bf16[64,768]{1,0:T(8,128)(2,1)S(1)}, u32[]{:S(2)}, u32[]{:S(2)}) collective-permute-start(bf16[64,768]{1,0:T(8,128)(2,1)S(1)} %get-tuple-element.18), channel_id=1, source_target_pairs={{0,12},{2,14},{4,8},{6,10},{8,4},{10,6},{12,0},{14,2},{1,13},{3,15... | collective-permute-start | bytes 294920 | tf_op jit(solution)/shard_map/ppermute | solution.py:206
  6.7 7.4 %collective-permute-start.11 = (bf16[64,768]{1,0:T(8,128)(2,1)S(1)}, bf16[64,768]{1,0:T(8,128)(2,1)S(1)}, u32[]{:S(2)}, u32[]{:S(2)}) collective-permute-start(bf16[64,768]{1,0:T(8,128)(2,1)S(1)} %get-tuple-element.23), channel_id=1, source_target_pairs={{0,4},{2,6},{4,0},{6,2},{8,12},{10,14},{12,8},{14,10},{1,5},{3,7},... | collective-permute-start | bytes 294920 | tf_op jit(solution)/shard_map/ppermute | solution.py:206
  6.7 11.6 %collective-permute-start.13 = (bf16[64,768]{1,0:T(8,128)(2,1)S(1)}, bf16[64,768]{1,0:T(8,128)(2,1)S(1)}, u32[]{:S(2)}, u32[]{:S(2)}) collective-permute-start(bf16[64,768]{1,0:T(8,128)(2,1)S(1)} %get-tuple-element.24), channel_id=1, source_target_pairs={{0,8},{2,10},{4,12},{6,14},{8,0},{10,2},{12,4},{14,6},{1,9},{3,11}... | collective-permute-start | bytes 294920 | tf_op jit(solution)/shard_map/ppermute | solution.py:206
  7.3 11.0 %collective-permute-start.9 = (bf16[64,768]{1,0:T(8,128)(2,1)S(1)}, bf16[64,768]{1,0:T(8,128)(2,1)S(1)}, u32[]{:S(2)}, u32[]{:S(2)}) collective-permute-start(bf16[64,768]{1,0:T(8,128)(2,1)S(1)} %get-tuple-element.22), channel_id=1, source_target_pairs={{0,2},{2,0},{4,6},{6,4},{8,10},{10,8},{12,14},{14,12},{1,3},{3,1},... | collective-permute-start | bytes 294920 | tf_op jit(solution)/shard_map/ppermute | solution.py:206
  8.9 13.8 %collective-permute-start.3 = (bf16[64,768]{1,0:T(8,128)(2,1)S(1)}, bf16[64,768]{1,0:T(8,128)(2,1)S(1)}, u32[]{:S(2)}, u32[]{:S(2)}) collective-permute-start(bf16[64,768]{1,0:T(8,128)(2,1)S(1)} %get-tuple-element.19), channel_id=1, source_target_pairs={{0,10},{2,8},{4,14},{6,12},{8,2},{10,0},{12,6},{14,4},{1,11},{3,9}... | collective-permute-start | bytes 294920 | tf_op jit(solution)/shard_map/ppermute | solution.py:206
  11.1 11.7 %collective-permute-start.5 = (bf16[64,768]{1,0:T(8,128)(2,1)S(1)}, bf16[64,768]{1,0:T(8,128)(2,1)S(1)}, u32[]{:S(2)}, u32[]{:S(2)}) collective-permute-start(bf16[64,768]{1,0:T(8,128)(2,1)S(1)} %get-tuple-element.20), channel_id=1, source_target_pairs={{0,6},{2,4},{4,2},{6,0},{8,14},{10,12},{12,10},{14,8},{1,7},{3,5},... | collective-permute-start | bytes 294920 | tf_op jit(solution)/shard_map/ppermute | solution.py:206
  14.0 9.2 %collective-permute-start.7 = (bf16[64,768]{1,0:T(8,128)(2,1)S(1)}, bf16[64,768]{1,0:T(8,128)(2,1)S(1)}, u32[]{:S(2)}, u32[]{:S(2)}) collective-permute-start(bf16[64,768]{1,0:T(8,128)(2,1)S(1)} %get-tuple-element.21), channel_id=1, source_target_pairs={{0,14},{2,12},{4,10},{6,8},{8,6},{10,4},{12,2},{14,0},{1,15},{3,13... | collective-permute-start | bytes 294920 | tf_op jit(solution)/shard_map/ppermute | solution.py:206
  18.3 5.0 %collective-permute-start = (bf16[64,768]{1,0:T(8,128)(2,1)S(1)}, bf16[64,768]{1,0:T(8,128)(2,1)S(1)}, u32[]{:S(2)}, u32[]{:S(2)}) collective-permute-start(bf16[64,768]{1,0:T(8,128)(2,1)S(1)} %get-tuple-element.17.refs_0_), channel_id=1, source_target_pairs={{0,1},{1,0},{2,3},{3,2},{4,5},{5,4},{6,7},{7,6},{8,9},{9,8},{10,11... | collective-permute-start | bytes 294920 | tf_op jit(solution)/shard_map/ppermute | solution.py:206
  18.3 5.5 %collective-permute-start.10 = (bf16[64,768]{1,0:T(8,128)(2,1)S(1)}, bf16[64,768]{1,0:T(8,128)(2,1)S(1)}, u32[]{:S(2)}, u32[]{:S(2)}) collective-permute-start(bf16[64,768]{1,0:T(8,128)(2,1)S(1)} %collective-permute-done.9.refs_5_), channel_id=1, source_target_pairs={{0,1},{1,0},{2,3},{3,2},{4,5},{5,4},{6,7},{7,6},{8,9},{9,8},{10,11... | collective-permute-start | bytes 294920 | tf_op jit(solution)/shard_map/ppermute | solution.py:206
  22.7 1.3 %collective-permute-start.12 = (bf16[64,768]{1,0:T(8,128)(2,1)S(1)}, bf16[64,768]{1,0:T(8,128)(2,1)S(1)}, u32[]{:S(2)}, u32[]{:S(2)}) collective-permute-start(bf16[64,768]{1,0:T(8,128)(2,1)S(1)} %collective-permute-done.11.refs_6_), channel_id=1, source_target_pairs={{0,1},{1,0},{2,3},{3,2},{4,5},{5,4},{6,7},{7,6},{8,9},{9,8},{10,11... | collective-permute-start | bytes 294920 | tf_op jit(solution)/shard_map/ppermute | solution.py:206
  22.7 2.2 %collective-permute-start.14 = (bf16[64,768]{1,0:T(8,128)(2,1)S(1)}, bf16[64,768]{1,0:T(8,128)(2,1)S(1)}, u32[]{:S(2)}, u32[]{:S(2)}) collective-permute-start(bf16[64,768]{1,0:T(8,128)(2,1)S(1)} %collective-permute-done.13.refs_7_), channel_id=1, source_target_pairs={{0,1},{1,0},{2,3},{3,2},{4,5},{5,4},{6,7},{7,6},{8,9},{9,8},{10,11... | collective-permute-start | bytes 294920 | tf_op jit(solution)/shard_map/ppermute | solution.py:206
  23.2 1.7 %collective-permute-start.2 = (bf16[64,768]{1,0:T(8,128)(2,1)S(1)}, bf16[64,768]{1,0:T(8,128)(2,1)S(1)}, u32[]{:S(2)}, u32[]{:S(2)}) collective-permute-start(bf16[64,768]{1,0:T(8,128)(2,1)S(1)} %collective-permute-done.1.refs_1_), channel_id=1, source_target_pairs={{0,1},{1,0},{2,3},{3,2},{4,5},{5,4},{6,7},{7,6},{8,9},{9,8},{10,11... | collective-permute-start | bytes 294920 | tf_op jit(solution)/shard_map/ppermute | solution.py:206
  23.3 1.6 %collective-permute-start.4 = (bf16[64,768]{1,0:T(8,128)(2,1)S(1)}, bf16[64,768]{1,0:T(8,128)(2,1)S(1)}, u32[]{:S(2)}, u32[]{:S(2)}) collective-permute-start(bf16[64,768]{1,0:T(8,128)(2,1)S(1)} %collective-permute-done.3.refs_2_), channel_id=1, source_target_pairs={{0,1},{1,0},{2,3},{3,2},{4,5},{5,4},{6,7},{7,6},{8,9},{9,8},{10,11... | collective-permute-start | bytes 294920 | tf_op jit(solution)/shard_map/ppermute | solution.py:206
  23.7 1.3 %collective-permute-start.6 = (bf16[64,768]{1,0:T(8,128)(2,1)S(1)}, bf16[64,768]{1,0:T(8,128)(2,1)S(1)}, u32[]{:S(2)}, u32[]{:S(2)}) collective-permute-start(bf16[64,768]{1,0:T(8,128)(2,1)S(1)} %collective-permute-done.5.refs_3_), channel_id=1, source_target_pairs={{0,1},{1,0},{2,3},{3,2},{4,5},{5,4},{6,7},{7,6},{8,9},{9,8},{10,11... | collective-permute-start | bytes 294920 | tf_op jit(solution)/shard_map/ppermute | solution.py:206
  24.0 1.3 %collective-permute-start.8 = (bf16[64,768]{1,0:T(8,128)(2,1)S(1)}, bf16[64,768]{1,0:T(8,128)(2,1)S(1)}, u32[]{:S(2)}, u32[]{:S(2)}) collective-permute-start(bf16[64,768]{1,0:T(8,128)(2,1)S(1)} %collective-permute-done.7.refs_4_), channel_id=1, source_target_pairs={{0,1},{1,0},{2,3},{3,2},{4,5},{5,4},{6,7},{7,6},{8,9},{9,8},{10,11... | collective-permute-start | bytes 294920 | tf_op jit(solution)/shard_map/ppermute | solution.py:206

commit v8 on v7

--- a/solution.py
+++ b/solution.py
@@ -110,7 +110,7 @@
         if own_block:
             row = lax.broadcasted_iota(jnp.int32, powers.shape, 0) + k * capacity
             powers = jnp.where(row == lax.broadcasted_iota(jnp.int32, powers.shape, 1), 0.0, powers)
-        living = block_ref[0:1, 0:1].astype(jnp.float32) < EMPTY_ABOVE
+        living = block_ref[0:16, 0:128].astype(jnp.float32)[0:1, 0:1] < EMPTY_ABOVE
         total = total + jnp.where(living, jnp.sum(powers, axis=0, keepdims=True), 0.0)
     return total
 

time: 37.1 us -> 37.1 us (level)
  no operation moved by 1% of the time
where the time goes in v8:
time: 37.1 us; the launch traced here: 36.9 us
  starting transfers between devices  16 us (43%)
  blocking collectives  10.2 us (27%)
  waiting for transfers between devices  7.05 us (19%)
  Pallas kernels  3.62 us (10%)
    ppermute x15, starting transfers between devices, swap(): return lax.ppermute(block, axis, [(i, i ^ step) for i in range(size)])  16 us
    all_to_all x1, blocking collectives, direct_shards(): lax.all_to_all(scores, 'blk', split_axis=0, concat_axis=0, tiled=True)  10.2 us
    ppermute x15, waiting for transfers between devices, swap(): return lax.ppermute(block, axis, [(i, i ^ step) for i in range(size)])  7.05 us
    pallas_call x1, Pallas kernels, prepare(): pl.pallas_call(functools.partial(prepare_kernel, owners, capacity), out_s...  1.55 us
  transfers between devices with their start and end apart: 15, of which 5 were waited for; matrix products, arithmetic and copies ran while one was open for 0% of the time, Pallas kernels for 2%

profile of v8, /device:TPU:0, one launch (start us, length us, event | category | flops | bytes accessed | tf_op | source)
XLA Modules:
  0.0 36.9 jit_solution(17451754012170013891)
XLA Ops:
  0.0 1.5 %shard_map.28 = (bf16[64,768]{1,0:T(8,128)(2,1)S(1)}, bf16[64,768]{1,0:T(8,128)(2,1)S(1)}, bf16[64,768]{1,0:T(8,128)(2,1)S(1)}, bf16[64,768]{1,0:T(8,128)(2,1)S(...) custom-call(s32[1]{0:T(128)} %bitcast.me_ref, ...), custom_call_target="tpu_custom_call" | custom-call | tf_op jit(solution)/shard_map/pallas_call | solution.py:79
  1.6 5.1 %collective-permute-start.1 = (bf16[64,768]{1,0:T(8,128)(2,1)S(1)}, bf16[64,768]{1,0:T(8,128)(2,1)S(1)}, u32[]{:S(2)}, u32[]{:S(2)}) collective-permute-start(bf16[64,768]{1,0:T(8,128)(2,1)S(1)} %get-tuple-element.18), channel_id=1, source_target_pairs={{0,12},{2,14},{4,8},{6,10},{8,4},{10,6},{12,0},{14,2},{1,13},{3,15... | collective-permute-start | bytes 294920 | tf_op jit(solution)/shard_map/ppermute | solution.py:206
  6.7 0.0 collective-permute-start.11
  6.7 0.6 %collective-permute-start.13 = (bf16[64,768]{1,0:T(8,128)(2,1)S(1)}, bf16[64,768]{1,0:T(8,128)(2,1)S(1)}, u32[]{:S(2)}, u32[]{:S(2)}) collective-permute-start(bf16[64,768]{1,0:T(8,128)(2,1)S(1)} %get-tuple-element.24), channel_id=1, source_target_pairs={{0,8},{2,10},{4,12},{6,14},{8,0},{10,2},{12,4},{14,6},{1,9},{3,11}... | collective-permute-start | bytes 294920 | tf_op jit(solution)/shard_map/ppermute | solution.py:206
  7.3 1.6 %collective-permute-start.9 = (bf16[64,768]{1,0:T(8,128)(2,1)S(1)}, bf16[64,768]{1,0:T(8,128)(2,1)S(1)}, u32[]{:S(2)}, u32[]{:S(2)}) collective-permute-start(bf16[64,768]{1,0:T(8,128)(2,1)S(1)} %get-tuple-element.22), channel_id=1, source_target_pairs={{0,2},{2,0},{4,6},{6,4},{8,10},{10,8},{12,14},{14,12},{1,3},{3,1},... | collective-permute-start | bytes 294920 | tf_op jit(solution)/shard_map/ppermute | solution.py:206
  8.9 2.1 %collective-permute-start.3 = (bf16[64,768]{1,0:T(8,128)(2,1)S(1)}, bf16[64,768]{1,0:T(8,128)(2,1)S(1)}, u32[]{:S(2)}, u32[]{:S(2)}) collective-permute-start(bf16[64,768]{1,0:T(8,128)(2,1)S(1)} %get-tuple-element.19), channel_id=1, source_target_pairs={{0,10},{2,8},{4,14},{6,12},{8,2},{10,0},{12,6},{14,4},{1,11},{3,9}... | collective-permute-start | bytes 294920 | tf_op jit(solution)/shard_map/ppermute | solution.py:206
  11.1 0.0 collective-permute-done.1.refs_1_
  11.1 3.0 %collective-permute-start.5 = (bf16[64,768]{1,0:T(8,128)(2,1)S(1)}, bf16[64,768]{1,0:T(8,128)(2,1)S(1)}, u32[]{:S(2)}, u32[]{:S(2)}) collective-permute-start(bf16[64,768]{1,0:T(8,128)(2,1)S(1)} %get-tuple-element.20), channel_id=1, source_target_pairs={{0,6},{2,4},{4,2},{6,0},{8,14},{10,12},{12,10},{14,8},{1,7},{3,5},... | collective-permute-start | bytes 294920 | tf_op jit(solution)/shard_map/ppermute | solution.py:206
  14.0 1.7 %collective-permute-start.7 = (bf16[64,768]{1,0:T(8,128)(2,1)S(1)}, bf16[64,768]{1,0:T(8,128)(2,1)S(1)}, u32[]{:S(2)}, u32[]{:S(2)}) collective-permute-start(bf16[64,768]{1,0:T(8,128)(2,1)S(1)} %get-tuple-element.21), channel_id=1, source_target_pairs={{0,14},{2,12},{4,10},{6,8},{8,6},{10,4},{12,2},{14,0},{1,15},{3,13... | collective-permute-start | bytes 294920 | tf_op jit(solution)/shard_map/ppermute | solution.py:206
  15.7 2.5 %collective-permute-done.13.refs_7_ = bf16[64,768]{1,0:T(8,128)(2,1)S(1)} collective-permute-done((bf16[64,768]{1,0:T(8,128)(2,1)S(1)}, bf16[64,768]{1,0:T(8,128)(2,1)S(1)}, u32[]{:S(2)}, u32[]{:S(2)}) %collective-permute-start.13) | collective-permute-done | bytes 98336 | tf_op jit(solution)/shard_map/ppermute | solution.py:206
  18.3 0.5 %collective-permute-start.10 = (bf16[64,768]{1,0:T(8,128)(2,1)S(1)}, bf16[64,768]{1,0:T(8,128)(2,1)S(1)}, u32[]{:S(2)}, u32[]{:S(2)}) collective-permute-start(bf16[64,768]{1,0:T(8,128)(2,1)S(1)} %collective-permute-done.9.refs_5_), channel_id=1, source_target_pairs={{0,1},{1,0},{2,3},{3,2},{4,5},{5,4},{6,7},{7,6},{8,9},{9,8},{10,11... | collective-permute-start | bytes 294920 | tf_op jit(solution)/shard_map/ppermute | solution.py:206
  18.8 3.9 %collective-permute-done.3.refs_2_ = bf16[64,768]{1,0:T(8,128)(2,1)S(1)} collective-permute-done((bf16[64,768]{1,0:T(8,128)(2,1)S(1)}, bf16[64,768]{1,0:T(8,128)(2,1)S(1)}, u32[]{:S(2)}, u32[]{:S(2)}) %collective-permute-start.3) | collective-permute-done | bytes 98336 | tf_op jit(solution)/shard_map/ppermute | solution.py:206
  22.7 0.5 %collective-permute-start.14 = (bf16[64,768]{1,0:T(8,128)(2,1)S(1)}, bf16[64,768]{1,0:T(8,128)(2,1)S(1)}, u32[]{:S(2)}, u32[]{:S(2)}) collective-permute-start(bf16[64,768]{1,0:T(8,128)(2,1)S(1)} %collective-permute-done.13.refs_7_), channel_id=1, source_target_pairs={{0,1},{1,0},{2,3},{3,2},{4,5},{5,4},{6,7},{7,6},{8,9},{9,8},{10,11... | collective-permute-start | bytes 294920 | tf_op jit(solution)/shard_map/ppermute | solution.py:206
  23.2 0.1 collective-permute-start.2
  23.3 0.4 %collective-permute-start.4 = (bf16[64,768]{1,0:T(8,128)(2,1)S(1)}, bf16[64,768]{1,0:T(8,128)(2,1)S(1)}, u32[]{:S(2)}, u32[]{:S(2)}) collective-permute-start(bf16[64,768]{1,0:T(8,128)(2,1)S(1)} %collective-permute-done.3.refs_2_), channel_id=1, source_target_pairs={{0,1},{1,0},{2,3},{3,2},{4,5},{5,4},{6,7},{7,6},{8,9},{9,8},{10,11... | collective-permute-start | bytes 294920 | tf_op jit(solution)/shard_map/ppermute | solution.py:206
  23.7 0.1 collective-permute-start.6
  23.8 0.2 collective-permute-done.12.refs_6_
  24.0 0.2 collective-permute-start.8
  24.3 0.7 %shard_map.29 = (bf16[512,768]{1,0:T(8,128)(2,1)S(1)}, f32[1,512]{1,0:T(1,128)S(1)}) custom-call(bf16[64,768]{1,0:T(8,128)(2,1)S(1)} %get-tuple-element.17.refs_0_, bf16[64,768]{1,0:T(8,128)(2,1)S(1)} %collective-permute-done.1.refs_1_, bf16[64,768]{1,0:T(8,128)(2,1)S(1)} %collective-permute-done.3.refs_2_, ...), custom_call_target="tpu_custom_call" | custom-call | flops 402653184 | bytes 1572864 | tf_op jit(solution)/shard_map/pallas_call | solution.py:130
  25.0 0.1 collective-permute-done.6.refs_3_
  25.1 0.3 collective-permute-done.8.refs_4_
  25.3 0.7 %shard_map.30 = f32[8,128]{1,0:T(8,128)S(1)} custom-call(s32[1]{0:T(128)} %bitcast.me_ref, bf16[64,768]{1,0:T(8,128)(2,1)S(1)} %collective-permute-done.refs_0_, bf16[64,768]{1,0:T(8,128)(2,1)S(1)} %collective-permute-done.2.refs_1_, bf16[64,768]{1,0:T(8,128)(2,1)S(1)} %collective-permute-done.4.refs_2_, bf16[64,768]{1,0:T(8,128)(2,1)S(1)} %collective-permute-done.6.refs_3_, ...), custom_call_target="tpu_custom_call" | custom-call | tf_op jit(solution)/shard_map/pallas_call | solution.py:160
  26.0 10.2 %all_to_all.11 = f32[8,1,128]{2,1,0:T(1,128)S(1)} all-to-all(f32[8,1,128]{2,1,0:T(1,128)S(1)} %bitcast.5), channel_id=1, replica_groups=mesh['groups'=2,'blk'=8,'pair'=2] {'blk'}, dimensions={0} | all-to-all | bytes 8192 | tf_op jit(solution)/shard_map/all_to_all | solution.py:220
  36.2 0.7 %shard_map.31 = f32[256]{0:T(256)} custom-call(f32[8,128]{1,0:T(8,128)S(1)} %bitcast.6, bf16[64,256]{1,0:T(8,128)(2,1)S(1)} %get-tuple-element.27.ranks_ref, s32[1,256]{1,0:T(1,128)S(1)} %get-tuple-element.28.ids_ref), custom_call_target="tpu_custom_call" | custom-call | tf_op jit(solution)/shard_map/pallas_call | solution.py:188
  (11 shorter events, 0.0 us)
Async XLA Ops:
  1.6 9.5 %collective-permute-start.1 = (bf16[64,768]{1,0:T(8,128)(2,1)S(1)}, bf16[64,768]{1,0:T(8,128)(2,1)S(1)}, u32[]{:S(2)}, u32[]{:S(2)}) collective-permute-start(bf16[64,768]{1,0:T(8,128)(2,1)S(1)} %get-tuple-element.18), channel_id=1, source_target_pairs={{0,12},{2,14},{4,8},{6,10},{8,4},{10,6},{12,0},{14,2},{1,13},{3,15... | collective-permute-start | bytes 294920 | tf_op jit(solution)/shard_map/ppermute | solution.py:206
  6.7 7.4 %collective-permute-start.11 = (bf16[64,768]{1,0:T(8,128)(2,1)S(1)}, bf16[64,768]{1,0:T(8,128)(2,1)S(1)}, u32[]{:S(2)}, u32[]{:S(2)}) collective-permute-start(bf16[64,768]{1,0:T(8,128)(2,1)S(1)} %get-tuple-element.23), channel_id=1, source_target_pairs={{0,4},{2,6},{4,0},{6,2},{8,12},{10,14},{12,8},{14,10},{1,5},{3,7},... | collective-permute-start | bytes 294920 | tf_op jit(solution)/shard_map/ppermute | solution.py:206
  6.7 11.6 %collective-permute-start.13 = (bf16[64,768]{1,0:T(8,128)(2,1)S(1)}, bf16[64,768]{1,0:T(8,128)(2,1)S(1)}, u32[]{:S(2)}, u32[]{:S(2)}) collective-permute-start(bf16[64,768]{1,0:T(8,128)(2,1)S(1)} %get-tuple-element.24), channel_id=1, source_target_pairs={{0,8},{2,10},{4,12},{6,14},{8,0},{10,2},{12,4},{14,6},{1,9},{3,11}... | collective-permute-start | bytes 294920 | tf_op jit(solution)/shard_map/ppermute | solution.py:206
  7.3 11.0 %collective-permute-start.9 = (bf16[64,768]{1,0:T(8,128)(2,1)S(1)}, bf16[64,768]{1,0:T(8,128)(2,1)S(1)}, u32[]{:S(2)}, u32[]{:S(2)}) collective-permute-start(bf16[64,768]{1,0:T(8,128)(2,1)S(1)} %get-tuple-element.22), channel_id=1, source_target_pairs={{0,2},{2,0},{4,6},{6,4},{8,10},{10,8},{12,14},{14,12},{1,3},{3,1},... | collective-permute-start | bytes 294920 | tf_op jit(solution)/shard_map/ppermute | solution.py:206
  8.9 13.8 %collective-permute-start.3 = (bf16[64,768]{1,0:T(8,128)(2,1)S(1)}, bf16[64,768]{1,0:T(8,128)(2,1)S(1)}, u32[]{:S(2)}, u32[]{:S(2)}) collective-permute-start(bf16[64,768]{1,0:T(8,128)(2,1)S(1)} %get-tuple-element.19), channel_id=1, source_target_pairs={{0,10},{2,8},{4,14},{6,12},{8,2},{10,0},{12,6},{14,4},{1,11},{3,9}... | collective-permute-start | bytes 294920 | tf_op jit(solution)/shard_map/ppermute | solution.py:206
  11.1 11.7 %collective-permute-start.5 = (bf16[64,768]{1,0:T(8,128)(2,1)S(1)}, bf16[64,768]{1,0:T(8,128)(2,1)S(1)}, u32[]{:S(2)}, u32[]{:S(2)}) collective-permute-start(bf16[64,768]{1,0:T(8,128)(2,1)S(1)} %get-tuple-element.20), channel_id=1, source_target_pairs={{0,6},{2,4},{4,2},{6,0},{8,14},{10,12},{12,10},{14,8},{1,7},{3,5},... | collective-permute-start | bytes 294920 | tf_op jit(solution)/shard_map/ppermute | solution.py:206
  14.0 9.2 %collective-permute-start.7 = (bf16[64,768]{1,0:T(8,128)(2,1)S(1)}, bf16[64,768]{1,0:T(8,128)(2,1)S(1)}, u32[]{:S(2)}, u32[]{:S(2)}) collective-permute-start(bf16[64,768]{1,0:T(8,128)(2,1)S(1)} %get-tuple-element.21), channel_id=1, source_target_pairs={{0,14},{2,12},{4,10},{6,8},{8,6},{10,4},{12,2},{14,0},{1,15},{3,13... | collective-permute-start | bytes 294920 | tf_op jit(solution)/shard_map/ppermute | solution.py:206
  18.3 5.0 %collective-permute-start = (bf16[64,768]{1,0:T(8,128)(2,1)S(1)}, bf16[64,768]{1,0:T(8,128)(2,1)S(1)}, u32[]{:S(2)}, u32[]{:S(2)}) collective-permute-start(bf16[64,768]{1,0:T(8,128)(2,1)S(1)} %get-tuple-element.17.refs_0_), channel_id=1, source_target_pairs={{0,1},{1,0},{2,3},{3,2},{4,5},{5,4},{6,7},{7,6},{8,9},{9,8},{10,11... | collective-permute-start | bytes 294920 | tf_op jit(solution)/shard_map/ppermute | solution.py:206
  18.3 5.5 %collective-permute-start.10 = (bf16[64,768]{1,0:T(8,128)(2,1)S(1)}, bf16[64,768]{1,0:T(8,128)(2,1)S(1)}, u32[]{:S(2)}, u32[]{:S(2)}) collective-permute-start(bf16[64,768]{1,0:T(8,128)(2,1)S(1)} %collective-permute-done.9.refs_5_), channel_id=1, source_target_pairs={{0,1},{1,0},{2,3},{3,2},{4,5},{5,4},{6,7},{7,6},{8,9},{9,8},{10,11... | collective-permute-start | bytes 294920 | tf_op jit(solution)/shard_map/ppermute | solution.py:206
  22.7 1.3 %collective-permute-start.12 = (bf16[64,768]{1,0:T(8,128)(2,1)S(1)}, bf16[64,768]{1,0:T(8,128)(2,1)S(1)}, u32[]{:S(2)}, u32[]{:S(2)}) collective-permute-start(bf16[64,768]{1,0:T(8,128)(2,1)S(1)} %collective-permute-done.11.refs_6_), channel_id=1, source_target_pairs={{0,1},{1,0},{2,3},{3,2},{4,5},{5,4},{6,7},{7,6},{8,9},{9,8},{10,11... | collective-permute-start | bytes 294920 | tf_op jit(solution)/shard_map/ppermute | solution.py:206
  22.7 2.2 %collective-permute-start.14 = (bf16[64,768]{1,0:T(8,128)(2,1)S(1)}, bf16[64,768]{1,0:T(8,128)(2,1)S(1)}, u32[]{:S(2)}, u32[]{:S(2)}) collective-permute-start(bf16[64,768]{1,0:T(8,128)(2,1)S(1)} %collective-permute-done.13.refs_7_), channel_id=1, source_target_pairs={{0,1},{1,0},{2,3},{3,2},{4,5},{5,4},{6,7},{7,6},{8,9},{9,8},{10,11... | collective-permute-start | bytes 294920 | tf_op jit(solution)/shard_map/ppermute | solution.py:206
  23.2 1.7 %collective-permute-start.2 = (bf16[64,768]{1,0:T(8,128)(2,1)S(1)}, bf16[64,768]{1,0:T(8,128)(2,1)S(1)}, u32[]{:S(2)}, u32[]{:S(2)}) collective-permute-start(bf16[64,768]{1,0:T(8,128)(2,1)S(1)} %collective-permute-done.1.refs_1_), channel_id=1, source_target_pairs={{0,1},{1,0},{2,3},{3,2},{4,5},{5,4},{6,7},{7,6},{8,9},{9,8},{10,11... | collective-permute-start | bytes 294920 | tf_op jit(solution)/shard_map/ppermute | solution.py:206
  23.3 1.6 %collective-permute-start.4 = (bf16[64,768]{1,0:T(8,128)(2,1)S(1)}, bf16[64,768]{1,0:T(8,128)(2,1)S(1)}, u32[]{:S(2)}, u32[]{:S(2)}) collective-permute-start(bf16[64,768]{1,0:T(8,128)(2,1)S(1)} %collective-permute-done.3.refs_2_), channel_id=1, source_target_pairs={{0,1},{1,0},{2,3},{3,2},{4,5},{5,4},{6,7},{7,6},{8,9},{9,8},{10,11... | collective-permute-start | bytes 294920 | tf_op jit(solution)/shard_map/ppermute | solution.py:206
  23.7 1.3 %collective-permute-start.6 = (bf16[64,768]{1,0:T(8,128)(2,1)S(1)}, bf16[64,768]{1,0:T(8,128)(2,1)S(1)}, u32[]{:S(2)}, u32[]{:S(2)}) collective-permute-start(bf16[64,768]{1,0:T(8,128)(2,1)S(1)} %collective-permute-done.5.refs_3_), channel_id=1, source_target_pairs={{0,1},{1,0},{2,3},{3,2},{4,5},{5,4},{6,7},{7,6},{8,9},{9,8},{10,11... | collective-permute-start | bytes 294920 | tf_op jit(solution)/shard_map/ppermute | solution.py:206
  24.0 1.3 %collective-permute-start.8 = (bf16[64,768]{1,0:T(8,128)(2,1)S(1)}, bf16[64,768]{1,0:T(8,128)(2,1)S(1)}, u32[]{:S(2)}, u32[]{:S(2)}) collective-permute-start(bf16[64,768]{1,0:T(8,128)(2,1)S(1)} %collective-permute-done.7.refs_4_), channel_id=1, source_target_pairs={{0,1},{1,0},{2,3},{3,2},{4,5},{5,4},{6,7},{7,6},{8,9},{9,8},{10,11... | collective-permute-start | bytes 294920 | tf_op jit(solution)/shard_map/ppermute | solution.py:206

commit v9 on v8

--- a/solution.py
+++ b/solution.py
@@ -196,7 +196,7 @@
 
 def steps_of(owners):
     if owners == 8:
-        return (0, 6, 5, 3, 7, 1, 2, 4)
+        return (0, 6, 5, 1, 7, 3, 2, 4)
     return tuple(range(owners))
 
 

time: 37.1 us -> 37.1 us (level)
  transfers between devices with their start and end apart: 15 -> 15, of which waited for: 5 -> 6; matrix products, arithmetic and copies ran while one was open for 0% -> 0% of each run, Pallas kernels for 2% -> 2%
where the time goes in v9:
time: 37.1 us; the launch traced here: 36.9 us
  starting transfers between devices  16 us (43%)
  blocking collectives  10.2 us (27%)
  waiting for transfers between devices  7.04 us (19%)
  Pallas kernels  3.62 us (10%)
    ppermute x15, starting transfers between devices, swap(): return lax.ppermute(block, axis, [(i, i ^ step) for i in range(size)])  16 us
    all_to_all x1, blocking collectives, direct_shards(): lax.all_to_all(scores, 'blk', split_axis=0, concat_axis=0, tiled=True)  10.2 us
    ppermute x15, waiting for transfers between devices, swap(): return lax.ppermute(block, axis, [(i, i ^ step) for i in range(size)])  7.04 us
    pallas_call x1, Pallas kernels, prepare(): pl.pallas_call(functools.partial(prepare_kernel, owners, capacity), out_s...  1.55 us
  transfers between devices with their start and end apart: 15, of which 6 were waited for; matrix products, arithmetic and copies ran while one was open for 0% of the time, Pallas kernels for 2%

profile of v9, /device:TPU:0, one launch (start us, length us, event | category | flops | bytes accessed | tf_op | source)
XLA Modules:
  0.0 36.9 jit_solution(3700462448143001483)
XLA Ops:
  0.0 1.5 %shard_map.28 = (bf16[64,768]{1,0:T(8,128)(2,1)S(1)}, bf16[64,768]{1,0:T(8,128)(2,1)S(1)}, bf16[64,768]{1,0:T(8,128)(2,1)S(1)}, bf16[64,768]{1,0:T(8,128)(2,1)S(...) custom-call(s32[1]{0:T(128)} %bitcast.me_ref, ...), custom_call_target="tpu_custom_call" | custom-call | tf_op jit(solution)/shard_map/pallas_call | solution.py:79
  1.6 5.1 %collective-permute-start.1 = (bf16[64,768]{1,0:T(8,128)(2,1)S(1)}, bf16[64,768]{1,0:T(8,128)(2,1)S(1)}, u32[]{:S(2)}, u32[]{:S(2)}) collective-permute-start(bf16[64,768]{1,0:T(8,128)(2,1)S(1)} %get-tuple-element.18), channel_id=1, source_target_pairs={{0,12},{2,14},{4,8},{6,10},{8,4},{10,6},{12,0},{14,2},{1,13},{3,15... | collective-permute-start | bytes 294920 | tf_op jit(solution)/shard_map/ppermute | solution.py:206
  6.7 0.6 %collective-permute-start.13 = (bf16[64,768]{1,0:T(8,128)(2,1)S(1)}, bf16[64,768]{1,0:T(8,128)(2,1)S(1)}, u32[]{:S(2)}, u32[]{:S(2)}) collective-permute-start(bf16[64,768]{1,0:T(8,128)(2,1)S(1)} %get-tuple-element.24), channel_id=1, source_target_pairs={{0,8},{2,10},{4,12},{6,14},{8,0},{10,2},{12,4},{14,6},{1,9},{3,11}... | collective-permute-start | bytes 294920 | tf_op jit(solution)/shard_map/ppermute | solution.py:206
  7.3 2.3 %collective-permute-start.9 = (bf16[64,768]{1,0:T(8,128)(2,1)S(1)}, bf16[64,768]{1,0:T(8,128)(2,1)S(1)}, u32[]{:S(2)}, u32[]{:S(2)}) collective-permute-start(bf16[64,768]{1,0:T(8,128)(2,1)S(1)} %get-tuple-element.22), channel_id=1, source_target_pairs={{0,6},{2,4},{4,2},{6,0},{8,14},{10,12},{12,10},{14,8},{1,7},{3,5},... | collective-permute-start | bytes 294920 | tf_op jit(solution)/shard_map/ppermute | solution.py:206
  9.6 2.9 %collective-permute-start.3 = (bf16[64,768]{1,0:T(8,128)(2,1)S(1)}, bf16[64,768]{1,0:T(8,128)(2,1)S(1)}, u32[]{:S(2)}, u32[]{:S(2)}) collective-permute-start(bf16[64,768]{1,0:T(8,128)(2,1)S(1)} %get-tuple-element.19), channel_id=1, source_target_pairs={{0,10},{2,8},{4,14},{6,12},{8,2},{10,0},{12,6},{14,4},{1,11},{3,9}... | collective-permute-start | bytes 294920 | tf_op jit(solution)/shard_map/ppermute | solution.py:206
  12.5 0.0 collective-permute-done.1.refs_1_
  12.5 1.5 %collective-permute-start.5 = (bf16[64,768]{1,0:T(8,128)(2,1)S(1)}, bf16[64,768]{1,0:T(8,128)(2,1)S(1)}, u32[]{:S(2)}, u32[]{:S(2)}) collective-permute-start(bf16[64,768]{1,0:T(8,128)(2,1)S(1)} %get-tuple-element.20), channel_id=1, source_target_pairs={{0,2},{2,0},{4,6},{6,4},{8,10},{10,8},{12,14},{14,12},{1,3},{3,1},... | collective-permute-start | bytes 294920 | tf_op jit(solution)/shard_map/ppermute | solution.py:206
  14.0 0.0 collective-permute-done.11.refs_6_
  14.0 2.2 %collective-permute-start.7 = (bf16[64,768]{1,0:T(8,128)(2,1)S(1)}, bf16[64,768]{1,0:T(8,128)(2,1)S(1)}, u32[]{:S(2)}, u32[]{:S(2)}) collective-permute-start(bf16[64,768]{1,0:T(8,128)(2,1)S(1)} %get-tuple-element.21), channel_id=1, source_target_pairs={{0,14},{2,12},{4,10},{6,8},{8,6},{10,4},{12,2},{14,0},{1,15},{3,13... | collective-permute-start | bytes 294920 | tf_op jit(solution)/shard_map/ppermute | solution.py:206
  16.2 0.1 collective-permute-done.13.refs_7_
  16.3 1.5 %collective-permute-done.9.refs_5_ = bf16[64,768]{1,0:T(8,128)(2,1)S(1)} collective-permute-done((bf16[64,768]{1,0:T(8,128)(2,1)S(1)}, bf16[64,768]{1,0:T(8,128)(2,1)S(1)}, u32[]{:S(2)}, u32[]{:S(2)}) %collective-permute-start.9) | collective-permute-done | bytes 98336 | tf_op jit(solution)/shard_map/ppermute | solution.py:206
  17.9 4.8 %collective-permute-done.3.refs_2_ = bf16[64,768]{1,0:T(8,128)(2,1)S(1)} collective-permute-done((bf16[64,768]{1,0:T(8,128)(2,1)S(1)}, bf16[64,768]{1,0:T(8,128)(2,1)S(1)}, u32[]{:S(2)}, u32[]{:S(2)}) %collective-permute-start.3) | collective-permute-done | bytes 98336 | tf_op jit(solution)/shard_map/ppermute | solution.py:206
  22.7 0.5 %collective-permute-start.14 = (bf16[64,768]{1,0:T(8,128)(2,1)S(1)}, bf16[64,768]{1,0:T(8,128)(2,1)S(1)}, u32[]{:S(2)}, u32[]{:S(2)}) collective-permute-start(bf16[64,768]{1,0:T(8,128)(2,1)S(1)} %collective-permute-done.13.refs_7_), channel_id=1, source_target_pairs={{0,1},{1,0},{2,3},{3,2},{4,5},{5,4},{6,7},{7,6},{8,9},{9,8},{10,11... | collective-permute-start | bytes 294920 | tf_op jit(solution)/shard_map/ppermute | solution.py:206
  23.2 0.1 collective-permute-start.2
  23.3 0.4 %collective-permute-start.4 = (bf16[64,768]{1,0:T(8,128)(2,1)S(1)}, bf16[64,768]{1,0:T(8,128)(2,1)S(1)}, u32[]{:S(2)}, u32[]{:S(2)}) collective-permute-start(bf16[64,768]{1,0:T(8,128)(2,1)S(1)} %collective-permute-done.3.refs_2_), channel_id=1, source_target_pairs={{0,1},{1,0},{2,3},{3,2},{4,5},{5,4},{6,7},{7,6},{8,9},{9,8},{10,11... | collective-permute-start | bytes 294920 | tf_op jit(solution)/shard_map/ppermute | solution.py:206
  23.7 0.1 collective-permute-start.6
  23.8 0.2 collective-permute-done.12.refs_6_
  24.0 0.2 collective-permute-start.8
  24.3 0.7 %shard_map.29 = (bf16[512,768]{1,0:T(8,128)(2,1)S(1)}, f32[1,512]{1,0:T(1,128)S(1)}) custom-call(bf16[64,768]{1,0:T(8,128)(2,1)S(1)} %get-tuple-element.17.refs_0_, bf16[64,768]{1,0:T(8,128)(2,1)S(1)} %collective-permute-done.1.refs_1_, bf16[64,768]{1,0:T(8,128)(2,1)S(1)} %collective-permute-done.3.refs_2_, ...), custom_call_target="tpu_custom_call" | custom-call | flops 402653184 | bytes 1572864 | tf_op jit(solution)/shard_map/pallas_call | solution.py:130
  25.0 0.1 collective-permute-done.6.refs_3_
  25.1 0.3 collective-permute-done.8.refs_4_
  25.3 0.7 %shard_map.30 = f32[8,128]{1,0:T(8,128)S(1)} custom-call(s32[1]{0:T(128)} %bitcast.me_ref, bf16[64,768]{1,0:T(8,128)(2,1)S(1)} %collective-permute-done.refs_0_, bf16[64,768]{1,0:T(8,128)(2,1)S(1)} %collective-permute-done.2.refs_1_, bf16[64,768]{1,0:T(8,128)(2,1)S(1)} %collective-permute-done.4.refs_2_, bf16[64,768]{1,0:T(8,128)(2,1)S(1)} %collective-permute-done.6.refs_3_, ...), custom_call_target="tpu_custom_call" | custom-call | tf_op jit(solution)/shard_map/pallas_call | solution.py:160
  26.0 10.2 %all_to_all.11 = f32[8,1,128]{2,1,0:T(1,128)S(1)} all-to-all(f32[8,1,128]{2,1,0:T(1,128)S(1)} %bitcast.5), channel_id=1, replica_groups=mesh['groups'=2,'blk'=8,'pair'=2] {'blk'}, dimensions={0} | all-to-all | bytes 8192 | tf_op jit(solution)/shard_map/all_to_all | solution.py:220
  36.2 0.7 %shard_map.31 = f32[256]{0:T(256)} custom-call(f32[8,128]{1,0:T(8,128)S(1)} %bitcast.6, bf16[64,256]{1,0:T(8,128)(2,1)S(1)} %get-tuple-element.27.ranks_ref, s32[1,256]{1,0:T(1,128)S(1)} %get-tuple-element.28.ids_ref), custom_call_target="tpu_custom_call" | custom-call | tf_op jit(solution)/shard_map/pallas_call | solution.py:188
  (11 shorter events, 0.0 us)
Async XLA Ops:
  1.6 11.0 %collective-permute-start.1 = (bf16[64,768]{1,0:T(8,128)(2,1)S(1)}, bf16[64,768]{1,0:T(8,128)(2,1)S(1)}, u32[]{:S(2)}, u32[]{:S(2)}) collective-permute-start(bf16[64,768]{1,0:T(8,128)(2,1)S(1)} %get-tuple-element.18), channel_id=1, source_target_pairs={{0,12},{2,14},{4,8},{6,10},{8,4},{10,6},{12,0},{14,2},{1,13},{3,15... | collective-permute-start | bytes 294920 | tf_op jit(solution)/shard_map/ppermute | solution.py:206
  6.7 7.4 %collective-permute-start.11 = (bf16[64,768]{1,0:T(8,128)(2,1)S(1)}, bf16[64,768]{1,0:T(8,128)(2,1)S(1)}, u32[]{:S(2)}, u32[]{:S(2)}) collective-permute-start(bf16[64,768]{1,0:T(8,128)(2,1)S(1)} %get-tuple-element.23), channel_id=1, source_target_pairs={{0,4},{2,6},{4,0},{6,2},{8,12},{10,14},{12,8},{14,10},{1,5},{3,7},... | collective-permute-start | bytes 294920 | tf_op jit(solution)/shard_map/ppermute | solution.py:206
  6.7 9.7 %collective-permute-start.13 = (bf16[64,768]{1,0:T(8,128)(2,1)S(1)}, bf16[64,768]{1,0:T(8,128)(2,1)S(1)}, u32[]{:S(2)}, u32[]{:S(2)}) collective-permute-start(bf16[64,768]{1,0:T(8,128)(2,1)S(1)} %get-tuple-element.24), channel_id=1, source_target_pairs={{0,8},{2,10},{4,12},{6,14},{8,0},{10,2},{12,4},{14,6},{1,9},{3,11}... | collective-permute-start | bytes 294920 | tf_op jit(solution)/shard_map/ppermute | solution.py:206
  7.3 10.6 %collective-permute-start.9 = (bf16[64,768]{1,0:T(8,128)(2,1)S(1)}, bf16[64,768]{1,0:T(8,128)(2,1)S(1)}, u32[]{:S(2)}, u32[]{:S(2)}) collective-permute-start(bf16[64,768]{1,0:T(8,128)(2,1)S(1)} %get-tuple-element.22), channel_id=1, source_target_pairs={{0,6},{2,4},{4,2},{6,0},{8,14},{10,12},{12,10},{14,8},{1,7},{3,5},... | collective-permute-start | bytes 294920 | tf_op jit(solution)/shard_map/ppermute | solution.py:206
  9.6 13.1 %collective-permute-start.3 = (bf16[64,768]{1,0:T(8,128)(2,1)S(1)}, bf16[64,768]{1,0:T(8,128)(2,1)S(1)}, u32[]{:S(2)}, u32[]{:S(2)}) collective-permute-start(bf16[64,768]{1,0:T(8,128)(2,1)S(1)} %get-tuple-element.19), channel_id=1, source_target_pairs={{0,10},{2,8},{4,14},{6,12},{8,2},{10,0},{12,6},{14,4},{1,11},{3,9}... | collective-permute-start | bytes 294920 | tf_op jit(solution)/shard_map/ppermute | solution.py:206
  12.5 10.2 %collective-permute-start.5 = (bf16[64,768]{1,0:T(8,128)(2,1)S(1)}, bf16[64,768]{1,0:T(8,128)(2,1)S(1)}, u32[]{:S(2)}, u32[]{:S(2)}) collective-permute-start(bf16[64,768]{1,0:T(8,128)(2,1)S(1)} %get-tuple-element.20), channel_id=1, source_target_pairs={{0,2},{2,0},{4,6},{6,4},{8,10},{10,8},{12,14},{14,12},{1,3},{3,1},... | collective-permute-start | bytes 294920 | tf_op jit(solution)/shard_map/ppermute | solution.py:206
  14.0 9.2 %collective-permute-start.7 = (bf16[64,768]{1,0:T(8,128)(2,1)S(1)}, bf16[64,768]{1,0:T(8,128)(2,1)S(1)}, u32[]{:S(2)}, u32[]{:S(2)}) collective-permute-start(bf16[64,768]{1,0:T(8,128)(2,1)S(1)} %get-tuple-element.21), channel_id=1, source_target_pairs={{0,14},{2,12},{4,10},{6,8},{8,6},{10,4},{12,2},{14,0},{1,15},{3,13... | collective-permute-start | bytes 294920 | tf_op jit(solution)/shard_map/ppermute | solution.py:206
  16.3 7.0 %collective-permute-start = (bf16[64,768]{1,0:T(8,128)(2,1)S(1)}, bf16[64,768]{1,0:T(8,128)(2,1)S(1)}, u32[]{:S(2)}, u32[]{:S(2)}) collective-permute-start(bf16[64,768]{1,0:T(8,128)(2,1)S(1)} %get-tuple-element.17.refs_0_), channel_id=1, source_target_pairs={{0,1},{1,0},{2,3},{3,2},{4,5},{5,4},{6,7},{7,6},{8,9},{9,8},{10,11... | collective-permute-start | bytes 294920 | tf_op jit(solution)/shard_map/ppermute | solution.py:206
  17.9 5.9 %collective-permute-start.10 = (bf16[64,768]{1,0:T(8,128)(2,1)S(1)}, bf16[64,768]{1,0:T(8,128)(2,1)S(1)}, u32[]{:S(2)}, u32[]{:S(2)}) collective-permute-start(bf16[64,768]{1,0:T(8,128)(2,1)S(1)} %collective-permute-done.9.refs_5_), channel_id=1, source_target_pairs={{0,1},{1,0},{2,3},{3,2},{4,5},{5,4},{6,7},{7,6},{8,9},{9,8},{10,11... | collective-permute-start | bytes 294920 | tf_op jit(solution)/shard_map/ppermute | solution.py:206
  22.7 1.3 %collective-permute-start.12 = (bf16[64,768]{1,0:T(8,128)(2,1)S(1)}, bf16[64,768]{1,0:T(8,128)(2,1)S(1)}, u32[]{:S(2)}, u32[]{:S(2)}) collective-permute-start(bf16[64,768]{1,0:T(8,128)(2,1)S(1)} %collective-permute-done.11.refs_6_), channel_id=1, source_target_pairs={{0,1},{1,0},{2,3},{3,2},{4,5},{5,4},{6,7},{7,6},{8,9},{9,8},{10,11... | collective-permute-start | bytes 294920 | tf_op jit(solution)/shard_map/ppermute | solution.py:206
  22.7 2.2 %collective-permute-start.14 = (bf16[64,768]{1,0:T(8,128)(2,1)S(1)}, bf16[64,768]{1,0:T(8,128)(2,1)S(1)}, u32[]{:S(2)}, u32[]{:S(2)}) collective-permute-start(bf16[64,768]{1,0:T(8,128)(2,1)S(1)} %collective-permute-done.13.refs_7_), channel_id=1, source_target_pairs={{0,1},{1,0},{2,3},{3,2},{4,5},{5,4},{6,7},{7,6},{8,9},{9,8},{10,11... | collective-permute-start | bytes 294920 | tf_op jit(solution)/shard_map/ppermute | solution.py:206
  23.2 1.7 %collective-permute-start.2 = (bf16[64,768]{1,0:T(8,128)(2,1)S(1)}, bf16[64,768]{1,0:T(8,128)(2,1)S(1)}, u32[]{:S(2)}, u32[]{:S(2)}) collective-permute-start(bf16[64,768]{1,0:T(8,128)(2,1)S(1)} %collective-permute-done.1.refs_1_), channel_id=1, source_target_pairs={{0,1},{1,0},{2,3},{3,2},{4,5},{5,4},{6,7},{7,6},{8,9},{9,8},{10,11... | collective-permute-start | bytes 294920 | tf_op jit(solution)/shard_map/ppermute | solution.py:206
  23.3 1.6 %collective-permute-start.4 = (bf16[64,768]{1,0:T(8,128)(2,1)S(1)}, bf16[64,768]{1,0:T(8,128)(2,1)S(1)}, u32[]{:S(2)}, u32[]{:S(2)}) collective-permute-start(bf16[64,768]{1,0:T(8,128)(2,1)S(1)} %collective-permute-done.3.refs_2_), channel_id=1, source_target_pairs={{0,1},{1,0},{2,3},{3,2},{4,5},{5,4},{6,7},{7,6},{8,9},{9,8},{10,11... | collective-permute-start | bytes 294920 | tf_op jit(solution)/shard_map/ppermute | solution.py:206
  23.7 1.3 %collective-permute-start.6 = (bf16[64,768]{1,0:T(8,128)(2,1)S(1)}, bf16[64,768]{1,0:T(8,128)(2,1)S(1)}, u32[]{:S(2)}, u32[]{:S(2)}) collective-permute-start(bf16[64,768]{1,0:T(8,128)(2,1)S(1)} %collective-permute-done.5.refs_3_), channel_id=1, source_target_pairs={{0,1},{1,0},{2,3},{3,2},{4,5},{5,4},{6,7},{7,6},{8,9},{9,8},{10,11... | collective-permute-start | bytes 294920 | tf_op jit(solution)/shard_map/ppermute | solution.py:206
  24.0 1.3 %collective-permute-start.8 = (bf16[64,768]{1,0:T(8,128)(2,1)S(1)}, bf16[64,768]{1,0:T(8,128)(2,1)S(1)}, u32[]{:S(2)}, u32[]{:S(2)}) collective-permute-start(bf16[64,768]{1,0:T(8,128)(2,1)S(1)} %collective-permute-done.7.refs_4_), channel_id=1, source_target_pairs={{0,1},{1,0},{2,3},{3,2},{4,5},{5,4},{6,7},{7,6},{8,9},{9,8},{10,11... | collective-permute-start | bytes 294920 | tf_op jit(solution)/shard_map/ppermute | solution.py:206
